TPU v7x, 32 devices: a whole 2x2x4 slice. The times are simulated.
32 devices in a mesh: seq: 8 (over y, x, core), kv: 4 (over z).
Axes of the slice: x: 2, y: 2, z: 4, core: 2. Of those that a mesh axis runs over, the one named last changes fastest.
Arguments:
- src_embed: bfloat16 [2, 8, 256, 1024], P(None, 'seq', 'kv'), may hold values from -6 to 6
- tgt_embed: bfloat16 [2, 8, 512, 1024], P(None, 'seq', 'kv'), may hold values from -6 to 6
- targets: int32 [2, 8, 512], P(None, None, 'kv'), may hold values from 0 to 50271
- src_len: int32 [2, 8], replicated, may hold values from 64 to 256, as said below
- tgt_len: int32 [2, 8], replicated, may hold values from 64 to 512, as said below
- task: int32 [2, 8], replicated, may hold values from 0 to 1
- step: int32 [1], replicated, may hold values from 2 to 20
- attn_in: bfloat16 [3, 1024, 3072], P(None, ('seq', 'kv')), may hold values from -0.1875 to 0.1875
- attn_out: bfloat16 [3, 1024, 1024], P(None, ('seq', 'kv')), may hold values from -0.75 to 0.75
- ffn_in: bfloat16 [2, 1024, 4096], P(None, ('seq', 'kv')), may hold values from -0.1875 to 0.1875
- ffn_out: bfloat16 [2, 4096, 1024], P(None, ('seq', 'kv')), may hold values from -0.09375 to 0.09375
- embed: bfloat16 [50272, 1024], P('seq'), may hold values from -0.375 to 0.375
- down_w: float32 [2, 2, 1024, 512], P(None, None, ('seq', 'kv')), may hold values from -0.1875 to 0.1875
- down_m: float32 [2, 2, 1024, 512], P(None, None, ('seq', 'kv')), may hold values from -1.5258789e-05 to 1.5258789e-05
- down_v: float32 [2, 2, 1024, 512], P(None, None, ('seq', 'kv')), may hold values from 9.536743e-14 to 3.8146973e-13
- up_w: float32 [2, 2, 512, 1024], P(None, None, ('seq', 'kv')), may hold values from -0.0625 to 0.0625
- up_m: float32 [2, 2, 512, 1024], P(None, None, ('seq', 'kv')), may hold values from -1.5258789e-05 to 1.5258789e-05
- up_v: float32 [2, 2, 512, 1024], P(None, None, ('seq', 'kv')), may hold values from 9.536743e-14 to 3.8146973e-13
- norm_params: float32 [2, 7, 1024], replicated
- norm_m: float32 [2, 7, 1024], replicated, may hold values from -0.00012207031 to 0.00012207031
- norm_v: float32 [2, 7, 1024], replicated, may hold values from 6.9754463e-12 to 2.7901785e-11
Outputs:
- loss_sum: float32 [], replicated
- token_count: float32 [], replicated
- grad_norm: float32 [], replicated
- down_new: float32 [2, 2, 1024, 512], P(None, None, ('seq', 'kv'))
- down_m_new: float32 [2, 2, 1024, 512], P(None, None, ('seq', 'kv'))
- down_v_new: float32 [2, 2, 1024, 512], P(None, None, ('seq', 'kv'))
- up_new: float32 [2, 2, 512, 1024], P(None, None, ('seq', 'kv'))
- up_m_new: float32 [2, 2, 512, 1024], P(None, None, ('seq', 'kv'))
- up_v_new: float32 [2, 2, 512, 1024], P(None, None, ('seq', 'kv'))
- norm_new: float32 [2, 7, 1024], replicated
- norm_m_new: float32 [2, 7, 1024], replicated
- norm_v_new: float32 [2, 7, 1024], replicated
- norm_grad: float32 [2, 7, 1024], replicated
Inputs may be any that keep to these rules, and one draw needn't show every extreme that they name: `src_len`: every micro-batch has an item of the full source length 256. `tgt_len`: every micro-batch has an item of the full target length 512.
All inputs are finite; a program needn't handle non-finite values.
Results may differ from a plain program's by a relative error of at most 0.005.
Values may be sent and summed in bfloat16 or wider, within the bound.
No kernel may reach another device: no remote copies, remote signals or barrier semaphores. Data moves between devices by JAX's collectives and lax.ppermute only.
A program may use at most 320 MiB of HBM per device.

v0:
```python
import jax
import jax.numpy as jnp
from jax import lax
from jax.sharding import PartitionSpec as P

HDIM = 64


norm_epsilon = 1e-05
score_scale = 0.125
clip_limit = 0.02
beta_one = 0.9
beta_two = 0.999
adam_epsilon = 1e-08
rate_adapter = 0.03
rate_norm = 0.25
weight_decay = 0.01


def bfloat(value):
    return value.astype(jnp.bfloat16)


def times_plain(left, right):
    return jnp.dot(left, right, preferred_element_type=jnp.float32)


def times_first(left, right):
    return lax.dot_general(
        left, right, (((0,), (0,)), ((), ())), preferred_element_type=jnp.float32
    )


def times_second(left, right):
    return lax.dot_general(
        left, right, (((1,), (1,)), ((), ())), preferred_element_type=jnp.float32
    )


def norm_forward(value, gain, bias):
    centered = value - jnp.mean(value, -1, keepdims=True)
    inverse = lax.rsqrt(jnp.mean(centered * centered, -1, keepdims=True) + norm_epsilon)
    normed = centered * inverse
    return (normed * gain + bias, (normed, inverse))


def norm_backward(grad, cache, gain):
    normed, inverse = cache
    scaled = grad * gain
    value_grad = inverse * (
        scaled
        - jnp.mean(scaled, -1, keepdims=True)
        - normed * jnp.mean(scaled * normed, -1, keepdims=True)
    )
    return (value_grad, jnp.stack([jnp.sum(grad * normed, 0), jnp.sum(grad, 0)]))


def gelu_slope(value):
    return (
        0.5 * (1.0 + lax.erf(value * 0.7071067811865476))
        + value * jnp.exp(-0.5 * value * value) * 0.3989422804014327
    )


def split_heads(value):
    return value.reshape(value.shape[0], -1, HDIM)


def scores_of(query, keys, mask):
    raw = (
        jnp.einsum(
            "qhd,khd->hqk",
            split_heads(query),
            split_heads(keys),
            preferred_element_type=jnp.float32,
        )
        * score_scale
    )
    return jnp.where(mask[None], raw, -1000000000.0)


def attention_forward(query_in, key_in, w_in, w_out, mask):
    width = w_out.shape[0]
    query = bfloat(times_plain(query_in, w_in[:, :width]))
    pair = bfloat(times_plain(key_in, w_in[:, width:]))
    gathered = lax.all_gather(pair, "kv", axis=0, tiled=True)
    scores = scores_of(query, gathered[:, :width], mask)
    top = jnp.max(scores, -1, keepdims=True)
    logsum = top + jnp.log(jnp.sum(jnp.exp(scores - top), -1, keepdims=True))
    weights = bfloat(jnp.exp(scores - logsum))
    out = jnp.einsum(
        "hqk,khd->qhd",
        weights,
        split_heads(gathered[:, width:]),
        preferred_element_type=jnp.float32,
    )
    out_low = bfloat(out.reshape(query.shape[0], width))
    return (times_plain(out_low, w_out), (query, gathered, logsum))


def attention_backward(branch_grad, cache, w_in, w_out, mask):
    query, gathered, logsum = cache
    width = w_out.shape[0]
    keys = gathered[:, :width]
    out_grad = split_heads(bfloat(times_second(bfloat(branch_grad), w_out)))
    probs = jnp.exp(scores_of(query, keys, mask) - logsum)
    value_grad = jnp.einsum(
        "hqk,qhd->khd", bfloat(probs), out_grad, preferred_element_type=jnp.float32
    )
    prob_grad = jnp.einsum(
        "qhd,khd->hqk",
        out_grad,
        split_heads(gathered[:, width:]),
        preferred_element_type=jnp.float32,
    )
    score_grad = bfloat(probs * (prob_grad - jnp.sum(probs * prob_grad, -1, keepdims=True)))
    query_grad = (
        jnp.einsum(
            "hqk,khd->qhd", score_grad, split_heads(keys), preferred_element_type=jnp.float32
        )
        * score_scale
    )
    key_grad = (
        jnp.einsum(
            "hqk,qhd->khd", score_grad, split_heads(query), preferred_element_type=jnp.float32
        )
        * score_scale
    )
    stacked = jnp.concatenate(
        [key_grad.reshape(keys.shape[0], width), value_grad.reshape(keys.shape[0], width)], 1
    )
    pair_grad = lax.psum_scatter(
        stacked.astype(jnp.bfloat16), "kv", scatter_dimension=0, tiled=True
    ).astype(jnp.float32)
    query_in_grad = times_second(bfloat(query_grad.reshape(query.shape[0], width)), w_in[:, :width])
    key_in_grad = times_second(bfloat(pair_grad), w_in[:, width:])
    return (query_in_grad, key_in_grad)


def feed_forward(value, w_first, w_second, down, upward):
    low_in = bfloat(value)
    hidden = times_plain(low_in, w_first)
    branch = times_plain(bfloat(jax.nn.gelu(hidden, approximate=False)), w_second)
    inner = times_plain(low_in, down)
    inner_low = bfloat(jax.nn.gelu(inner, approximate=False))
    return (branch + 4.0 * times_plain(inner_low, upward), (low_in, hidden, inner, inner_low))


def feed_backward(grad, cache, w_first, w_second, down, upward):
    low_in, hidden, inner, inner_low = cache
    hidden_grad = bfloat(times_second(bfloat(grad), w_second) * gelu_slope(hidden))
    adapter_grad = bfloat(4.0 * grad)
    upward_grad = times_first(inner_low, adapter_grad)
    inner_grad = bfloat(times_second(adapter_grad, upward) * gelu_slope(inner))
    down_grad = times_first(low_in, inner_grad)
    value_grad = times_second(hidden_grad, w_first) + times_second(inner_grad, down)
    return (value_grad, down_grad, upward_grad)


def reduce_grads(down_grad, up_grad, norm_grad, loss_part):
    down_part, up_part = (
        lax.psum_scatter(down_grad, ("seq", "kv"), scatter_dimension=2, tiled=True),
        lax.psum_scatter(up_grad, ("seq", "kv"), scatter_dimension=2, tiled=True),
    )
    norm_sum, loss_sum = lax.psum((norm_grad, loss_part), ("seq", "kv"))
    return (down_part, up_part, norm_sum, loss_sum)


def adam_update(weight, first, second, grad, rate, decay, count_step):
    first_new = beta_one * first + (1.0 - beta_one) * grad
    second_new = beta_two * second + (1.0 - beta_two) * grad * grad
    first_hat = first_new / (1.0 - jnp.power(beta_one, count_step))
    second_hat = second_new / (1.0 - jnp.power(beta_two, count_step))
    weight_new = weight - rate * (
        first_hat / (jnp.sqrt(second_hat) + adam_epsilon) + decay * weight
    )
    return (weight_new, first_new, second_new)


def per_device(
    src_embed,
    tgt_embed,
    targets,
    src_len,
    tgt_len,
    task,
    step,
    attn_in,
    attn_out,
    ffn_in,
    ffn_out,
    embed,
    down_w,
    down_m,
    down_v,
    up_w,
    up_m,
    up_v,
    norm_params,
    norm_m,
    norm_v,
):
    attn_all, out_all, first_all, second_all, down_all, up_all = (
        lax.all_gather(attn_in, ("seq", "kv"), axis=1, tiled=True),
        lax.all_gather(attn_out, ("seq", "kv"), axis=1, tiled=True),
        lax.all_gather(ffn_in, ("seq", "kv"), axis=1, tiled=True),
        lax.all_gather(ffn_out, ("seq", "kv"), axis=1, tiled=True),
        lax.all_gather(bfloat(down_w), ("seq", "kv"), axis=2, tiled=True),
        lax.all_gather(bfloat(up_w), ("seq", "kv"), axis=2, tiled=True),
    )
    seq_index = lax.axis_index("seq")
    kv_index = lax.axis_index("kv")
    kv_count = lax.axis_size("kv")
    micro = src_embed.shape[0]
    enc_rows = src_embed.shape[2]
    dec_rows = tgt_embed.shape[2]
    vocab_rows = embed.shape[0]
    vocab_total = vocab_rows * lax.axis_size("seq")
    gains = norm_params[0]
    biases = norm_params[1]
    count = jnp.sum(tgt_len).astype(jnp.float32)
    src_keys = jnp.arange(enc_rows * kv_count, dtype=jnp.int32)
    dec_keys = jnp.arange(dec_rows * kv_count, dtype=jnp.int32)
    dec_query = kv_index * dec_rows + jnp.arange(dec_rows, dtype=jnp.int32)
    vocab_ids = seq_index * vocab_rows + jnp.arange(vocab_rows, dtype=jnp.int32)
    task_ids = jnp.arange(down_all.shape[1], dtype=jnp.int32)
    totals = None
    for batch in range(micro):
        source_length = src_len[batch, seq_index]
        target_length = tgt_len[batch, seq_index]
        kind = task[batch, seq_index]
        enc_mask = jnp.broadcast_to(
            src_keys[None, :] < source_length, (enc_rows, src_keys.shape[0])
        )
        self_mask = (dec_keys[None, :] <= dec_query[:, None]) & (dec_keys[None, :] < target_length)
        cross_mask = jnp.broadcast_to(
            src_keys[None, :] < source_length, (dec_rows, src_keys.shape[0])
        )
        down_enc = down_all[0, kind]
        up_enc = up_all[0, kind]
        down_dec = down_all[1, kind]
        up_dec = up_all[1, kind]
        x0, cache0 = norm_forward(src_embed[batch, 0].astype(jnp.float32), gains[0], biases[0])
        x0_low = bfloat(x0)
        branch, enc_attn = attention_forward(x0_low, x0_low, attn_all[0], out_all[0], enc_mask)
        x1, cache1 = norm_forward(x0 + branch, gains[1], biases[1])
        branch, enc_feed = feed_forward(x1, first_all[0], second_all[0], down_enc, up_enc)
        x2, cache2 = norm_forward(x1 + branch, gains[2], biases[2])
        y0, cache3 = norm_forward(tgt_embed[batch, 0].astype(jnp.float32), gains[3], biases[3])
        y0_low = bfloat(y0)
        branch, self_attn = attention_forward(y0_low, y0_low, attn_all[1], out_all[1], self_mask)
        y1, cache4 = norm_forward(y0 + branch, gains[4], biases[4])
        branch, cross_attn = attention_forward(
            bfloat(y1), bfloat(x2), attn_all[2], out_all[2], cross_mask
        )
        y2, cache5 = norm_forward(y1 + branch, gains[5], biases[5])
        branch, dec_feed = feed_forward(y2, first_all[1], second_all[1], down_dec, up_dec)
        y3, cache6 = norm_forward(y2 + branch, gains[6], biases[6])
        logits = times_second(lax.all_gather(bfloat(y3), "seq", axis=0, tiled=True), embed)
        row_target = targets[batch].reshape(-1)
        target_hit = vocab_ids[None, :] == row_target[:, None]
        picked_local = jnp.sum(jnp.where(target_hit, logits, 0.0), 1)
        summed_local = jnp.sum(logits, 1)
        local_top = jnp.max(logits, 1)
        top = lax.pmax(local_top, "seq")
        local_total = jnp.sum(jnp.exp(logits - top[:, None]), 1)
        total, picked, summed = (
            lax.psum(local_total.astype(jnp.bfloat16), "seq").astype(jnp.float32),
            lax.psum(picked_local.astype(jnp.bfloat16), "seq").astype(jnp.float32),
            lax.psum(summed_local.astype(jnp.bfloat16), "seq").astype(jnp.float32),
        )
        logsum = top + jnp.log(total)
        row_pos = kv_index * dec_rows + jnp.arange(dec_rows, dtype=jnp.int32)
        alive = (row_pos[None, :] < tgt_len[batch][:, None]).reshape(-1).astype(jnp.float32)
        live = alive / count
        row_loss = alive * (logsum - 0.9 * picked - 0.1 * summed / vocab_total)
        loss_part = jnp.sum(lax.dynamic_slice_in_dim(row_loss, seq_index * dec_rows, dec_rows))
        logit_grad = bfloat(
            (
                jnp.exp(logits - logsum[:, None])
                - 0.9 * target_hit.astype(jnp.float32)
                - 0.1 / vocab_total
            )
            * live[:, None]
        )
        final_grad = lax.psum_scatter(
            times_plain(logit_grad, embed).astype(jnp.bfloat16),
            "seq",
            scatter_dimension=0,
            tiled=True,
        ).astype(jnp.float32)
        grad, grad6 = norm_backward(final_grad, cache6, gains[6])
        inner_grad, down_dec_grad, up_dec_grad = feed_backward(
            grad, dec_feed, first_all[1], second_all[1], down_dec, up_dec
        )
        grad, grad5 = norm_backward(grad + inner_grad, cache5, gains[5])
        query_grad, enc_grad = attention_backward(
            grad, cross_attn, attn_all[2], out_all[2], cross_mask
        )
        grad, grad4 = norm_backward(grad + query_grad, cache4, gains[4])
        query_grad, key_grad = attention_backward(
            grad, self_attn, attn_all[1], out_all[1], self_mask
        )
        unused, grad3 = norm_backward(grad + query_grad + key_grad, cache3, gains[3])
        grad, grad2 = norm_backward(enc_grad, cache2, gains[2])
        inner_grad, down_enc_grad, up_enc_grad = feed_backward(
            grad, enc_feed, first_all[0], second_all[0], down_enc, up_enc
        )
        grad, grad1 = norm_backward(grad + inner_grad, cache1, gains[1])
        query_grad, key_grad = attention_backward(grad, enc_attn, attn_all[0], out_all[0], enc_mask)
        unused, grad0 = norm_backward(grad + query_grad + key_grad, cache0, gains[0])
        norm_grad = jnp.stack([grad0, grad1, grad2, grad3, grad4, grad5, grad6], 1)
        chosen = (task_ids == kind).astype(jnp.float32)[:, None, None]
        down_grad = jnp.stack([chosen * down_enc_grad[None], chosen * down_dec_grad[None]])
        up_grad = jnp.stack([chosen * up_enc_grad[None], chosen * up_dec_grad[None]])
        reduced = reduce_grads(down_grad, up_grad, norm_grad, loss_part)
        totals = reduced if totals is None else jax.tree.map(jnp.add, totals, reduced)
    down_part, up_part, norm_sum, loss_sum = totals
    square = lax.psum(jnp.sum(down_part * down_part) + jnp.sum(up_part * up_part), ("seq", "kv"))
    grad_norm = jnp.sqrt(square + jnp.sum(norm_sum * norm_sum))
    factor = clip_limit / jnp.maximum(grad_norm, clip_limit)
    count_step = step[0].astype(jnp.float32)
    down_new = adam_update(
        down_w, down_m, down_v, factor * down_part, rate_adapter, weight_decay, count_step
    )
    up_new = adam_update(up_w, up_m, up_v, factor * up_part, rate_adapter, weight_decay, count_step)
    norm_grad_out = factor * norm_sum
    norm_new = adam_update(norm_params, norm_m, norm_v, norm_grad_out, rate_norm, 0.0, count_step)
    return (
        loss_sum,
        count,
        grad_norm,
        down_new[0],
        down_new[1],
        down_new[2],
        up_new[0],
        up_new[1],
        up_new[2],
        norm_new[0],
        norm_new[1],
        norm_new[2],
        norm_grad_out,
    )


def solution(mesh):
    placed = (
        P(None, "seq", "kv", None),
        P(None, "seq", "kv", None),
        P(None, None, "kv"),
        P(),
        P(),
        P(),
        P(),
        P(None, ("seq", "kv"), None),
        P(None, ("seq", "kv"), None),
        P(None, ("seq", "kv"), None),
        P(None, ("seq", "kv"), None),
        P("seq", None),
        P(None, None, ("seq", "kv"), None),
        P(None, None, ("seq", "kv"), None),
        P(None, None, ("seq", "kv"), None),
        P(None, None, ("seq", "kv"), None),
        P(None, None, ("seq", "kv"), None),
        P(None, None, ("seq", "kv"), None),
        P(),
        P(),
        P(),
    )
    return jax.shard_map(
        per_device,
        mesh=mesh,
        in_specs=placed,
        out_specs=(
            P(),
            P(),
            P(),
            P(None, None, ("seq", "kv"), None),
            P(None, None, ("seq", "kv"), None),
            P(None, None, ("seq", "kv"), None),
            P(None, None, ("seq", "kv"), None),
            P(None, None, ("seq", "kv"), None),
            P(None, None, ("seq", "kv"), None),
            P(),
            P(),
            P(),
            P(),
        ),
        check_vma=False,
    )
```

profile of v0, /device:TPU:0, one launch (start us, length us, event | category | flops | bytes accessed | tf_op | source)
XLA Modules:
  0.0 1779.4 jit_solution(17749458515645525809)
XLA Ops:
  11.9 126.4 %all-gather.15.cloned.1.call-done = bf16[3,1024,3072]{2,1,0:T(8,128)(2,1)} async-done(((bf16[3,32,3072]{2,1,0:T(8,128)(2,1)}), bf16[3,1024,3072]{2,1,0:T(8,128)(2,1)}) %all-gather.15.cloned.1.call-update) | async-done | bytes 18874384 | tf_op jit(solution)/shard_map/all_gather | solution.py:204
  184.8 68.4 %all-gather.19.cloned.1.call-done = bf16[3,1024,1024]{2,1,0:T(8,128)(2,1)} async-done(((bf16[3,32,1024]{2,1,0:T(8,128)(2,1)}), bf16[3,1024,1024]{2,1,0:T(8,128)(2,1)}) %all-gather.19.cloned.1.call-update) | async-done | bytes 6291472 | tf_op jit(solution)/shard_map/all_gather | solution.py:205
  255.7 26.4 %all-gather.37.cloned.1.call-done = bf16[256,2048]{1,0:T(8,128)(2,1)} async-done(((bf16[64,2048]{1,0:T(8,128)(2,1)}), bf16[256,2048]{1,0:T(8,128)(2,1)}) %all-gather.37.cloned.1.call-update) | async-done | bytes 1048592 | tf_op jit(solution)/shard_map/all_gather | solution.py:86
  288.4 59.0 %all-gather.27.cloned.1.call-done = bf16[2,2,1024,512]{3,2,1,0:T(8,128)(2,1)} async-done(((bf16[2,2,32,512]{3,2,1,0:T(8,128)(2,1)}), bf16[2,2,1024,512]{3,2,1,0:T(8,128)(2,1)}) %all-gather.27.cloned.1.call-update) | async-done | bytes 4194320 | tf_op jit(solution)/shard_map/all_gather | solution.py:208
  348.9 114.9 %all-gather.23.cloned.1.call-done = bf16[2,1024,4096]{2,1,0:T(8,128)(2,1)} async-done(((bf16[2,32,4096]{2,1,0:T(8,128)(2,1)}), bf16[2,1024,4096]{2,1,0:T(8,128)(2,1)}) %all-gather.23.cloned.1.call-update) | async-done | bytes 16777232 | tf_op jit(solution)/shard_map/all_gather | solution.py:206
  468.7 111.0 %all-gather.25.cloned.1.call-done = bf16[2,4096,1024]{2,1,0:T(8,128)(2,1)} async-done(((bf16[2,128,1024]{2,1,0:T(8,128)(2,1)}), bf16[2,4096,1024]{2,1,0:T(8,128)(2,1)}) %all-gather.25.cloned.1.call-update) | async-done | bytes 16777232 | tf_op jit(solution)/shard_map/all_gather | solution.py:207
  585.5 58.3 %all-gather.29.cloned.1.call-done = bf16[2,2,512,1024]{3,2,1,0:T(8,128)(2,1)} async-done(((bf16[2,2,16,1024]{3,2,1,0:T(8,128)(2,1)}), bf16[2,2,512,1024]{3,2,1,0:T(8,128)(2,1)}) %all-gather.29.cloned.1.call-update) | async-done | bytes 4194320 | tf_op jit(solution)/shard_map/all_gather | solution.py:209
  699.9 18.9 %all-gather.31.cloned.1.call-done = bf16[256,2048]{1,0:T(8,128)(2,1)} async-done(((bf16[64,2048]{1,0:T(8,128)(2,1)}), bf16[256,2048]{1,0:T(8,128)(2,1)}) %all-gather.31.cloned.1.call-update) | async-done | bytes 1048592 | tf_op jit(solution)/shard_map/all_gather | solution.py:86
  723.1 25.4 %all-gather.39.cloned.1.call-done = bf16[256,2048]{1,0:T(8,128)(2,1)} async-done(((bf16[64,2048]{1,0:T(8,128)(2,1)}), bf16[256,2048]{1,0:T(8,128)(2,1)}) %all-gather.39.cloned.1.call-update) | async-done | bytes 1048592 | tf_op jit(solution)/shard_map/all_gather | solution.py:86
  755.0 40.3 %all-gather.35.cloned.1.call-done = bf16[512,2048]{1,0:T(8,128)(2,1)} async-done(((bf16[128,2048]{1,0:T(8,128)(2,1)}), bf16[512,2048]{1,0:T(8,128)(2,1)}) %all-gather.35.cloned.1.call-update) | async-done | bytes 2097168 | tf_op jit(solution)/shard_map/all_gather | solution.py:86
  846.4 25.2 %all-gather.41.cloned.1.call-done = bf16[1024,1024]{1,0:T(8,128)(2,1)} async-done(((bf16[128,1024]{1,0:T(8,128)(2,1)}), bf16[1024,1024]{1,0:T(8,128)(2,1)}) %all-gather.41.cloned.1.call-update) | async-done | bytes 2097168 | tf_op jit(solution)/shard_map/all_gather | solution.py:259
  871.7 22.2 %fusion.845 = (f32[1024]{0:T(1024)S(1)}, f32[1024,6284]{0,1:T(8,128)}) fusion(bf16[1024,1024]{1,0:T(8,128)(2,1)} %all-gather.41.cloned.1.call-done, bf16[6284,1024]{1,0:T(8,128)(2,1)} %param.32), kind=kOutput, calls=%fused_computation.1126 | convolution fusion | flops 13184936960 | bytes 40710144 | tf_op jit(solution)/shard_map/dot_general | solution.py:35
  901.9 22.4 %fusion.846 = (f32[1024]{0:T(1024)S(1)}, f32[1024,6284]{0,1:T(8,128)}) fusion(bf16[1024,1024]{1,0:T(8,128)(2,1)} %all-gather.33.cloned.1.call-done, bf16[6284,1024]{1,0:T(8,128)(2,1)} %param.32), kind=kOutput, calls=%fused_computation.1127 | convolution fusion | flops 13184936960 | bytes 40710144 | tf_op jit(solution)/shard_map/dot_general | solution.py:35
  937.7 21.6 %fusion.5 = (bf16[1024]{0:T(1024)(128)(2,1)S(1)}, bf16[1024]{0:T(1024)(128)(2,1)S(1)}, bf16[1024]{0:T(1024)(128)(2,1)S(1)}, bf16[1024]{0:T(1024)(128)(2,1)S(1)},...) fusion(f32[1024,6284]{0,1:T(8,128)} %get-tuple-element.213, s32[1024]{0:T(1024)S(1)} %get-tuple-element.133, ...), kind=kLoop, calls=%fused_computation.9 | loop fusion | flops 77211648 | bytes 51532336 | tf_op jit(solution)/shard_map/reduce_sum | solution.py:262
  959.3 22.5 %all-reduce.2 = (bf16[1024]{0:T(1024)(128)(2,1)S(1)}, bf16[1024]{0:T(1024)(128)(2,1)S(1)}, bf16[1024]{0:T(1024)(128)(2,1)S(1)}, bf16[1024]{0:T(1024)(128)(2,1)S(...) all-reduce(bf16[1024]{0:T(1024)(128)(2,1)S(1)} %get-tuple-element.7, ...), channel_id=1, replica_groups=mesh['seq'=8,'kv'=4] {'seq'}, use_global_device_ids=true, to_apply=%region_27.28 | all-reduce | flops 6144 | bytes 24576 | tf_op jit(solution)/shard_map/psum | solution.py:270
  982.4 24.3 %fusion.114 = bf16[1024,1024]{1,0:T(8,128)(2,1)} fusion(bf16[6284,1024]{1,0:T(8,128)(2,1)} %param.32, f32[1024,6284]{0,1:T(8,128)} %get-tuple-element.215, f32[1024]{0:T(1024)S(1)} %get-tuple-element.175, f32[1024]{0:T(1024)S(1)} %get-tuple-element.177, s32[1024]{0:T(1024)S(1)} %get-tuple-element.132, s32[6284]{0:T(1024)S(1)} %iota_add_fusion), kind=kOutput, calls=%fused_computation.170 | convolution fusion | flops 13224595456 | bytes 40743472 | tf_op jit(solution)/shard_map/dot_general | solution.py:25
  1006.8 24.3 %fusion.117 = bf16[1024,1024]{1,0:T(8,128)(2,1)} fusion(bf16[6284,1024]{1,0:T(8,128)(2,1)} %param.32, f32[1024,6284]{0,1:T(8,128)} %get-tuple-element.213, f32[1024]{0:T(1024)S(1)} %get-tuple-element.157, f32[1024]{0:T(1024)S(1)} %get-tuple-element.100, s32[1024]{0:T(1024)S(1)} %get-tuple-element.133, s32[6284]{0:T(1024)S(1)} %iota_add_fusion), kind=kOutput, calls=%fused_computation.171 | convolution fusion | flops 13224595456 | bytes 40743472 | tf_op jit(solution)/shard_map/dot_general | solution.py:25
  1031.1 17.0 reduce-scatter.23.cloned.1.call-done
  1048.2 44.8 %reduce-scatter.25.cloned.1.call-done = bf16[128,1024]{1,0:T(8,128)(2,1)} async-done(((bf16[1024,1024]{1,0:T(8,128)(2,1)}), bf16[128,1024]{1,0:T(8,128)(2,1)}) %reduce-scatter.25.cloned.1.call-update) | async-done | bytes 262160 | tf_op jit(solution)/shard_map/reduce_scatter | solution.py:286
  1305.7 15.3 reduce-scatter.35.cloned.1.call-done
  1327.5 21.7 %reduce-scatter.39.cloned.1.call-done = bf16[64,2048]{1,0:T(8,128)(2,1)} async-done(((bf16[256,2048]{1,0:T(8,128)(2,1)}), bf16[64,2048]{1,0:T(8,128)(2,1)}) %reduce-scatter.39.cloned.1.call-update) | async-done | bytes 262160
  1356.1 179.9 %reduce-scatter.27.cloned.1.call-done = f32[2,2,32,512]{3,2,1,0:T(8,128)} async-done(((f32[2,2,1024,512]{3,2,1,0:T(8,128)}), f32[2,2,32,512]{3,2,1,0:T(8,128)}) %reduce-scatter.27.cloned.1.call-update) | async-done | bytes 262160 | tf_op jit(solution)/shard_map/reduce_scatter | solution.py:162
  1537.6 184.1 %reduce-scatter.29.cloned.1.call-done = f32[2,2,16,1024]{3,2,1,0:T(8,128)} async-done(((f32[2,2,512,1024]{3,2,1,0:T(8,128)}), f32[2,2,16,1024]{3,2,1,0:T(8,128)}) %reduce-scatter.29.cloned.1.call-update) | async-done | bytes 262160 | tf_op jit(solution)/shard_map/reduce_scatter | solution.py:163
  1724.6 38.4 %all-reduce = (f32[]{:T(128)}, f32[]{:T(128)}, f32[2,7,1024]{2,0,1:T(2,128)S(1)}) all-reduce(f32[]{:T(128)S(6)} %add.657, f32[]{:T(128)S(6)} %add.676, f32[2,7,1024]{2,0,1:T(2,128)S(1)} %add.695), channel_id=1, replica_groups=mesh['seq'=8,'kv'=4] {'seq','kv'}, use_global_device_ids=true, to_apply=%region_29.30 | all-reduce | flops 14338 | bytes 114704 | tf_op jit(solution)/shard_map/psum | solution.py:165
  (964 shorter events, 435.0 us)
Async XLA Ops:
  7.2 131.2 %all-gather.15.cloned.1.call-start = ((), (), s32[]{:S(2)}) async-start(), calls=%async_computation.10 | async-start | bytes 19464192 | tf_op jit(solution)/shard_map/all_gather | solution.py:204
  7.9 173.4 %all-gather.21.cloned.1.call-start = ((), (), s32[]{:S(2)}) async-start(), calls=%async_computation.13 | async-start | bytes 1310720 | tf_op jit(solution)/shard_map/all_gather | solution.py:86
  155.1 98.1 %all-gather.19.cloned.1.call-start = ((), (), s32[]{:S(2)}) async-start(), calls=%async_computation.12 | async-start | bytes 6488064 | tf_op jit(solution)/shard_map/all_gather | solution.py:205
  155.9 126.2 %all-gather.37.cloned.1.call-start = ((), (), s32[]{:S(2)}) async-start(), calls=%async_computation.21 | async-start | bytes 1310720 | tf_op jit(solution)/shard_map/all_gather | solution.py:86
  159.8 187.6 %all-gather.27.cloned.1.call-start = ((), (), s32[]{:S(2)}) async-start(), calls=%async_computation.16 | async-start | bytes 4325376 | tf_op jit(solution)/shard_map/all_gather | solution.py:208
  160.5 303.2 %all-gather.23.cloned.1.call-start = ((), (), s32[]{:S(2)}) async-start(), calls=%async_computation.14 | async-start | bytes 17301504 | tf_op jit(solution)/shard_map/all_gather | solution.py:206
  161.1 418.7 %all-gather.25.cloned.1.call-start = ((), (), s32[]{:S(2)}) async-start(), calls=%async_computation.15 | async-start | bytes 17301504 | tf_op jit(solution)/shard_map/all_gather | solution.py:207
  161.9 482.0 %all-gather.29.cloned.1.call-start = ((), (), s32[]{:S(2)}) async-start(), calls=%async_computation.17 | async-start | bytes 4325376 | tf_op jit(solution)/shard_map/all_gather | solution.py:209
  162.6 527.5 %all-gather.17.cloned.1.call-start = ((), (), s32[]{:S(2)}) async-start(), calls=%async_computation.11 | async-start | bytes 2621440 | tf_op jit(solution)/shard_map/all_gather | solution.py:86
  177.7 541.1 %all-gather.31.cloned.1.call-start = ((), (), s32[]{:S(2)}) async-start(), calls=%async_computation.18 | async-start | bytes 1310720 | tf_op jit(solution)/shard_map/all_gather | solution.py:86
  649.8 98.7 %all-gather.39.cloned.1.call-start = ((), (), s32[]{:S(2)}) async-start(), calls=%async_computation.22 | async-start | bytes 1310720 | tf_op jit(solution)/shard_map/all_gather | solution.py:86
  667.3 128.0 %all-gather.35.cloned.1.call-start = ((), (), s32[]{:S(2)}) async-start(), calls=%async_computation.20 | async-start | bytes 2621440 | tf_op jit(solution)/shard_map/all_gather | solution.py:86
  678.8 192.9 %all-gather.41.cloned.1.call-start = ((), (), s32[]{:S(2)}) async-start(), calls=%async_computation.23 | async-start | bytes 2359296 | tf_op jit(solution)/shard_map/all_gather | solution.py:259
  844.9 57.0 %all-gather.33.cloned.1.call-start = ((), (), s32[]{:S(2)}) async-start(), calls=%async_computation.19 | async-start | bytes 2359296 | tf_op jit(solution)/shard_map/all_gather | solution.py:259
  846.4 201.8 %reduce-scatter.23.cloned.1.call-start = ((), (), s32[]{:S(2)}) async-start(), calls=%async_computation.24 | async-start | bytes 2359296 | tf_op jit(solution)/shard_map/reduce_scatter | solution.py:286
  1006.7 86.2 %reduce-scatter.25.cloned.1.call-start = ((), (), s32[]{:S(2)}) async-start(), calls=%async_computation.25 | async-start | bytes 2359296 | tf_op jit(solution)/shard_map/reduce_scatter | solution.py:286
  1031.1 169.0 %reduce-scatter.33.cloned.1.call-start = ((), (), s32[]{:S(2)}) async-start(), calls=%async_computation.29 | async-start | bytes 1310720
  1146.5 58.0 %reduce-scatter.31.cloned.1.call-start = ((), (), s32[]{:S(2)}) async-start(), calls=%async_computation.28 | async-start | bytes 1310720
  1163.9 128.2 %reduce-scatter.37.cloned.1.call-start = ((), (), s32[]{:S(2)}) async-start(), calls=%async_computation.31 | async-start | bytes 2621440
  1178.9 119.8 %reduce-scatter.41.cloned.1.call-start = ((), (), s32[]{:S(2)}) async-start(), calls=%async_computation.33 | async-start | bytes 2621440
  1199.9 121.1 %reduce-scatter.35.cloned.1.call-start = ((), (), s32[]{:S(2)}) async-start(), calls=%async_computation.30 | async-start | bytes 1310720
  1248.4 100.9 %reduce-scatter.39.cloned.1.call-start = ((), (), s32[]{:S(2)}) async-start(), calls=%async_computation.32 | async-start | bytes 1310720
  1257.7 278.4 %reduce-scatter.27.cloned.1.call-start = ((), (), s32[]{:S(2)}) async-start(), calls=%async_computation.26 | async-start | bytes 8650752 | tf_op jit(solution)/shard_map/reduce_scatter | solution.py:162
  1268.1 453.6 %reduce-scatter.29.cloned.1.call-start = ((), (), s32[]{:S(2)}) async-start(), calls=%async_computation.27 | async-start | bytes 8650752 | tf_op jit(solution)/shard_map/reduce_scatter | solution.py:163
  (313 other events, 15083.3 us)
Sparse Core Ops, SparseCore 0:
  10.9 127.3 all-gather.14
  155.3 25.9 all-gather.20
  184.3 68.8 all-gather.18
  255.2 26.8 all-gather.36
  285.6 61.7 all-gather.26
  350.2 113.5 all-gather.22
  466.8 112.9 all-gather.24
  583.4 60.3 all-gather.28
  645.4 44.6 all-gather.16
  692.1 26.6 all-gather.30
  721.0 27.4 all-gather.38
  749.9 45.4 all-gather.34
  845.0 26.6 all-gather.40
  874.0 27.8 all-gather.32
  1006.8 41.2 reduce-scatter.22
  1051.6 41.2 reduce-scatter.24
  1146.7 27.1 reduce-scatter.32
  1176.1 25.7 reduce-scatter.30
  1204.2 42.1 reduce-scatter.36
  1248.6 43.4 reduce-scatter.40
  1294.5 26.4 reduce-scatter.34
  1323.4 25.7 reduce-scatter.38
  1351.5 184.4 reduce-scatter.26
  1538.2 183.4 reduce-scatter.28
where the time goes:
time: 1790 us; the launch traced here: 1780 us
  waiting for transfers between devices  1160 us (65%)
  matrix products  361 us (20%)
  other arithmetic  82.5 us (5%)
  blocking collectives  74.3 us (4%)
  local copies, waits for them, and re-layouts  65.7 us (4%)
  between operations  31.7 us (2%)
    reduce_scatter x1, waiting for transfers between devices, reduce_grads(): lax.psum_scatter(up_grad, ('seq', 'kv'), scatter_dimension=2, tiled=True)  184 us
    reduce_scatter x1, waiting for transfers between devices, reduce_grads(): lax.psum_scatter(down_grad, ('seq', 'kv'), scatter_dimension=2, tiled=True)  180 us
    dot_general x32, matrix products, times_second(): lax.dot_general(left, right, (((1,), (1,)), ((), ())), preferred_element_...  161 us
    dot_general x36, matrix products, times_plain(): return jnp.dot(left, right, preferred_element_type=jnp.float32)  149 us
    all_gather x1, waiting for transfers between devices, per_device(): lax.all_gather(attn_in, ('seq', 'kv'), axis=1, tiled=True)  126 us
    all_gather x6, waiting for transfers between devices, attention_forward(): gathered = lax.all_gather(pair, 'kv', axis=0, tiled=True)  125 us
    all_gather x1, waiting for transfers between devices, per_device(): lax.all_gather(ffn_in, ('seq', 'kv'), axis=1, tiled=True)  115 us
    all_gather x1, waiting for transfers between devices, per_device(): lax.all_gather(ffn_out, ('seq', 'kv'), axis=1, tiled=True)  111 us
  transfers between devices with their start and end apart: 24, of which 20 were waited for; matrix products, arithmetic and copies ran while one was open for 17% of the time, Pallas kernels for 0%

commit v1 on v0

v1 whole, which is shorter than its diff:
```python
import functools

import jax
import jax.numpy as jnp
from jax import lax
from jax.experimental import pallas as pl
from jax.experimental.pallas import tpu as pltpu
from jax.sharding import PartitionSpec as P

HDIM = 64


norm_epsilon = 1e-05
score_scale = 0.125
clip_limit = 0.02
beta_one = 0.9
beta_two = 0.999
adam_epsilon = 1e-08
rate_adapter = 0.03
rate_norm = 0.25
weight_decay = 0.01


def bfloat(value):
    return value.astype(jnp.bfloat16)


def times_plain(left, right):
    return jnp.dot(left, right, preferred_element_type=jnp.float32)


def times_first(left, right):
    return lax.dot_general(
        left, right, (((0,), (0,)), ((), ())), preferred_element_type=jnp.float32
    )


def times_second(left, right):
    return lax.dot_general(
        left, right, (((1,), (1,)), ((), ())), preferred_element_type=jnp.float32
    )


def norm_forward(value, gain, bias):
    centered = value - jnp.mean(value, -1, keepdims=True)
    inverse = lax.rsqrt(jnp.mean(centered * centered, -1, keepdims=True) + norm_epsilon)
    normed = centered * inverse
    return (normed * gain + bias, (normed, inverse))


def norm_backward(grad, cache, gain):
    normed, inverse = cache
    scaled = grad * gain
    value_grad = inverse * (
        scaled
        - jnp.mean(scaled, -1, keepdims=True)
        - normed * jnp.mean(scaled * normed, -1, keepdims=True)
    )
    return (value_grad, jnp.stack([jnp.sum(grad * normed, 0), jnp.sum(grad, 0)]))


def gelu_slope(value):
    return (
        0.5 * (1.0 + lax.erf(value * 0.7071067811865476))
        + value * jnp.exp(-0.5 * value * value) * 0.3989422804014327
    )


def split_heads(value):
    return value.reshape(value.shape[0], -1, HDIM)


AXES = ("seq", "kv")
MEBI = 2**20
LOWEST = -3e38


def swap(value, seq_mask, kv_mask):
    seq_count, kv_count = lax.axis_size("seq"), lax.axis_size("kv")
    pairs = [
        (s * kv_count + z, (s ^ seq_mask) * kv_count + (z ^ kv_mask))
        for s in range(seq_count)
        for z in range(kv_count)
    ]
    return lax.ppermute(value, AXES, pairs)


def plane_bits():
    count = lax.axis_size("seq").bit_length() - 2
    bits = [2 << place for place in range(count)]
    return (bits[: count // 2], bits[count // 2 :])


def after(value, earlier):
    return lax.optimization_barrier((value, earlier))[0]


def spread(blocks, bits):
    for bit in bits:
        keys = sorted(blocks)
        got = swap(jnp.stack([blocks[key] for key in keys]), bit, 0)
        blocks = blocks | {key | bit: got[place] for place, key in enumerate(keys)}
    return blocks


def gather_depth_first(own, earlier):
    own = after(own, earlier) if earlier is not None else own
    kv_count = lax.axis_size("kv")
    column = [own] + [swap(own, 0, step) for step in range(1, kv_count)]
    half = kv_count // 2
    x_bits, y_bits = plane_bits()
    pieces = []
    for first, bits in ((0, x_bits + y_bits), (half, y_bits + x_bits)):
        parts = [((0,), jnp.stack(column[first : first + half]))]
        stack = parts[0][1][None]
        labels = [0]
        for bit in bits:
            got = swap(stack, bit, 0)
            pieces.append((labels, first, stack)) if bit == bits[-1] else None
            fresh = [label | bit for label in labels]
            if bit == bits[-1]:
                pieces.append((fresh, first, got))
            else:
                stack = jnp.concatenate([stack, got])
                labels = labels + fresh
    pieces = pieces + [
        ([label | 1 for label in labels], first, swap(stack, 1, 0))
        for labels, first, stack in pieces
    ]
    return pieces, column[-1]


def gather_plane_first(own, earlier):
    kv_count = lax.axis_size("kv")
    x_bits, y_bits = plane_bits()
    half = own.shape[1] // 2
    stacks = []
    for part, bits in ((own[:, :half], x_bits + y_bits), (own[:, half:], y_bits + x_bits)):
        blocks = spread({0: part}, bits)
        labels = sorted(blocks)
        stacks.append(jnp.stack([blocks[label] for label in labels]))
    whole = jnp.concatenate(stacks, 2)
    sent = after(whole, earlier)
    pieces = [(labels, 0, whole[:, None])] + [
        (labels, step, swap(sent, 0, step)[:, None]) for step in range(1, kv_count)
    ]
    pieces = pieces + [
        ([label | 1 for label in names], first, swap(stack, 1, 0))
        for names, first, stack in pieces
    ]
    return pieces


def place_kernel(plan, where_ref, *refs):
    sources = refs[: len(plan)]
    count = len(refs) - len(plan) - 1
    targets = refs[len(plan) : len(plan) + count]
    sems = refs[-1]
    own = where_ref[0]
    kind = where_ref[1]
    copies = []
    for source, labels in zip(sources, plan):
        for first, row in enumerate(labels):
            for second, label in enumerate(row):
                block = source.at[first, second]
                where = own ^ label
                if count == 2 and len(source.shape) == 5:
                    start = 0
                    for target in targets:
                        width = target.shape[-1]
                        copies.append((block.at[0, :, start : start + width], target.at[where]))
                        start += width
                elif count == 1:
                    copies.append((block.at[0], targets[0].at[where]))
                else:
                    for layer in range(2):
                        copies.append((block.at[2 * layer + kind], targets[0].at[layer, where]))
                        copies.append((block.at[4 + 2 * layer + kind], targets[1].at[layer, :, where]))
    started = []
    for place, (origin, target) in enumerate(copies):
        copy = pltpu.make_async_copy(origin, target, sems.at[place])
        copy.start()
        started.append(copy)
    for copy in started:
        copy.wait()


def place_blocks(pieces, where, shapes):
    kv_count = lax.axis_size("kv")
    plan = []
    total = 0
    for labels, first, stack in pieces:
        plan.append([[label * kv_count + first + k for k in range(stack.shape[1])] for label in labels])
        total += len(labels) * stack.shape[1]
    copies = total * (4 if pieces[0][2].ndim == 6 else len(shapes))
    anywhere = pl.BlockSpec(memory_space=pl.ANY)
    return pl.pallas_call(
        functools.partial(place_kernel, plan),
        grid_spec=pltpu.PrefetchScalarGridSpec(
            num_scalar_prefetch=1,
            grid=(1,),
            in_specs=[anywhere] * len(pieces),
            out_specs=[anywhere] * len(shapes),
            scratch_shapes=[pltpu.SemaphoreType.DMA((copies,))],
        ),
        out_shape=[jax.ShapeDtypeStruct(shape, jnp.bfloat16) for shape in shapes],
    )(where, *[stack for _, _, stack in pieces])


def with_partner(value):
    return jnp.concatenate([value, swap(value, 1, 0)])


def scores_of(query, keys, mask):
    raw = (
        jnp.einsum(
            "qhd,khd->hqk",
            split_heads(query),
            split_heads(keys),
            preferred_element_type=jnp.float32,
        )
        * score_scale
    )
    return jnp.where(mask[None], raw, -1000000000.0)


def attention_forward(query_in, key_in, w_in, w_out, mask):
    width = w_out.shape[0]
    query = bfloat(times_plain(query_in, w_in[:, :width]))
    gathered = with_partner(bfloat(times_plain(key_in, w_in[:, width:])))
    scores = scores_of(query, gathered[:, :width], mask)
    top = jnp.max(scores, -1, keepdims=True)
    logsum = top + jnp.log(jnp.sum(jnp.exp(scores - top), -1, keepdims=True))
    weights = bfloat(jnp.exp(scores - logsum))
    out = jnp.einsum(
        "hqk,khd->qhd",
        weights,
        split_heads(gathered[:, width:]),
        preferred_element_type=jnp.float32,
    )
    out_low = bfloat(out.reshape(query.shape[0], width))
    return (times_plain(out_low, w_out), (query, gathered, logsum))


def attention_backward(branch_grad, cache, w_in, w_out, mask):
    query, gathered, logsum = cache
    width = w_out.shape[0]
    keys = gathered[:, :width]
    out_grad = split_heads(bfloat(times_second(bfloat(branch_grad), w_out)))
    probs = jnp.exp(scores_of(query, keys, mask) - logsum)
    value_grad = jnp.einsum(
        "hqk,qhd->khd", bfloat(probs), out_grad, preferred_element_type=jnp.float32
    )
    prob_grad = jnp.einsum(
        "qhd,khd->hqk",
        out_grad,
        split_heads(gathered[:, width:]),
        preferred_element_type=jnp.float32,
    )
    score_grad = bfloat(probs * (prob_grad - jnp.sum(probs * prob_grad, -1, keepdims=True)))
    query_grad = (
        jnp.einsum(
            "hqk,khd->qhd", score_grad, split_heads(keys), preferred_element_type=jnp.float32
        )
        * score_scale
    )
    key_grad = (
        jnp.einsum(
            "hqk,qhd->khd", score_grad, split_heads(query), preferred_element_type=jnp.float32
        )
        * score_scale
    )
    stacked = jnp.concatenate(
        [key_grad.reshape(keys.shape[0], width), value_grad.reshape(keys.shape[0], width)], 1
    )
    rows = keys.shape[0] // 2
    pair_grad = stacked[:rows] + swap(bfloat(stacked[rows:]), 1, 0).astype(jnp.float32)
    query_in_grad = times_second(bfloat(query_grad.reshape(query.shape[0], width)), w_in[:, :width])
    key_in_grad = times_second(bfloat(pair_grad), w_in[:, width:])
    return (query_in_grad, key_in_grad)


def feed_forward(value, w_first, w_second, down, upward):
    low_in = bfloat(value)
    hidden = times_plain(low_in, w_first)
    branch = times_plain(bfloat(jax.nn.gelu(hidden, approximate=False)), w_second)
    inner = times_plain(low_in, down)
    inner_low = bfloat(jax.nn.gelu(inner, approximate=False))
    return (branch + 4.0 * times_plain(inner_low, upward), (low_in, hidden, inner, inner_low))


def feed_backward(grad, cache, w_first, w_second, down, upward):
    low_in, hidden, inner, inner_low = cache
    hidden_grad = bfloat(times_second(bfloat(grad), w_second) * gelu_slope(hidden))
    adapter_grad = bfloat(4.0 * grad)
    upward_grad = times_first(inner_low, adapter_grad)
    inner_grad = bfloat(times_second(adapter_grad, upward) * gelu_slope(inner))
    down_grad = times_first(low_in, inner_grad)
    value_grad = times_second(hidden_grad, w_first) + times_second(inner_grad, down)
    return (value_grad, down_grad, upward_grad)


def vocab_kernel(count, tile, rows_ref, table_ref, mixed_ref, stats_ref, scores):
    rows = rows_ref[...]
    block = rows.shape[0]
    padded = table_ref.shape[0]
    top = jnp.full((block, 1), LOWEST, jnp.float32)
    for start in range(0, padded, tile):
        part = times_second(rows, table_ref[start : start + tile, :])
        if start + tile > count:
            entry = lax.broadcasted_iota(jnp.int32, part.shape, 1) + start
            part = jnp.where(entry < count, part, LOWEST)
        scores[:, start : start + tile] = part
        top = jnp.maximum(top, jnp.max(part, 1, keepdims=True))
    total = jnp.zeros((block, 1), jnp.float32)
    mixed = jnp.zeros(mixed_ref.shape, jnp.float32)
    for start in range(0, padded, tile):
        weights = jnp.exp(scores[:, start : start + tile] - top)
        total = total + jnp.sum(weights, 1, keepdims=True)
        mixed = mixed + times_plain(bfloat(weights), table_ref[start : start + tile, :])
    mixed_ref[...] = mixed
    stats_ref[...] = jnp.concatenate(
        [jnp.broadcast_to(top, (block, 64)), jnp.broadcast_to(total, (block, 64))], 1
    )


def vocab_pass(rows, table, count, block, tile):
    total, width = rows.shape
    padded = table.shape[0]
    return pl.pallas_call(
        functools.partial(vocab_kernel, count, tile),
        grid=(total // block,),
        in_specs=[
            pl.BlockSpec((block, width), lambda i: (i, 0)),
            pl.BlockSpec((padded, width), lambda i: (0, 0), pipeline_mode=pl.Buffered(1)),
        ],
        out_specs=[
            pl.BlockSpec((block, width), lambda i: (i, 0)),
            pl.BlockSpec((block, 128), lambda i: (i, 0)),
        ],
        out_shape=[
            jax.ShapeDtypeStruct((total, width), jnp.float32),
            jax.ShapeDtypeStruct((total, 128), jnp.float32),
        ],
        scratch_shapes=[pltpu.VMEM((block, padded), jnp.float32)],
        compiler_params=pltpu.CompilerParams(vmem_limit_bytes=56 * MEBI),
        cost_estimate=pl.CostEstimate(
            flops=4 * total * width * padded,
            bytes_accessed=2 * padded * width + 6 * total * width,
            transcendentals=total * padded,
        ),
    )(rows, table)


def halved_sum(blocks, bits):
    for bit in bits:
        keys = [key for key in sorted(blocks) if not key & bit]
        got = swap(jnp.stack([bfloat(blocks[key | bit]) for key in keys]), bit, 0)
        blocks = {key: blocks[key] + got[place].astype(jnp.float32) for place, key in enumerate(keys)}
    return blocks


def pick(value, axis, index):
    return lax.dynamic_index_in_dim(value, index, axis, keepdims=False)


def adapter_sum(down_grad, up_grad, kind, tasks):
    seq_count, kv_count = lax.axis_size("seq"), lax.axis_size("kv")
    seq_index, kv_index = lax.axis_index("seq"), lax.axis_index("kv")
    devices = seq_count * kv_count
    hidden = down_grad.shape[1]
    down_rows = down_grad.shape[0] // devices
    up_rows = up_grad.shape[0] // devices
    folds = up_grad.shape[1] // hidden
    down_part = down_grad.reshape(devices, down_rows, hidden)
    up_part = (
        up_grad.reshape(devices, up_rows, folds, hidden)
        .transpose(0, 2, 1, 3)
        .reshape(devices, folds * up_rows, hidden)
    )
    grad = jnp.concatenate([down_part, up_part], 1)
    height = grad.shape[1]
    core = seq_index % 2
    grad = grad.reshape(seq_count // 2, 2, kv_count, height, hidden)
    grad = pick(grad, 1, core) + swap(bfloat(pick(grad, 1, 1 - core)), 1, 0).astype(jnp.float32)
    x_bits, y_bits = plane_bits()
    by_task = []
    for task in range(tasks):
        part = grad * (kind == task).astype(jnp.float32)
        part = part.reshape([2] * (len(x_bits) + len(y_bits)) + [kv_count, height, hidden])
        order = (x_bits + y_bits, y_bits + x_bits)[task % 2]
        left = [bit for bit in reversed(x_bits + y_bits)]
        for bit in order:
            axis = left.index(bit)
            left.remove(bit)
            mine = (seq_index // bit) % 2
            part = pick(part, axis, mine) + swap(bfloat(pick(part, axis, 1 - mine)), bit, 0).astype(
                jnp.float32
            )
        by_task.append(part)
    part = jnp.stack(by_task, 1)
    total = pick(part, 0, kv_index)
    for step in range(1, kv_count):
        sent = bfloat(pick(part, 0, kv_index ^ step))
        total = total + swap(sent, 0, step).astype(jnp.float32)
    down_total = total[:, :down_rows]
    up_total = (
        total[:, down_rows:]
        .reshape(tasks, folds, up_rows, hidden)
        .transpose(0, 2, 1, 3)
        .reshape(tasks, up_rows, folds * hidden)
    )
    return (down_total, up_total)


def total_sum(value):
    step = 1
    while step < lax.axis_size("seq"):
        value = value + swap(value, step, 0)
        step *= 2
    step = 1
    while step < lax.axis_size("kv"):
        value = value + swap(value, 0, step)
        step *= 2
    return value


def item_rows(embeds):
    seq_count, kv_count = lax.axis_size("seq"), lax.axis_size("kv")
    kv_index = lax.axis_index("kv")
    got = []
    for turn in range(2):
        pairs = []
        for s in range(seq_count):
            for z in range(kv_count):
                source = (s - s % 2 + z % 2) * kv_count + 2 * (s % 2) + ((z // 2) ^ turn)
                pairs.append((source, s * kv_count + z))
        sent = pick(embeds[:, 0], 0, (kv_index % 2) ^ turn)
        got.append(lax.ppermute(sent, AXES, pairs))
    swapped = kv_index // 2 == 1
    return jnp.concatenate(
        [jnp.where(swapped, got[1], got[0]), jnp.where(swapped, got[0], got[1])]
    )


def adam_update(weight, first, second, grad, rate, decay, count_step):
    first_new = beta_one * first + (1.0 - beta_one) * grad
    second_new = beta_two * second + (1.0 - beta_two) * grad * grad
    first_hat = first_new / (1.0 - jnp.power(beta_one, count_step))
    second_hat = second_new / (1.0 - jnp.power(beta_two, count_step))
    weight_new = weight - rate * (
        first_hat / (jnp.sqrt(second_hat) + adam_epsilon) + decay * weight
    )
    return (weight_new, first_new, second_new)


def per_device(
    src_embed,
    tgt_embed,
    targets,
    src_len,
    tgt_len,
    task,
    step,
    attn_in,
    attn_out,
    ffn_in,
    ffn_out,
    embed,
    down_w,
    down_m,
    down_v,
    up_w,
    up_m,
    up_v,
    norm_params,
    norm_m,
    norm_v,
):
    seq_count, kv_count = lax.axis_size("seq"), lax.axis_size("kv")
    seq_index, kv_index = lax.axis_index("seq"), lax.axis_index("kv")
    devices = seq_count * kv_count
    width = attn_out.shape[2]
    hidden = ffn_in.shape[2]
    bottleneck = down_w.shape[3]
    tasks = down_w.shape[1]
    vocab_rows = embed.shape[0]
    vocab_total = vocab_rows * seq_count
    core = seq_index % 2
    batch = kv_index // 2
    item = seq_index - core + kv_index % 2
    source_length = src_len[batch, item]
    target_length = tgt_len[batch, item]
    kind = task[batch, item]
    count = jnp.sum(tgt_len).astype(jnp.float32)
    gains = norm_params[0]
    biases = norm_params[1]

    source = item_rows(src_embed)
    target = item_rows(tgt_embed)
    enc_rows = source.shape[0]
    dec_rows = target.shape[0]
    ids_all = lax.all_gather(targets, "kv", axis=2, tiled=True)

    share = width // devices
    up_low = bfloat(up_w).reshape(2 * tasks, up_w.shape[2], 2, bottleneck).transpose(0, 2, 1, 3)
    down_low = bfloat(down_w).reshape(2 * tasks, 2, share // 2, bottleneck)
    own = [
        jnp.concatenate([attn_in[0], attn_out[0]], 1)[None],
        jnp.concatenate([attn_in[1], attn_out[1]], 1)[None],
        ffn_in[0][None],
        jnp.concatenate([down_low, up_low]),
        ffn_out[0][None],
        jnp.concatenate([attn_in[2], attn_out[2]], 1)[None],
        ffn_in[1][None],
        ffn_out[1][None],
    ]
    attn_shapes = [(devices, share, 3 * width), (devices, share, width)]
    first_shapes = [(devices, share, hidden)]
    second_shapes = [(devices, hidden // devices, width)]
    adapter_shapes = [
        (2, devices, 2, share // 2, bottleneck),
        (2, 2, devices, up_w.shape[2], bottleneck),
    ]
    shapes = [
        attn_shapes,
        attn_shapes,
        first_shapes,
        adapter_shapes,
        second_shapes,
        attn_shapes,
        first_shapes,
        second_shapes,
    ]
    where = jnp.stack([seq_index * kv_count + kv_index, kind]).astype(jnp.int32)
    placed = []
    earlier = source
    for block, shape in zip(own[:-1], shapes[:-1]):
        pieces, earlier = gather_depth_first(block, earlier)
        placed.append(place_blocks(pieces, where, shape))
    placed.append(place_blocks(gather_plane_first(own[-1], earlier), where, shapes[-1]))
    attn_w = [
        (placed[g][0].reshape(width, 3 * width), placed[g][1].reshape(width, width))
        for g in (0, 1, 5)
    ]
    first_w = [placed[g][0].reshape(width, hidden) for g in (2, 6)]
    second_w = [placed[g][0].reshape(hidden, width) for g in (4, 7)]
    down_all = placed[3][0].reshape(2, width, bottleneck)
    up_all = placed[3][1].reshape(2, 2, bottleneck, bottleneck)
    up_all = jnp.concatenate([up_all[:, 0], up_all[:, 1]], 2)

    half = dec_rows // 2
    relative = seq_index ^ jnp.arange(seq_count, dtype=jnp.int32)
    row_items = relative - relative % 2 + kv_index % 2
    row_pos = (
        (relative % 2)[None, :, None] * dec_rows
        + jnp.arange(2, dtype=jnp.int32)[:, None, None] * half
        + jnp.arange(half, dtype=jnp.int32)[None, None, :]
    )
    plane_ids = pick(ids_all, 0, batch)
    row_ids = plane_ids[row_items[None, :, None], row_pos].reshape(-1)
    plane_lengths = pick(tgt_len, 0, batch)[row_items]
    alive = (row_pos < plane_lengths[None, :, None]).reshape(-1).astype(jnp.float32)
    live = alive / count
    local_ids = row_ids - seq_index * vocab_rows
    local_hit = (local_ids >= 0) & (local_ids < vocab_rows)
    target_rows = jnp.take(embed, jnp.clip(local_ids, 0, vocab_rows - 1), axis=0)
    target_rows = jnp.where(local_hit[:, None], target_rows, jnp.zeros((), jnp.bfloat16))
    table_sum = jnp.sum(embed.astype(jnp.float32), 0)
    tile = 1280
    table = jnp.pad(embed, ((0, -vocab_rows % tile), (0, 0)))

    enc_order = jnp.stack([core, 1 - core])[:, None] * enc_rows + jnp.arange(enc_rows)[None]
    dec_order = jnp.stack([core, 1 - core])[:, None] * dec_rows + jnp.arange(dec_rows)[None]
    src_keys = enc_order.reshape(-1)
    dec_keys = dec_order.reshape(-1)
    dec_query = core * dec_rows + jnp.arange(dec_rows)
    enc_mask = jnp.broadcast_to(src_keys[None, :] < source_length, (enc_rows, src_keys.shape[0]))
    self_mask = (dec_keys[None, :] <= dec_query[:, None]) & (dec_keys[None, :] < target_length)
    cross_mask = jnp.broadcast_to(src_keys[None, :] < source_length, (dec_rows, src_keys.shape[0]))

    x0, cache0 = norm_forward(source.astype(jnp.float32), gains[0], biases[0])
    x0_low = bfloat(x0)
    branch, enc_attn = attention_forward(x0_low, x0_low, *attn_w[0], enc_mask)
    x1, cache1 = norm_forward(x0 + branch, gains[1], biases[1])
    branch, enc_feed = feed_forward(x1, first_w[0], second_w[0], down_all[0], up_all[0])
    x2, cache2 = norm_forward(x1 + branch, gains[2], biases[2])
    y0, cache3 = norm_forward(target.astype(jnp.float32), gains[3], biases[3])
    y0_low = bfloat(y0)
    branch, self_attn = attention_forward(y0_low, y0_low, *attn_w[1], self_mask)
    y1, cache4 = norm_forward(y0 + branch, gains[4], biases[4])
    branch, cross_attn = attention_forward(bfloat(y1), bfloat(x2), *attn_w[2], cross_mask)
    y2, cache5 = norm_forward(y1 + branch, gains[5], biases[5])
    branch, dec_feed = feed_forward(y2, first_w[1], second_w[1], down_all[1], up_all[1])
    y3, cache6 = norm_forward(y2 + branch, gains[6], biases[6])

    x_bits, y_bits = plane_bits()
    orders = ([1] + x_bits + y_bits, [1] + y_bits + x_bits)
    y3_low = bfloat(y3)
    gathered = []
    for part, bits in zip((y3_low[:half], y3_low[half:]), orders):
        blocks = spread({0: part}, bits)
        gathered += [blocks[key] for key in sorted(blocks)]
    rows = jnp.concatenate(gathered)
    mixed, stats = vocab_pass(rows, table, vocab_rows, 512, tile)
    top = stats[:, 0].reshape(2, seq_count, half)
    total = stats[:, 64].reshape(2, seq_count, half)
    row_top, row_total = top, total
    for bit in [1] + x_bits + y_bits:
        flipped = [key ^ bit for key in range(seq_count)]
        got = swap(jnp.stack([row_top, row_total]), bit, 0)
        got = jnp.stack([got[:, :, key] for key in flipped], 2)
        best = jnp.maximum(row_top, got[0])
        row_total = row_total * jnp.exp(row_top - best) + got[1] * jnp.exp(got[0] - best)
        row_top = best
    logsum = (row_top + jnp.log(row_total)).reshape(-1)
    own_rows = (jnp.arange(seq_count) == 0).astype(jnp.float32)
    own_rows = jnp.broadcast_to(own_rows[None, :, None], row_top.shape).reshape(-1)
    linear = 0.9 * target_rows.astype(jnp.float32) + (0.1 / vocab_total) * table_sum[None]
    loss_part = jnp.sum(alive * own_rows * logsum) - jnp.sum(
        alive[:, None] * rows.astype(jnp.float32) * linear
    )
    row_scale = jnp.exp(top.reshape(-1) - logsum)
    share_grad = (mixed * row_scale[:, None] - linear) * live[:, None]
    share_grad = share_grad.reshape(2, seq_count, half, width)
    final_grad = jnp.concatenate(
        [
            halved_sum({key: share_grad[h, key] for key in range(seq_count)}, orders[h])[0]
            for h in range(2)
        ]
    )

    grad, grad6 = norm_backward(final_grad, cache6, gains[6])
    inner_grad, down_grad, up_grad = feed_backward(
        grad, dec_feed, first_w[1], second_w[1], down_all[1], up_all[1]
    )
    dec_sums = adapter_sum(down_grad, up_grad, kind, tasks)
    grad, grad5 = norm_backward(grad + inner_grad, cache5, gains[5])
    query_grad, enc_grad = attention_backward(grad, cross_attn, *attn_w[2], cross_mask)
    dec_grad, grad4 = norm_backward(grad + query_grad, cache4, gains[4])
    grad, grad2 = norm_backward(enc_grad, cache2, gains[2])
    inner_grad, down_grad, up_grad = feed_backward(
        grad, enc_feed, first_w[0], second_w[0], down_all[0], up_all[0]
    )
    enc_sums = adapter_sum(down_grad, up_grad, kind, tasks)
    query_grad, key_grad = attention_backward(dec_grad, self_attn, *attn_w[1], self_mask)
    _, grad3 = norm_backward(dec_grad + query_grad + key_grad, cache3, gains[3])
    grad, grad1 = norm_backward(grad + inner_grad, cache1, gains[1])
    query_grad, key_grad = attention_backward(grad, enc_attn, *attn_w[0], enc_mask)
    _, grad0 = norm_backward(grad + query_grad + key_grad, cache0, gains[0])

    norm_grad = jnp.stack([grad0, grad1, grad2, grad3, grad4, grad5, grad6], 1)
    down_part = jnp.stack([enc_sums[0], dec_sums[0]])
    up_part = jnp.stack([enc_sums[1], dec_sums[1]])
    square = jnp.sum(down_part * down_part) + jnp.sum(up_part * up_part)
    scalars = jnp.zeros((1, width), jnp.float32).at[0, 0].set(loss_part).at[0, 1].set(square)
    summed = total_sum(jnp.concatenate([norm_grad.reshape(-1, width), scalars]))
    norm_sum = summed[:-1].reshape(norm_grad.shape)
    loss_sum = summed[-1, 0]
    grad_norm = jnp.sqrt(summed[-1, 1] + jnp.sum(norm_sum * norm_sum))
    factor = clip_limit / jnp.maximum(grad_norm, clip_limit)
    count_step = step[0].astype(jnp.float32)
    down_new = adam_update(
        down_w, down_m, down_v, factor * down_part, rate_adapter, weight_decay, count_step
    )
    up_new = adam_update(up_w, up_m, up_v, factor * up_part, rate_adapter, weight_decay, count_step)
    norm_grad_out = factor * norm_sum
    norm_new = adam_update(norm_params, norm_m, norm_v, norm_grad_out, rate_norm, 0.0, count_step)
    return (
        loss_sum,
        count,
        grad_norm,
        down_new[0],
        down_new[1],
        down_new[2],
        up_new[0],
        up_new[1],
        up_new[2],
        norm_new[0],
        norm_new[1],
        norm_new[2],
        norm_grad_out,
    )


def solution(mesh):
    placed = (
        P(None, "seq", "kv", None),
        P(None, "seq", "kv", None),
        P(None, None, "kv"),
        P(),
        P(),
        P(),
        P(),
        P(None, ("seq", "kv"), None),
        P(None, ("seq", "kv"), None),
        P(None, ("seq", "kv"), None),
        P(None, ("seq", "kv"), None),
        P("seq", None),
        P(None, None, ("seq", "kv"), None),
        P(None, None, ("seq", "kv"), None),
        P(None, None, ("seq", "kv"), None),
        P(None, None, ("seq", "kv"), None),
        P(None, None, ("seq", "kv"), None),
        P(None, None, ("seq", "kv"), None),
        P(),
        P(),
        P(),
    )
    return jax.shard_map(
        per_device,
        mesh=mesh,
        in_specs=placed,
        out_specs=(
            P(),
            P(),
            P(),
            P(None, None, ("seq", "kv"), None),
            P(None, None, ("seq", "kv"), None),
            P(None, None, ("seq", "kv"), None),
            P(None, None, ("seq", "kv"), None),
            P(None, None, ("seq", "kv"), None),
            P(None, None, ("seq", "kv"), None),
            P(),
            P(),
            P(),
            P(),
        ),
        check_vma=False,
    )
```

time: 1790 us -> 2810 us (1.57)
  Pallas kernels: 0 us -> 1990 us
  waiting for transfers between devices: 1160 us -> 235 us
  matrix products: 361 us -> 163 us
  starting transfers between devices: 2.3 us -> 152 us
  blocking collectives: 74.3 us -> 19.3 us
  local copies, waits for them, and re-layouts: 65.7 us -> 116 us
    pallas_call x0 -> x9, Pallas kernels: none -> 1990 us  [the longest x8 1920 us: place_blocks(): pl.pallas_call(functools.partial(place_kernel, plan), grid_spec=pltpu.Pre...]
    all_gather x14 -> x0, waiting for transfers between devices: 697 us -> none  [the longest x1 126 us: per_device(): lax.all_gather(attn_in, ('seq', 'kv'), axis=1, tiled=True)]
    reduce_scatter x4 -> x0, waiting for transfers between devices: 426 us -> none  [the longest x1 184 us: reduce_grads(): lax.psum_scatter(up_grad, ('seq', 'kv'), scatter_dimension=2, tiled=True)]
    ppermute x0 -> x134, waiting for transfers between devices: none -> 235 us  [the longest x130 235 us: swap(): return lax.ppermute(value, AXES, pairs)]
    ppermute x0 -> x134, starting transfers between devices: none -> 152 us  [the longest x130 146 us: swap(): return lax.ppermute(value, AXES, pairs)]
    dot_general x32 -> x15, matrix products: 161 us -> 58.8 us  [times_second(): lax.dot_general(left, right, (((1,), (1,)), ((), ())), preferred_element_...]
    dot_general x36 -> x17, matrix products: 149 us -> 59.6 us  [times_plain(): return jnp.dot(left, right, preferred_element_type=jnp.float32)]
    psum x2 -> x0, blocking collectives: 60.9 us -> none  [the longest x1 38.4 us: reduce_grads(): norm_sum, loss_sum = lax.psum((norm_grad, loss_part), ('seq', 'kv'))]
  transfers between devices with their start and end apart: 24 -> 134, of which waited for: 20 -> 43; matrix products, arithmetic and copies ran while one was open for 17% -> 9% of each run, Pallas kernels for 0% -> 69%
where the time goes in v1:
time: 2810 us; the launch traced here: 2800 us
  Pallas kernels  1990 us (71%)
  waiting for transfers between devices  235 us (8%)
  matrix products  163 us (6%)
  starting transfers between devices  152 us (5%)
  local copies, waits for them, and re-layouts  116 us (4%)
  other arithmetic  107 us (4%)
    pallas_call x8, Pallas kernels, place_blocks(): pl.pallas_call(functools.partial(place_kernel, plan), grid_spec=pltpu.Pre...  1920 us
    ppermute x130, waiting for transfers between devices, swap(): return lax.ppermute(value, AXES, pairs)  235 us
    ppermute x130, starting transfers between devices, swap(): return lax.ppermute(value, AXES, pairs)  146 us
    pallas_call x1, Pallas kernels, vocab_pass(): pl.pallas_call(functools.partial(vocab_kernel, count, tile), grid=(total...  69.2 us
    dot_general x17, matrix products, times_plain(): return jnp.dot(left, right, preferred_element_type=jnp.float32)  59.6 us
    dot_general x15, matrix products, times_second(): lax.dot_general(left, right, (((1,), (1,)), ((), ())), preferred_element_...  58.8 us
  transfers between devices with their start and end apart: 134, of which 43 were waited for; matrix products, arithmetic and copies ran while one was open for 9% of the time, Pallas kernels for 69%

profile of v1, /device:TPU:0, one launch (start us, length us, event | category | flops | bytes accessed | tf_op | source)
XLA Modules:
  0.0 2800.7 jit_solution(17413715552685448611)
XLA Ops:
  23.2 19.3 all_gather.3
  74.3 12.2 collective-permute-start.53
  121.8 14.1 collective-permute-start.38
  158.7 14.3 collective-permute-done.30
  221.8 11.2 collective-permute-done.32
  233.8 17.7 collective-permute-done.28
  273.3 256.6 %shard_map.300 = (bf16[32,32,3072]{2,1,0:T(8,128)(2,1)}, bf16[32,32,1024]{2,1,0:T(8,128)(2,1)}) custom-call(s32[2]{0:T(128)} %pad_add_fusion.where_ref, bf16[2,2,1,32,4096]{4,3,2,1,0:T(8,128)(2,1)} %get-tuple-element.206.refs_0_, bf16[2,2,1,32,4096]{4,3,2,1,0:T(8,128)(2,1)} %bitcast.814, bf16[2,2,1,32,4096]{4,3,2,1,0:T(8,128)(2,1)} %copy-done.60, ...), custom_call_target="tpu_custom_call" | custom-call | tf_op jit(solution)/shard_map/pallas_call | solution.py:197
  539.1 16.2 collective-permute-done.17
  560.3 256.6 %shard_map.304 = (bf16[32,32,3072]{2,1,0:T(8,128)(2,1)}, bf16[32,32,1024]{2,1,0:T(8,128)(2,1)}) custom-call(s32[2]{0:T(128)} %pad_add_fusion.where_ref, bf16[2,2,1,32,4096]{4,3,2,1,0:T(8,128)(2,1)} %get-tuple-element.198.refs_0_, bf16[2,2,1,32,4096]{4,3,2,1,0:T(8,128)(2,1)} %bitcast.813, bf16[2,2,1,32,4096]{4,3,2,1,0:T(8,128)(2,1)} %copy-done.59, ...), custom_call_target="tpu_custom_call" | custom-call | tf_op jit(solution)/shard_map/pallas_call | solution.py:197
  830.8 256.2 %shard_map.301 = bf16[32,32,4096]{2,1,0:T(8,128)(2,1)} custom-call(s32[2]{0:T(128)} %pad_add_fusion.where_ref, bf16[2,2,1,32,4096]{4,3,2,1,0:T(8,128)(2,1)} %get-tuple-element.200.refs_0_, bf16[2,2,1,32,4096]{4,3,2,1,0:T(8,128)(2,1)} %bitcast.40.refs_1_, bf16[2,2,1,32,4096]{4,3,2,1,0:T(8,128)(2,1)} %copy-done.58, ...), custom_call_target="tpu_custom_call" | custom-call | tf_op jit(solution)/shard_map/pallas_call | solution.py:197
  1100.2 130.0 %shard_map.303 = (bf16[2,32,2,16,512]{4,3,2,1,0:T(8,128)(2,1)}, bf16[2,2,32,16,512]{4,3,2,1,0:T(8,128)(2,1)}) custom-call(s32[2]{0:T(128)} %pad_add_fusion.where_ref, bf16[2,2,8,2,16,512]{5,4,3,2,1,0:T(8,128)(2,1)} %pad_maximum_fusion.11.refs_0_, bf16[2,2,8,2,16,512]{5,4,3,2,1,0:T(8,128)(2,1)} %collective-permute-done.40.refs_1_, ...), custom_call_target="tpu_custom_call" | custom-call | tf_op jit(solution)/shard_map/pallas_call | solution.py:197
  1239.3 256.2 %shard_map.302 = bf16[32,128,1024]{2,1,0:T(8,128)(2,1)} custom-call(s32[2]{0:T(128)} %pad_add_fusion.where_ref, bf16[2,2,1,128,1024]{4,3,2,1,0:T(8,128)(2,1)} %get-tuple-element.202.refs_0_, bf16[2,2,1,128,1024]{4,3,2,1,0:T(8,128)(2,1)} %bitcast.54.refs_1_, bf16[2,2,1,128,1024]{4,3,2,1,0:T(8,128)(2,1)} %pad_maximum_fusion.10.refs_2_, ...), custom_call_target="tpu_custom_call" | custom-call | tf_op jit(solution)/shard_map/pallas_call | solution.py:197
  1508.1 256.2 %shard_map.307 = bf16[32,128,1024]{2,1,0:T(8,128)(2,1)} custom-call(s32[2]{0:T(128)} %pad_add_fusion.where_ref, bf16[4,1,1,128,1024]{4,3,2,1,0:T(8,128)(2,1)} %fusion.601.refs_0_, bf16[4,1,1,128,1024]{4,3,2,1,0:T(8,128)(2,1)} %bitcast.817, bf16[4,1,1,128,1024]{4,3,2,1,0:T(8,128)(2,1)} %bitcast.142.refs_2_, bf16[4,1,1,128,1024]{4,3,2,1,0:T(8,128)(2,1)} %bitcast.143.refs_3_, ...), custom_call_target="tpu_custom_call" | custom-call | tf_op jit(solution)/shard_map/pallas_call | solution.py:197
  1797.1 256.6 %shard_map.305 = (bf16[32,32,3072]{2,1,0:T(8,128)(2,1)}, bf16[32,32,1024]{2,1,0:T(8,128)(2,1)}) custom-call(s32[2]{0:T(128)} %pad_add_fusion.where_ref, bf16[2,2,1,32,4096]{4,3,2,1,0:T(8,128)(2,1)} %get-tuple-element.208.refs_0_, bf16[2,2,1,32,4096]{4,3,2,1,0:T(8,128)(2,1)} %bitcast.105.refs_1_, bf16[2,2,1,32,4096]{4,3,2,1,0:T(8,128)(2,1)} %pad_maximum_fusion.16.refs_2_, ...), custom_call_target="tpu_custom_call" | custom-call | tf_op jit(solution)/shard_map/pallas_call | solution.py:197
  2067.8 256.3 %shard_map.306 = bf16[32,32,4096]{2,1,0:T(8,128)(2,1)} custom-call(s32[2]{0:T(128)} %pad_add_fusion.where_ref, bf16[2,2,1,32,4096]{4,3,2,1,0:T(8,128)(2,1)} %get-tuple-element.194.refs_0_, bf16[2,2,1,32,4096]{4,3,2,1,0:T(8,128)(2,1)} %bitcast.127.refs_1_, bf16[2,2,1,32,4096]{4,3,2,1,0:T(8,128)(2,1)} %pad_maximum_fusion.18.refs_2_, ...), custom_call_target="tpu_custom_call" | custom-call | tf_op jit(solution)/shard_map/pallas_call | solution.py:197
  2348.7 11.0 fusion.518
  2370.9 13.0 gather_fusion
  2387.1 11.4 collective-permute-done.96
  2400.8 22.6 collective-permute-done.97
  2427.0 69.2 %shard_map.308 = (f32[2048,1024]{1,0:T(8,128)}, f32[2048,128]{1,0:T(8,128)}) custom-call(bf16[2048,1024]{1,0:T(8,128)(2,1)} %copy-done.39, bf16[6400,1024]{1,0:T(8,128)(2,1)} %pad.14.table_ref), custom_call_target="tpu_custom_call" | custom-call | flops 53687091200 | bytes 25690112 | tf_op jit(solution)/shard_map/pallas_call | solution.py:330
  2506.0 17.3 gather_fusion.1
  2553.2 12.2 collective-permute-done.108
  2582.6 13.2 multiply_reduce_fusion.5
  2660.1 13.0 multiply_reduce_fusion.17
  (1151 shorter events, 572.9 us)
Async XLA Ops:
  256.9 273.0 %collective-permute-start.56 = (bf16[2,2,1,32,4096]{4,3,1,2,0:T(8,128)(2,1)}, bf16[2,2,1,32,4096]{4,3,1,2,0:T(8,128)(2,1)}, u32[]{:S(2)}, u32[]{:S(2)}) collective-permute-start(bf16[2,2,1,32,4096]{4,3,1,2,0:T(8,128)(2,1)} %get-tuple-element.197), channel_id=1, source_target_pairs={{0,4},{1,5},{2,6},{3,7},{4,0},{5,1},{6,2},{7,3},{8,12},{9,13},{10,... | collective-permute-start | bytes 3145736 | tf_op jit(solution)/shard_map/ppermute | solution.py:85
  265.2 265.0 %collective-permute-start.21 = (bf16[2,2,1,32,4096]{4,3,2,1,0:T(8,128)(2,1)S(1)}, bf16[2,2,1,32,4096]{4,3,2,1,0:T(8,128)(2,1)}, u32[]{:S(2)}, u32[]{:S(2)}) collective-permute-start(bf16[2,2,1,32,4096]{4,3,2,1,0:T(8,128)(2,1)S(1)} %pad_maximum_fusion.8.refs_2_), channel_id=1, source_target_pairs={{0,8},{1,9},{2,10},{3,11},{4,12},{5,13},{6,14},{7,15},{8,0},{9,1},... | collective-permute-start | bytes 3145736 | tf_op jit(solution)/shard_map/ppermute | solution.py:85
  555.3 271.2 %collective-permute-start.43 = (bf16[2,2,8,2,16,512]{5,4,3,2,1,0:T(8,128)(2,1)S(1)}, bf16[2,2,8,2,16,512]{5,4,3,2,1,0:T(8,128)(2,1)}, u32[]{:S(2)}, u32[]{:S(2)}) collective-permute-start(bf16[2,2,8,2,16,512]{5,4,3,2,1,0:T(8,128)(2,1)S(1)} %pad_maximum_fusion.12.refs_2_), channel_id=1, source_target_pairs={{0,8},{1,9},{2,10},{3,11},{4,12},{5,13},{6,14},{7,15},{8,0},{9,1},... | collective-permute-start | bytes 3145736 | tf_op jit(solution)/shard_map/ppermute | solution.py:85
  555.7 271.0 %collective-permute-start.46 = (bf16[2,2,8,2,16,512]{5,4,3,2,1,0:T(8,128)(2,1)S(1)}, bf16[2,2,8,2,16,512]{5,4,3,2,1,0:T(8,128)(2,1)}, u32[]{:S(2)}, u32[]{:S(2)}) collective-permute-start(bf16[2,2,8,2,16,512]{5,4,3,2,1,0:T(8,128)(2,1)S(1)} %pad_maximum_fusion.12.refs_2_), channel_id=1, source_target_pairs={{0,4},{1,5},{2,6},{3,7},{4,0},{5,1},{6,2},{7,3},{8,12},{9,13},{10,... | collective-permute-start | bytes 3145736 | tf_op jit(solution)/shard_map/ppermute | solution.py:85
  555.8 272.2 %collective-permute-start.40 = (bf16[2,2,8,2,16,512]{5,4,3,2,1,0:T(8,128)(2,1)}, bf16[2,2,8,2,16,512]{5,4,3,2,1,0:T(8,128)(2,1)}, u32[]{:S(2)}, u32[]{:S(2)}) collective-permute-start(bf16[2,2,8,2,16,512]{5,4,3,2,1,0:T(8,128)(2,1)} %pad_maximum_fusion.11.refs_0_), channel_id=1, source_target_pairs={{0,16},{1,17},{2,18},{3,19},{4,20},{5,21},{6,22},{7,23},{8,24},{9,... | collective-permute-start | bytes 3145736 | tf_op jit(solution)/shard_map/ppermute | solution.py:85
  556.8 271.2 %collective-permute-start.25 = (bf16[2,2,1,32,4096]{4,3,2,1,0:T(8,128)(2,1)}, bf16[2,2,1,32,4096]{4,3,2,1,0:T(8,128)(2,1)}, u32[]{:S(2)}, u32[]{:S(2)}) collective-permute-start(bf16[2,2,1,32,4096]{4,3,2,1,0:T(8,128)(2,1)} %collective-permute-done.21.refs_3_), channel_id=1, source_target_pairs={{0,4},{1,5},{2,6},{3,7},{4,0},{5,1},{6,2},{7,3},{8,12},{9,13},{10,... | collective-permute-start | bytes 3145736 | tf_op jit(solution)/shard_map/ppermute | solution.py:85
  557.0 271.5 %collective-permute-start.23 = (bf16[2,2,1,32,4096]{4,3,1,2,0:T(8,128)(2,1)}, bf16[2,2,1,32,4096]{4,3,1,2,0:T(8,128)(2,1)}, u32[]{:S(2)}, u32[]{:S(2)}) collective-permute-start(bf16[2,2,1,32,4096]{4,3,1,2,0:T(8,128)(2,1)} %collective-permute-done.17), channel_id=1, source_target_pairs={{0,4},{1,5},{2,6},{3,7},{4,0},{5,1},{6,2},{7,3},{8,12},{9,13},{10,... | collective-permute-start | bytes 3145736 | tf_op jit(solution)/shard_map/ppermute | solution.py:85
  826.7 266.0 %collective-permute-start.33 = (bf16[2,2,1,128,1024]{4,3,2,1,0:T(8,128)(2,1)}, bf16[2,2,1,128,1024]{4,3,2,1,0:T(8,128)(2,1)}, u32[]{:S(2)}, u32[]{:S(2)}) collective-permute-start(bf16[2,2,1,128,1024]{4,3,2,1,0:T(8,128)(2,1)} %pad_maximum_fusion.10.refs_2_), channel_id=1, source_target_pairs={{0,8},{1,9},{2,10},{3,11},{4,12},{5,13},{6,14},{7,15},{8,0},{9,1},... | collective-permute-start | bytes 3145736 | tf_op jit(solution)/shard_map/ppermute | solution.py:85
  828.0 264.9 %collective-permute-start.36 = (bf16[2,2,1,128,1024]{4,3,2,1,0:T(8,128)(2,1)}, bf16[2,2,1,128,1024]{4,3,2,1,0:T(8,128)(2,1)}, u32[]{:S(2)}, u32[]{:S(2)}) collective-permute-start(bf16[2,2,1,128,1024]{4,3,2,1,0:T(8,128)(2,1)} %pad_maximum_fusion.10.refs_2_), channel_id=1, source_target_pairs={{0,4},{1,5},{2,6},{3,7},{4,0},{5,1},{6,2},{7,3},{8,12},{9,13},{10,... | collective-permute-start | bytes 3145736 | tf_op jit(solution)/shard_map/ppermute | solution.py:85
  828.0 265.1 %collective-permute-start.47 = (bf16[2,2,8,2,16,512]{5,4,3,2,1,0:T(8,128)(2,1)}, bf16[2,2,8,2,16,512]{5,4,3,2,1,0:T(8,128)(2,1)}, u32[]{:S(2)}, u32[]{:S(2)}) collective-permute-start(bf16[2,2,8,2,16,512]{5,4,3,2,1,0:T(8,128)(2,1)} %collective-permute-done.43.refs_3_), channel_id=1, source_target_pairs={{0,4},{1,5},{2,6},{3,7},{4,0},{5,1},{6,2},{7,3},{8,12},{9,13},{10,... | collective-permute-start | bytes 3145736 | tf_op jit(solution)/shard_map/ppermute | solution.py:85
  828.5 268.0 %collective-permute-start.45 = (bf16[2,2,8,2,16,512]{5,4,3,2,1,0:T(8,128)(2,1)}, bf16[2,2,8,2,16,512]{5,4,3,2,1,0:T(8,128)(2,1)}, u32[]{:S(2)}, u32[]{:S(2)}) collective-permute-start(bf16[2,2,8,2,16,512]{5,4,3,2,1,0:T(8,128)(2,1)} %collective-permute-done.40.refs_1_), channel_id=1, source_target_pairs={{0,4},{1,5},{2,6},{3,7},{4,0},{5,1},{6,2},{7,3},{8,12},{9,13},{10,... | collective-permute-start | bytes 3145736 | tf_op jit(solution)/shard_map/ppermute | solution.py:85
  1230.2 265.3 %collective-permute-start.91 = (bf16[4,1,1,128,1024]{4,3,0,2,1:T(8,128)(2,1)}, bf16[4,1,1,128,1024]{4,3,0,2,1:T(8,128)(2,1)}, u32[]{:S(2)}, u32[]{:S(2)}) collective-permute-start(bf16[4,1,1,128,1024]{4,3,0,2,1:T(8,128)(2,1)} %fusion.600), channel_id=1, source_target_pairs={{0,4},{1,5},{2,6},{3,7},{4,0},{5,1},{6,2},{7,3},{8,12},{9,13},{10,... | collective-permute-start | bytes 3145736 | tf_op jit(solution)/shard_map/ppermute | solution.py:85
  1231.5 265.1 %collective-permute-start.92 = (bf16[4,1,1,128,1024]{4,3,0,2,1:T(8,128)(2,1)S(1)}, bf16[4,1,1,128,1024]{4,3,0,2,1:T(8,128)(2,1)}, u32[]{:S(2)}, u32[]{:S(2)}) collective-permute-start(bf16[4,1,1,128,1024]{4,3,0,2,1:T(8,128)(2,1)S(1)} %bitcast.816), channel_id=1, source_target_pairs={{0,4},{1,5},{2,6},{3,7},{4,0},{5,1},{6,2},{7,3},{8,12},{9,13},{10,... | collective-permute-start | bytes 3145736 | tf_op jit(solution)/shard_map/ppermute | solution.py:85
  1231.5 265.3 %collective-permute-start.93 = (bf16[4,1,1,128,1024]{4,3,0,2,1:T(8,128)(2,1)}, bf16[4,1,1,128,1024]{4,3,0,2,1:T(8,128)(2,1)}, u32[]{:S(2)}, u32[]{:S(2)}) collective-permute-start(bf16[4,1,1,128,1024]{4,3,0,2,1:T(8,128)(2,1)} %bitcast.141), channel_id=1, source_target_pairs={{0,4},{1,5},{2,6},{3,7},{4,0},{5,1},{6,2},{7,3},{8,12},{9,13},{10,... | collective-permute-start | bytes 3145736 | tf_op jit(solution)/shard_map/ppermute | solution.py:85
  1238.8 532.5 %collective-permute-start.67 = (bf16[2,2,1,32,4096]{4,3,2,1,0:T(8,128)(2,1)}, bf16[2,2,1,32,4096]{4,3,2,1,0:T(8,128)(2,1)}, u32[]{:S(2)}, u32[]{:S(2)}) collective-permute-start(bf16[2,2,1,32,4096]{4,3,2,1,0:T(8,128)(2,1)} %pad_maximum_fusion.16.refs_2_), channel_id=1, source_target_pairs={{0,8},{1,9},{2,10},{3,11},{4,12},{5,13},{6,14},{7,15},{8,0},{9,1},... | collective-permute-start | bytes 3145736 | tf_op jit(solution)/shard_map/ppermute | solution.py:85
  1495.5 277.3 %collective-permute-start.70 = (bf16[2,2,1,32,4096]{4,3,2,1,0:T(8,128)(2,1)}, bf16[2,2,1,32,4096]{4,3,2,1,0:T(8,128)(2,1)}, u32[]{:S(2)}, u32[]{:S(2)}) collective-permute-start(bf16[2,2,1,32,4096]{4,3,2,1,0:T(8,128)(2,1)} %pad_maximum_fusion.16.refs_2_), channel_id=1, source_target_pairs={{0,4},{1,5},{2,6},{3,7},{4,0},{5,1},{6,2},{7,3},{8,12},{9,13},{10,... | collective-permute-start | bytes 3145736 | tf_op jit(solution)/shard_map/ppermute | solution.py:85
  1495.6 277.1 %collective-permute-start.63 = (bf16[2,2,1,32,4096]{4,3,1,2,0:T(8,128)(2,1)}, bf16[2,2,1,32,4096]{4,3,1,2,0:T(8,128)(2,1)}, u32[]{:S(2)}, u32[]{:S(2)}) collective-permute-start(bf16[2,2,1,32,4096]{4,3,1,2,0:T(8,128)(2,1)} %get-tuple-element.207), channel_id=1, source_target_pairs={{0,16},{1,17},{2,18},{3,19},{4,20},{5,21},{6,22},{7,23},{8,24},{9,... | collective-permute-start | bytes 3145736 | tf_op jit(solution)/shard_map/ppermute | solution.py:85
  1496.8 268.8 %collective-permute-start.60 = (bf16[256,2048]{1,0:T(8,128)(2,1)}, bf16[256,2048]{1,0:T(8,128)(2,1)}, u32[]{:S(2)}, u32[]{:S(2)}) collective-permute-start(bf16[256,2048]{1,0:T(8,128)(2,1)} %fusion.31), channel_id=1, source_target_pairs={{0,4},{1,5},{2,6},{3,7},{4,0},{5,1},{6,2},{7,3},{8,12},{9,13},{10,... | collective-permute-start | bytes 3145736 | tf_op jit(solution)/shard_map/ppermute | solution.py:85
  1507.1 277.5 %collective-permute-start.68 = (bf16[2,2,1,32,4096]{4,3,1,2,0:T(8,128)(2,1)}, bf16[2,2,1,32,4096]{4,3,1,2,0:T(8,128)(2,1)}, u32[]{:S(2)}, u32[]{:S(2)}) collective-permute-start(bf16[2,2,1,32,4096]{4,3,1,2,0:T(8,128)(2,1)} %get-tuple-element.207), channel_id=1, source_target_pairs={{0,4},{1,5},{2,6},{3,7},{4,0},{5,1},{6,2},{7,3},{8,12},{9,13},{10,... | collective-permute-start | bytes 3145736 | tf_op jit(solution)/shard_map/ppermute | solution.py:85
  1784.6 283.1 %collective-permute-start.82 = (bf16[2,2,1,32,4096]{4,3,2,1,0:T(8,128)(2,1)}, bf16[2,2,1,32,4096]{4,3,2,1,0:T(8,128)(2,1)}, u32[]{:S(2)}, u32[]{:S(2)}) collective-permute-start(bf16[2,2,1,32,4096]{4,3,2,1,0:T(8,128)(2,1)} %pad_maximum_fusion.18.refs_2_), channel_id=1, source_target_pairs={{0,4},{1,5},{2,6},{3,7},{4,0},{5,1},{6,2},{7,3},{8,12},{9,13},{10,... | collective-permute-start | bytes 3145736 | tf_op jit(solution)/shard_map/ppermute | solution.py:85
  1791.1 276.7 %collective-permute-start.80 = (bf16[2,2,1,32,4096]{4,3,1,2,0:T(8,128)(2,1)}, bf16[2,2,1,32,4096]{4,3,1,2,0:T(8,128)(2,1)}, u32[]{:S(2)}, u32[]{:S(2)}) collective-permute-start(bf16[2,2,1,32,4096]{4,3,1,2,0:T(8,128)(2,1)} %get-tuple-element.193), channel_id=1, source_target_pairs={{0,4},{1,5},{2,6},{3,7},{4,0},{5,1},{6,2},{7,3},{8,12},{9,13},{10,... | collective-permute-start | bytes 3145736 | tf_op jit(solution)/shard_map/ppermute | solution.py:85
  1796.6 271.2 %collective-permute-start.83 = (bf16[2,2,1,32,4096]{4,3,2,1,0:T(8,128)(2,1)}, bf16[2,2,1,32,4096]{4,3,2,1,0:T(8,128)(2,1)}, u32[]{:S(2)}, u32[]{:S(2)}) collective-permute-start(bf16[2,2,1,32,4096]{4,3,2,1,0:T(8,128)(2,1)} %collective-permute-done.79.refs_3_), channel_id=1, source_target_pairs={{0,4},{1,5},{2,6},{3,7},{4,0},{5,1},{6,2},{7,3},{8,12},{9,13},{10,... | collective-permute-start | bytes 3145736 | tf_op jit(solution)/shard_map/ppermute | solution.py:85
  1796.6 271.2 %collective-permute-start.81 = (bf16[2,2,1,32,4096]{4,3,1,2,0:T(8,128)(2,1)}, bf16[2,2,1,32,4096]{4,3,1,2,0:T(8,128)(2,1)}, u32[]{:S(2)}, u32[]{:S(2)}) collective-permute-start(bf16[2,2,1,32,4096]{4,3,1,2,0:T(8,128)(2,1)} %collective-permute-done.75), channel_id=1, source_target_pairs={{0,4},{1,5},{2,6},{3,7},{4,0},{5,1},{6,2},{7,3},{8,12},{9,13},{10,... | collective-permute-start | bytes 3145736 | tf_op jit(solution)/shard_map/ppermute | solution.py:85
  2057.5 266.6 %collective-permute-start.72 = (bf16[128,2048]{1,0:T(8,128)(2,1)}, bf16[128,2048]{1,0:T(8,128)(2,1)S(1)}, u32[]{:S(2)}, u32[]{:S(2)}) collective-permute-start(bf16[128,2048]{1,0:T(8,128)(2,1)} %fusion.37), channel_id=1, source_target_pairs={{0,4},{1,5},{2,6},{3,7},{4,0},{5,1},{6,2},{7,3},{8,12},{9,13},{10,... | collective-permute-start | bytes 1572872 | tf_op jit(solution)/shard_map/ppermute | solution.py:85
  (390 other events, 22960.6 us)

commit v2 on v0

v2 whole, which is shorter than its diff:
```python
import functools

import jax
import jax.numpy as jnp
from jax import lax
from jax.experimental import pallas as pl
from jax.experimental.pallas import tpu as pltpu
from jax.sharding import PartitionSpec as P

HDIM = 64


norm_epsilon = 1e-05
score_scale = 0.125
clip_limit = 0.02
beta_one = 0.9
beta_two = 0.999
adam_epsilon = 1e-08
rate_adapter = 0.03
rate_norm = 0.25
weight_decay = 0.01


def bfloat(value):
    return value.astype(jnp.bfloat16)


def times_plain(left, right):
    return jnp.dot(left, right, preferred_element_type=jnp.float32)


def times_first(left, right):
    return lax.dot_general(
        left, right, (((0,), (0,)), ((), ())), preferred_element_type=jnp.float32
    )


def times_second(left, right):
    return lax.dot_general(
        left, right, (((1,), (1,)), ((), ())), preferred_element_type=jnp.float32
    )


def norm_forward(value, gain, bias):
    centered = value - jnp.mean(value, -1, keepdims=True)
    inverse = lax.rsqrt(jnp.mean(centered * centered, -1, keepdims=True) + norm_epsilon)
    normed = centered * inverse
    return (normed * gain + bias, (normed, inverse))


def norm_backward(grad, cache, gain):
    normed, inverse = cache
    scaled = grad * gain
    value_grad = inverse * (
        scaled
        - jnp.mean(scaled, -1, keepdims=True)
        - normed * jnp.mean(scaled * normed, -1, keepdims=True)
    )
    return (value_grad, jnp.stack([jnp.sum(grad * normed, 0), jnp.sum(grad, 0)]))


def gelu_slope(value):
    return (
        0.5 * (1.0 + lax.erf(value * 0.7071067811865476))
        + value * jnp.exp(-0.5 * value * value) * 0.3989422804014327
    )


AXES = ("seq", "kv")
MEBI = 2**20
LOWEST = -3e38
LIVE_ROWS = 64
LIGHT = pl.CostEstimate(flops=1, bytes_accessed=1, transcendentals=0)


def swap(value, seq_mask, kv_mask):
    seq_count, kv_count = lax.axis_size("seq"), lax.axis_size("kv")
    pairs = [
        (s * kv_count + z, (s ^ seq_mask) * kv_count + (z ^ kv_mask))
        for s in range(seq_count)
        for z in range(kv_count)
    ]
    return lax.ppermute(value, AXES, pairs)


def trade_bits(value):
    seq_count, kv_count = lax.axis_size("seq"), lax.axis_size("kv")
    pairs = [
        (s * kv_count + z, (s - s % 4 + 2 * (s % 2) + s // 2 % 2) * kv_count + z)
        for s in range(seq_count)
        for z in range(kv_count)
    ]
    return lax.ppermute(value, AXES, pairs)


def plane_bits():
    count = lax.axis_size("seq").bit_length() - 2
    bits = [2 << place for place in range(count)]
    return (bits[: count // 2], bits[count // 2 :])


def after(value, earlier):
    return lax.optimization_barrier((value, earlier))[0]


def pick(value, axis, index):
    return lax.dynamic_index_in_dim(value, index, axis, keepdims=False)


def in_order(core, mine, other):
    first = core == 0
    return (jnp.where(first, mine, other), jnp.where(first, other, mine))


def core_sum(value):
    return value + swap(bfloat(value), 1, 0).astype(jnp.float32)


def core_columns(value, lead):
    seq_count = lax.axis_size("seq")
    total = value.shape[-1]
    chunk = total // seq_count
    parts = value.reshape(value.shape[:-1] + (seq_count // (2 * lead), 2, lead * chunk))
    flat = value.shape[:-1] + (total // 2,)
    return (parts[..., 0, :].reshape(flat), parts[..., 1, :].reshape(flat))


def plane_steps(stacks, orders, firsts):
    labels = [[0] for _ in stacks]
    for turn in range(len(orders[0])):
        got = [swap(stack, bits[turn], 0) for stack, bits in zip(stacks, orders)]
        done = yield list(stacks) + got
        stacks, got = done[: len(stacks)], done[len(stacks) :]
        fresh = [[label | bits[turn] for label in old] for old, bits in zip(labels, orders)]
        if turn == len(orders[0]) - 1:
            break
        stacks = [jnp.concatenate(pair) for pair in zip(stacks, got)]
        labels = [old + new for old, new in zip(labels, fresh)]
    return [
        piece
        for old, new, first, stack, other in zip(labels, fresh, firsts, stacks, got)
        for piece in ((old, first, stack), (new, first, other))
    ]


def column_first_steps(own):
    (column,) = yield [lax.all_gather(own, "kv")]
    half = column.shape[0] // 2
    x_bits, y_bits = plane_bits()
    orders = (x_bits + y_bits, y_bits + x_bits)
    return (yield from plane_steps([column[None, :half], column[None, half:]], orders, (0, half)))


def plane_first_steps(own):
    x_bits, y_bits = plane_bits()
    half = own.shape[1] // 2
    orders = (x_bits + y_bits, y_bits + x_bits)
    parts = [own[None, None, :, :half], own[None, None, :, half:]]
    pieces = yield from plane_steps(parts, orders, (0, 0))
    stacks = []
    for first, second in (pieces[:2], pieces[2:]):
        labels = first[0] + second[0]
        stack = jnp.concatenate([first[2], second[2]])[:, 0]
        stacks.append(jnp.stack([stack[labels.index(label)] for label in sorted(labels)]))
    return (sorted(labels), jnp.concatenate(stacks, 2))


def run_rounds(starts, extras):
    live = {}
    results = {}
    turn = 0
    made = {}
    while turn < len(starts) or live:
        if turn < len(starts):
            for name, steps in starts[turn](made):
                live[name] = (steps, None)
        values, spans = [], {}
        for name, (steps, sent) in list(live.items()):
            try:
                out = steps.send(sent)
            except StopIteration as stop:
                results[name] = stop.value
                made[name] = stop.value
                del live[name]
                continue
            spans[name] = (len(values), len(values) + len(out))
            values += out
        if not values:
            turn += 1
            continue
        more = extras.get(turn, lambda made: {})(made)
        names = list(more)
        leaves, shape = jax.tree.flatten([more[name] for name in names])
        values = lax.optimization_barrier(tuple(values) + tuple(leaves))
        for name, (first, last) in spans.items():
            live[name] = (live[name][0], list(values[first:last]))
        made.update(zip(names, jax.tree.unflatten(shape, values[len(values) - len(leaves) :])))
        made["tie"] = values[0]
        turn += 1
    return results, made


def place_kernel(plan, form, where_ref, *refs):
    sources = refs[: len(plan)]
    count = (len(refs) - len(plan) - 2) // 2
    targets = refs[len(plan) : len(plan) + count]
    staged = refs[len(plan) + count : len(plan) + 2 * count]
    in_sems, out_sems = refs[-2:]
    own = where_ref[0]
    kind = where_ref[1]
    copies = []
    for source, (labels, first) in zip(sources, plan):
        for place, label in enumerate(labels):
            chip = own ^ (label // 2)
            for step in range(source.shape[1]):
                block = source.at[place, step]
                z = first + step
                if form == "attention":
                    split = staged[0].shape[-1]
                    half = staged[1].shape[-1]
                    for side in range(2):
                        copies.append((block.at[side, :, :split], 0, (chip, side, z)))
                        copies.append((block.at[side, :, split:], 1, (side, chip, z)))
                elif form == "first":
                    for side in range(2):
                        copies.append((block.at[side], 0, (chip, side, z)))
                elif form == "second":
                    copies.append((block.at[0], 0, (chip, z)))
                else:
                    for layer in range(2):
                        down = block.at[2 * layer + kind]
                        for side in range(2):
                            copies.append((down.at[side], 0, (layer, chip, side, z)))
                        up = block.at[4 + 2 * layer + kind]
                        for fold in range(4):
                            copies.append((up.at[fold // 2, fold % 2], 1, (layer, fold, chip, z)))
    started = []
    for place, (origin, turn, index) in enumerate(copies):
        copy = pltpu.make_async_copy(origin, staged[turn].at[index], in_sems.at[place])
        copy.start()
        started.append(copy)
    ended = []
    for place, (origin, turn, index) in enumerate(copies):
        started[place].wait()
        copy = pltpu.make_async_copy(
            staged[turn].at[index], targets[turn].at[index], out_sems.at[place]
        )
        copy.start()
        ended.append(copy)
    for copy in ended:
        copy.wait()


def place_blocks(pieces, where, form, shapes):
    plan = [(labels, first) for labels, first, _ in pieces]
    blocks = sum(len(labels) * stack.shape[1] for labels, _, stack in pieces)
    copies = blocks * {"attention": 4, "first": 2, "second": 1, "adapter": 12}[form]
    anywhere = pl.BlockSpec(memory_space=pl.ANY)
    return pl.pallas_call(
        functools.partial(place_kernel, plan, form),
        grid_spec=pltpu.PrefetchScalarGridSpec(
            num_scalar_prefetch=1,
            grid=(1,),
            in_specs=[anywhere] * len(pieces),
            out_specs=[anywhere] * len(shapes),
            scratch_shapes=[pltpu.VMEM(shape, jnp.bfloat16) for shape in shapes]
            + [pltpu.SemaphoreType.DMA((copies,))] * 2,
        ),
        out_shape=[jax.ShapeDtypeStruct(shape, jnp.bfloat16) for shape in shapes],
        compiler_params=pltpu.CompilerParams(vmem_limit_bytes=24 * MEBI),
        cost_estimate=LIGHT,
    )(where, *[stack for _, _, stack in pieces])


def head_scores(length, causal, query, keys):
    scores = times_second(query, keys) * score_scale
    key = lax.broadcasted_iota(jnp.int32, scores.shape, 1)
    mask = key < length
    if causal:
        mask = mask & (key <= lax.broadcasted_iota(jnp.int32, scores.shape, 0))
    return jnp.where(mask, scores, -1000000000.0)


def softmax(scores):
    weights = jnp.exp(scores - jnp.max(scores, 1, keepdims=True))
    return weights * (1.0 / jnp.sum(weights, 1, keepdims=True))


def one_head(value, head):
    lane = lax.broadcasted_iota(jnp.int32, value.shape, 1)
    return jnp.where(lane // HDIM == head, value, jnp.zeros((), value.dtype))


def attention_kernel(causal, length_ref, query_ref, key_ref, value_ref, out_ref):
    query, keys, values = query_ref[...], key_ref[...], value_ref[...]
    out = jnp.zeros(out_ref.shape, jnp.float32)
    for head in range(query.shape[1] // HDIM):
        scores = head_scores(length_ref[0], causal, query, one_head(keys, head))
        out = out + times_plain(bfloat(softmax(scores)), one_head(values, head))
    out_ref[...] = bfloat(out)


def attention_grad_kernel(
    causal, length_ref, query_ref, key_ref, value_ref, out_ref, query_out, key_out, value_out
):
    query, keys, values, out_grad = query_ref[...], key_ref[...], value_ref[...], out_ref[...]
    query_grad = jnp.zeros(query.shape, jnp.float32)
    key_grad = jnp.zeros(keys.shape, jnp.float32)
    value_grad = jnp.zeros(values.shape, jnp.float32)
    for head in range(query.shape[1] // HDIM):
        head_keys = one_head(keys, head)
        head_out = one_head(out_grad, head)
        probs = softmax(head_scores(length_ref[0], causal, query, head_keys))
        prob_grad = times_second(head_out, values)
        spread = jnp.sum(probs * prob_grad, 1, keepdims=True)
        score_grad = bfloat(probs * (prob_grad - spread))
        value_grad = value_grad + times_first(bfloat(probs), head_out)
        query_grad = query_grad + times_plain(score_grad, head_keys)
        key_grad = key_grad + times_first(score_grad, one_head(query, head))
    query_out[...] = bfloat(query_grad * score_scale)
    key_out[...] = bfloat(key_grad * score_scale)
    value_out[...] = bfloat(value_grad)


def attention_call(kernel, length, causal, arrays, outs):
    lanes = 2 * HDIM
    columns = outs[0][1]

    def spec(rows, first):
        return pl.BlockSpec((rows, lanes), lambda i, _: (0, i + first // lanes))

    return pl.pallas_call(
        functools.partial(kernel, causal),
        grid_spec=pltpu.PrefetchScalarGridSpec(
            num_scalar_prefetch=1,
            grid=(columns // lanes,),
            in_specs=[spec(array.shape[0], first) for array, first in arrays],
            out_specs=[spec(rows, 0) for rows, _ in outs],
        ),
        out_shape=[jax.ShapeDtypeStruct(out, jnp.bfloat16) for out in outs],
        compiler_params=pltpu.CompilerParams(vmem_limit_bytes=48 * MEBI),
        cost_estimate=LIGHT,
    )(length.reshape(1), *[array for array, _ in arrays])


def attend(length, causal, query, pair):
    rows = query[0].shape[0]
    width = pair[0].shape[1] - pair[1]
    half = width // 2
    arrays = [query, pair, (pair[0], pair[1] + half)]
    return attention_call(attention_kernel, length, causal, arrays, [(rows, half)])[0]


def attend_back(length, causal, query, pair, out_grad):
    rows = query[0].shape[0]
    keys = pair[0].shape[0]
    half = (pair[0].shape[1] - pair[1]) // 2
    arrays = [query, pair, (pair[0], pair[1] + half), (out_grad, 0)]
    outs = [(rows, half), (keys, half), (keys, half)]
    return attention_call(attention_grad_kernel, length, causal, arrays, outs)


def gelu_pair(value):
    phi = 0.5 * (1.0 + lax.erf(value * 0.7071067811865476))
    slope = phi + value * jnp.exp(-0.5 * value * value) * 0.3989422804014327
    return lax.optimization_barrier((bfloat(value * phi), slope))


def feed_forward(low_in, w_first, w_second, down, upward):
    hidden = times_plain(low_in, w_first)
    inner = times_plain(low_in, down)
    hidden_low, slope = gelu_pair(hidden)
    inner_low, inner_slope = gelu_pair(inner)
    branch = times_plain(hidden_low, w_second) + 4.0 * times_plain(inner_low, upward)
    return (branch, (low_in, slope, inner_slope, inner_low))


def feed_backward(grad, cache, w_first, w_second, down, upward):
    low_in, slope, inner_slope, inner_low = cache
    hidden_grad = bfloat(times_second(bfloat(grad), w_second) * slope)
    adapter_grad = bfloat(4.0 * grad)
    upward_grad = times_first(inner_low, adapter_grad)
    inner_grad = bfloat(times_second(adapter_grad, upward) * inner_slope)
    down_grad = times_first(low_in, inner_grad)
    value_grad = times_second(hidden_grad, w_first) + times_second(inner_grad, down)
    return (value_grad, down_grad, upward_grad)


def vocab_kernel(
    count, tile, step, order_ref, rows_ref, table_ref, mixed_ref, stats_ref,
    scores, table, mixed, stats, table_sems, out_sems,
):
    parts = step // LIVE_ROWS
    turn = pl.program_id(0)
    alive = order_ref[order_ref.shape[0] - 1]
    padded = table.shape[0]
    tiles = range(0, padded, tile)

    def table_copy(place):
        span = slice(place * tile, (place + 1) * tile)
        return pltpu.make_async_copy(table_ref.at[span], table.at[span], table_sems.at[place])

    def out_copies(first):
        copies = []
        for part in range(parts):
            row = pl.multiple_of(order_ref[first + part] * LIVE_ROWS, LIVE_ROWS)
            span = slice(part * LIVE_ROWS, (part + 1) * LIVE_ROWS)
            for place, (origin, target) in enumerate(((mixed, mixed_ref), (stats, stats_ref))):
                copies.append(
                    pltpu.make_async_copy(
                        origin.at[span],
                        target.at[pl.ds(row, LIVE_ROWS)],
                        out_sems.at[place, part],
                    )
                )
        return copies

    @pl.when(turn == 0)
    def _():
        for place in range(len(tiles)):
            table_copy(place).start()
        for place in range(len(tiles)):
            table_copy(place).wait()

    first = turn * parts

    @pl.when(first < alive)
    def _():
        places = [
            pl.ds(pl.multiple_of(order_ref[first + part] * LIVE_ROWS, LIVE_ROWS), LIVE_ROWS)
            for part in range(parts)
        ]
        rows = jnp.concatenate([rows_ref[place, :] for place in places])
        top = jnp.full((step, 1), LOWEST, jnp.float32)
        for start in tiles:
            part = times_second(rows, table[start : start + tile, :])
            if start + tile > count:
                entry = lax.broadcasted_iota(jnp.int32, part.shape, 1) + start
                part = jnp.where(entry < count, part, LOWEST)
            scores[:, start : start + tile] = part
            top = jnp.maximum(top, jnp.max(part, 1, keepdims=True))
        total = jnp.zeros((step, 1), jnp.float32)
        mix = jnp.zeros((step, rows.shape[1]), jnp.float32)
        for start in tiles:
            weights = jnp.exp(scores[:, start : start + tile] - top)
            total = total + jnp.sum(weights, 1, keepdims=True)
            mix = mix + times_plain(bfloat(weights), table[start : start + tile, :])

        @pl.when(turn > 0)
        def _():
            for copy in out_copies(first - parts):
                copy.wait()

        mixed[...] = mix
        stats[...] = jnp.concatenate(
            [jnp.broadcast_to(top, (step, 64)), jnp.broadcast_to(total, (step, 64))], 1
        )
        for copy in out_copies(first):
            copy.start()

        @pl.when(first + parts >= alive)
        def _():
            for copy in out_copies(first):
                copy.wait()


def vocab_pass(rows, live_blocks, table, count, step, tile):
    total, width = rows.shape
    padded = table.shape[0]
    flags = live_blocks.astype(jnp.int32)
    alive_count = jnp.sum(flags)
    rank = jnp.where(
        live_blocks, jnp.cumsum(flags) - 1, alive_count + jnp.cumsum(1 - flags) - 1
    )
    ids = jnp.arange(flags.shape[0], dtype=jnp.int32)
    order = jnp.sum(jnp.where(rank[None, :] == ids[:, None], ids[None, :], 0), 1)
    order = jnp.concatenate([order, alive_count[None]]).astype(jnp.int32)

    anywhere = pl.BlockSpec(memory_space=pl.ANY)
    return pl.pallas_call(
        functools.partial(vocab_kernel, count, tile, step),
        grid_spec=pltpu.PrefetchScalarGridSpec(
            num_scalar_prefetch=1,
            grid=(total // step,),
            in_specs=[
                pl.BlockSpec((total, width), lambda i, _: (0, 0), pipeline_mode=pl.Buffered(1)),
                anywhere,
            ],
            out_specs=[anywhere, anywhere],
            scratch_shapes=[
                pltpu.VMEM((step, padded), jnp.float32),
                pltpu.VMEM((padded, width), jnp.bfloat16),
                pltpu.VMEM((step, width), jnp.float32),
                pltpu.VMEM((step, 128), jnp.float32),
                pltpu.SemaphoreType.DMA((padded // tile,)),
                pltpu.SemaphoreType.DMA((2, step // LIVE_ROWS)),
            ],
        ),
        out_shape=[
            jax.ShapeDtypeStruct((total, width), jnp.float32),
            jax.ShapeDtypeStruct((total, 128), jnp.float32),
        ],
        compiler_params=pltpu.CompilerParams(vmem_limit_bytes=56 * MEBI),
        cost_estimate=pl.CostEstimate(
            flops=3 * total * width * padded,
            bytes_accessed=2 * padded * width + 6 * total * width,
            transcendentals=total * padded,
        ),
    )(order, rows, table)


def exchange(values, bits):
    got = [swap(value, bit, 0) for value, bit in zip(values, bits)]
    return lax.optimization_barrier(got)


def spread(halves, orders):
    halves = [{0: half} for half in halves]
    for turn in range(len(orders[0])):
        keys = sorted(halves[0])
        got = exchange(
            [jnp.stack([half[k] for k in sorted(half)]) for half in halves],
            [bits[turn] for bits in orders],
        )
        halves = [
            half | {key | bits[turn]: other[place] for place, key in enumerate(sorted(half))}
            for half, other, bits in zip(halves, got, orders)
        ]
    return halves


def halved_sum(halves, orders):
    for turn in range(len(orders[0])):
        sent, kept = [], []
        for half, bits in zip(halves, orders):
            keep = [key for key in sorted(half) if not key & bits[turn]]
            kept.append(keep)
            sent.append(jnp.stack([bfloat(half[key | bits[turn]]) for key in keep]))
        got = exchange(sent, [bits[turn] for bits in orders])
        halves = [
            {key: half[key] + other[place].astype(jnp.float32) for place, key in enumerate(keep)}
            for half, keep, other in zip(halves, kept, got)
        ]
    return [half[0] for half in halves]


def merged_sum(halves, orders):
    for turn in range(len(orders[0])):
        sent, kept = [], []
        for half, bits in zip(halves, orders):
            keep = [key for key in sorted(half) if not key & bits[turn]]
            kept.append(keep)
            away = [half[key | bits[turn]] for key in keep]
            sent.append(jnp.stack([bfloat(mix) for mix, _ in away]))
            sent.append(jnp.stack([stats for _, stats in away]))
        got = exchange(sent, [bits[turn] for bits in orders for _ in range(2)])
        merged = []
        for place, (half, keep) in enumerate(zip(halves, kept)):
            mixes, stats = got[2 * place], got[2 * place + 1]
            blocks = {}
            for index, key in enumerate(keep):
                mix, (top, total) = half[key]
                other_top, other_total = stats[index]
                best = jnp.maximum(top, other_top)
                scale = jnp.exp(top - best)
                other_scale = jnp.exp(other_top - best)
                mix = mix * scale[:, None] + mixes[index].astype(jnp.float32) * other_scale[:, None]
                total = total * scale + other_total * other_scale
                blocks[key] = (mix, jnp.stack([best, total]))
            merged.append(blocks)
        halves = merged
    return [half[0] for half in halves]


def adapter_steps(down_grad, up_grad, kind, tasks, lead):
    seq_count, kv_count = lax.axis_size("seq"), lax.axis_size("kv")
    seq_index, kv_index = lax.axis_index("seq"), lax.axis_index("kv")
    chips = seq_count // 2
    devices = seq_count * kv_count
    core = seq_index % 2
    lanes = down_grad.shape[1]
    down_rows = down_grad.shape[0] // devices
    up_rows = up_grad.shape[0] // (chips * kv_count)
    folds = up_grad.shape[1] // lanes
    down_part = down_grad.reshape(chips, 2, kv_count, down_rows, lanes)
    up_part = up_grad.reshape(chips, kv_count, up_rows, folds, lanes).transpose(0, 1, 3, 2, 4)
    up_part = up_part.reshape(chips, kv_count, folds * up_rows, lanes)
    mine, other, up_part = yield [
        pick(down_part, 1, core),
        swap(bfloat(pick(down_part, 1, 1 - core)), 1, 0),
        up_part,
    ]
    grad = jnp.concatenate([mine, other.astype(jnp.float32), up_part], 2)
    height = grad.shape[2]
    x_bits, y_bits = plane_bits()
    orders = [(x_bits + y_bits, y_bits + x_bits)[task % 2] for task in range(tasks)]
    lefts = [list(reversed(x_bits + y_bits)) for _ in range(tasks)]
    parts = []
    for task in range(tasks):
        part = grad * (kind == task).astype(jnp.float32)
        parts.append(
            part.reshape([2] * (len(x_bits) + len(y_bits)) + [kv_count, height, lanes])
        )
    for turn in range(len(orders[0])):
        kept, got = [], []
        for part, bits, left in zip(parts, orders, lefts):
            bit = bits[turn]
            axis = left.index(bit)
            left.remove(bit)
            place = (seq_index // bit) % 2
            kept.append(pick(part, axis, place))
            got.append(swap(bfloat(pick(part, axis, 1 - place)), bit, 0))
        done = yield kept + got
        parts = [
            part + other.astype(jnp.float32) for part, other in zip(done[:tasks], done[tasks:])
        ]
    part = jnp.stack(parts, 1)
    done = yield [pick(part, 0, kv_index)] + [
        swap(bfloat(pick(part, 0, kv_index ^ step)), 0, step) for step in range(1, kv_count)
    ]
    total = done[0]
    for other in done[1:]:
        total = total + other.astype(jnp.float32)
    sides = in_order(core, total[:, :down_rows], total[:, down_rows : 2 * down_rows])
    sides = [
        side.reshape(tasks, down_rows, seq_count // (2 * lead), lanes * 2 * lead // seq_count)
        for side in sides
    ]
    down_total = jnp.stack(sides, 3).reshape(tasks, down_rows, 2 * lanes)
    up_total = total[:, 2 * down_rows :].reshape(tasks, folds, up_rows, lanes)
    up_total = up_total.transpose(0, 2, 1, 3).reshape(tasks, up_rows, folds * lanes)
    if lead == 2:
        up_total = trade_bits(up_total)
    return (down_total, up_total)


class Steps:
    def __init__(self, steps):
        self.steps = steps
        self.sent = next(steps)
        self.result = None

    def after(self, value):
        if self.result is not None:
            return
        count = len(self.sent)
        try:
            self.sent = self.steps.send(
                list(lax.optimization_barrier(tuple(self.sent) + (value,))[:count])
            )
        except StopIteration as stop:
            self.result = stop.value

    def finish(self):
        while self.result is None:
            try:
                self.sent = self.steps.send(self.sent)
            except StopIteration as stop:
                self.result = stop.value
        return self.result


def total_sum(value):
    step = 1
    while step < lax.axis_size("seq"):
        value = value + swap(value, step, 0)
        step *= 2
    step = 1
    while step < lax.axis_size("kv"):
        value = value + swap(value, 0, step)
        step *= 2
    return value


def item_rows(embeds):
    seq_count, kv_count = lax.axis_size("seq"), lax.axis_size("kv")
    seq_index, kv_index = lax.axis_index("seq"), lax.axis_index("kv")
    got = []
    for turn in range(2):
        pairs = []
        for s in range(seq_count):
            for z in range(kv_count):
                source = (s - s % 2 + z % 2) * kv_count + 2 * (s % 2) + ((z // 2) ^ turn)
                pairs.append((source, s * kv_count + z))
        sent = pick(embeds[:, 0], 0, (kv_index % 2) ^ turn)
        got.append(lax.ppermute(sent, AXES, pairs))
    swapped = kv_index // 2 == 1
    mine = jnp.concatenate(
        [jnp.where(swapped, got[1], got[0]), jnp.where(swapped, got[0], got[1])]
    )
    return jnp.concatenate(in_order(seq_index % 2, mine, swap(mine, 1, 0)))


def adam_update(weight, first, second, grad, rate, decay, count_step):
    first_new = beta_one * first + (1.0 - beta_one) * grad
    second_new = beta_two * second + (1.0 - beta_two) * grad * grad
    first_hat = first_new / (1.0 - jnp.power(beta_one, count_step))
    second_hat = second_new / (1.0 - jnp.power(beta_two, count_step))
    weight_new = weight - rate * (
        first_hat / (jnp.sqrt(second_hat) + adam_epsilon) + decay * weight
    )
    return (weight_new, first_new, second_new)


def per_device(
    src_embed,
    tgt_embed,
    targets,
    src_len,
    tgt_len,
    task,
    step,
    attn_in,
    attn_out,
    ffn_in,
    ffn_out,
    embed,
    down_w,
    down_m,
    down_v,
    up_w,
    up_m,
    up_v,
    norm_params,
    norm_m,
    norm_v,
):
    seq_count, kv_count = lax.axis_size("seq"), lax.axis_size("kv")
    seq_index, kv_index = lax.axis_index("seq"), lax.axis_index("kv")
    chips = seq_count // 2
    devices = seq_count * kv_count
    width = attn_out.shape[2]
    hidden = ffn_in.shape[2]
    bottleneck = down_w.shape[3]
    tasks = down_w.shape[1]
    vocab_rows = embed.shape[0]
    vocab_total = vocab_rows * seq_count
    core = seq_index % 2
    batch = kv_index // 2
    item = seq_index - core + kv_index % 2
    source_length = src_len[batch, item]
    target_length = tgt_len[batch, item]
    kind = task[batch, item]
    count = jnp.sum(tgt_len).astype(jnp.float32)
    gains = norm_params[0]
    biases = norm_params[1]

    x_bits, y_bits = plane_bits()
    orders = (x_bits + y_bits, y_bits + x_bits)
    share = width // devices
    lead = 1 if kv_count * share % HDIM == 0 else 2
    sides = [
        core_columns(part, lead)
        for part in (
            [attn_in[j].reshape(share, 3, width) for j in range(3)]
            + [ffn_in[0], ffn_in[1]]
            + [bfloat(down_w[l, t]) for l in range(2) for t in range(tasks)]
        )
    ]
    flat = [jnp.concatenate([part[c].reshape(share, -1) for part in sides], 1) for c in range(2)]
    mine = jnp.where(core == 0, flat[0], flat[1])
    theirs = swap(jnp.where(core == 0, flat[1], flat[0]), 1, 0)
    split = jnp.stack(in_order(core, mine, theirs))
    edges = [0]
    for part in sides:
        edges.append(edges[-1] + part[0].size // share)
    split = [split[:, :, first:last] for first, last in zip(edges, edges[1:])]
    out_low, second_low, up_low = attn_out, ffn_out, bfloat(up_w)
    if lead == 2:
        out_low, second_low, up_low = trade_bits((out_low, second_low, up_low))
    half_w = width // 2
    own_attn = [
        jnp.concatenate(
            [split[j], out_low[j].reshape(share, 2, half_w).transpose(1, 0, 2)], 2
        )
        for j in range(3)
    ]
    lanes = bottleneck // 2
    up_rows = up_w.shape[2]
    own_down = jnp.stack(split[5:]).reshape(2 * tasks, 2, 2, share // 2, lanes)
    own_up = up_low.reshape(2 * tasks, up_rows, 4, lanes).transpose(0, 2, 1, 3)
    own_adapter = jnp.concatenate([own_down, own_up.reshape(2 * tasks, 2, 2, up_rows, lanes)])
    attn_shapes = [
        (chips, 2, kv_count, share, 3 * half_w),
        (2, chips, kv_count, share, half_w),
    ]
    first_shapes = [(chips, 2, kv_count, share, hidden // 2)]
    second_shapes = [(chips, kv_count, hidden // devices, width)]
    adapter_shapes = [
        (2, chips, 2, kv_count, 2, share // 2, lanes),
        (2, 4, chips, kv_count, up_rows, lanes),
    ]
    groups = [
        (second_low[0][None], "second", second_shapes),
        (own_attn[0], "attention", attn_shapes),
        (own_attn[1], "attention", attn_shapes),
        (split[3], "first", first_shapes),
        (own_adapter, "adapter", adapter_shapes),
        (own_attn[2], "attention", attn_shapes),
        (split[4], "first", first_shapes),
        (second_low[1][None], "second", second_shapes),
    ]
    where = jnp.stack([seq_index // 2, kind]).astype(jnp.int32)
    tile = 1280

    def column_start(place):
        return lambda made: [(place, column_first_steps(groups[place][0]))]

    def with_last(made):
        return [
            (len(groups) - 1, plane_first_steps(groups[-1][0])),
            (0, column_first_steps(groups[0][0])),
        ]

    def ids_in(made):
        parts = [pick(targets, 0, batch)]
        for turn in range(1, kv_count):
            parts.append(swap(pick(targets, 0, batch ^ (turn // 2)), 0, turn))
        order = kv_index ^ jnp.arange(kv_count, dtype=jnp.int32)
        chosen = order[:, None] == jnp.arange(kv_count, dtype=jnp.int32)[None, :]
        parts = jnp.sum(jnp.where(chosen[:, :, None, None], jnp.stack(parts)[:, None], 0), 0)
        return {"ids": parts.transpose(1, 0, 2)}

    def rows_in(made):
        return {
            "source": item_rows(src_embed),
            "target": item_rows(tgt_embed),
        }

    def table_in(made):
        low = after(embed, made["tie"])
        return {"table": jnp.pad(low, ((0, -vocab_rows % tile), (0, 0)))}

    def sum_in(made):
        return {"table_sum": jnp.sum(after(embed, made["tie"]).astype(jnp.float32), 0)}

    own_rows = tgt_embed.shape[2] * kv_count // 2
    half = own_rows // 2
    relative = seq_index ^ jnp.arange(seq_count, dtype=jnp.int32)
    row_items = relative - relative % 2 + kv_index % 2
    row_pos = (
        (relative % 2)[None, :, None] * own_rows
        + jnp.arange(2, dtype=jnp.int32)[:, None, None] * half
        + jnp.arange(half, dtype=jnp.int32)[None, None, :]
    )
    plane_lengths = pick(tgt_len, 0, batch)
    plane_lengths = jnp.sum(
        jnp.where(row_items[:, None] == jnp.arange(seq_count)[None, :], plane_lengths[None], 0), 1
    )
    alive = row_pos < plane_lengths[None, :, None]
    live = alive.astype(jnp.float32) / count

    def linear_in(made):
        ids = made["ids"].reshape(seq_count, 2, 2, half)
        chosen = (row_items[:, None] == jnp.arange(seq_count)[None, :])[:, :, None] & (
            (relative % 2)[:, None, None] == jnp.arange(2)[None, None, :]
        )
        row_ids = jnp.sum(jnp.where(chosen[:, :, :, None, None], ids[None], 0), (1, 2))
        row_ids = row_ids.transpose(1, 0, 2).reshape(-1)
        local_ids = after(row_ids - seq_index * vocab_rows, made["tie"])
        local_hit = (local_ids >= 0) & (local_ids < vocab_rows)
        target_rows = jnp.take(embed, jnp.clip(local_ids, 0, vocab_rows - 1), axis=0)
        linear = bfloat(
            jnp.where(local_hit[:, None], 0.9 * target_rows.astype(jnp.float32), 0.0)
            + (0.1 / vocab_total) * made["table_sum"][None]
        )
        return {"linear": linear.reshape(2, seq_count, half, width)}

    def last_in(made):
        return {"last": step + 0}

    starts = [with_last] + [column_start(place) for place in range(1, len(groups) - 1)]
    def place(made, group):
        _, form, shape = groups[group]
        return place_blocks(made[group], where, form, shape)

    def attention_weights(made, group):
        w_in, w_out = place(made, group)
        w_out = jnp.concatenate(list(w_out.reshape(2, half_w, half_w)), 1)
        return (w_in.reshape(width, 3 * half_w), w_out)

    def encoder_attention(made):
        w_in, w_out = attention_weights(made, 1)
        x0, cache = norm_forward(made["source"].astype(jnp.float32), gains[0], biases[0])
        pair = bfloat(times_plain(bfloat(x0), w_in))
        out = attend(source_length, False, (pair, 0), (pair, half_w))
        return {
            "enc": (x0, cache, pair, times_plain(out, w_out)),
            "enc_w": (w_in, w_out),
        }

    def decoder_attention(made):
        x0, cache0, pair, part = made["enc"]
        x1, cache1 = norm_forward(x0 + core_sum(part), gains[1], biases[1])
        w_in, w_out = attention_weights(made, 2)
        y0, cache3 = norm_forward(made["target"].astype(jnp.float32), gains[3], biases[3])
        self_pair = bfloat(times_plain(bfloat(y0), w_in))
        out = attend(target_length, True, (self_pair, 0), (self_pair, half_w))
        return {
            "x1": (x1, cache1),
            "dec": (y0, cache3, self_pair, times_plain(out, w_out)),
            "dec_w": (w_in, w_out),
        }

    def encoder_hidden(made):
        y0, cache3, self_pair, part = made["dec"]
        y1, cache4 = norm_forward(y0 + core_sum(part), gains[4], biases[4])
        first = place(made, 3)[0].reshape(width, hidden // 2)
        low_in = bfloat(made["x1"][0])
        return {
            "y1": (y1, cache4),
            "first0": first,
            "hidden0": (low_in,) + gelu_pair(times_plain(low_in, first)),
        }

    def encoder_branch(made):
        down_all, up_all = place(made, 4)
        down_all = down_all.reshape(2, width, lanes)
        up_all = up_all.reshape(2, 4, lanes, lanes)
        up_all = jnp.concatenate([up_all[:, fold] for fold in range(4)], 2)
        second = place(made, 0)[0].reshape(hidden // 2, width)
        low_in, hidden_low, slope = made["hidden0"]
        inner_low, inner_slope = gelu_pair(times_plain(low_in, down_all[0]))
        part = times_plain(hidden_low, second) + 4.0 * times_plain(inner_low, up_all[0])
        return {
            "adapters": (down_all, up_all),
            "second0": second,
            "feed0": (part, (low_in, slope, inner_slope, inner_low)),
        }

    def cross_attention(made):
        x2, cache2 = norm_forward(made["x1"][0] + core_sum(made["feed0"][0]), gains[2], biases[2])
        w_in, w_out = attention_weights(made, 5)
        cross_query = bfloat(times_plain(bfloat(made["y1"][0]), w_in[:, :half_w]))
        cross_pair = bfloat(times_plain(bfloat(x2), w_in[:, half_w:]))
        out = attend(source_length, False, (cross_query, 0), (cross_pair, 0))
        return {
            "cross": (cache2, cross_query, cross_pair, times_plain(out, w_out)),
            "cross_w": (w_in, w_out),
        }

    extras = {
        0: rows_in,
        1: ids_in,
        2: table_in,
        3: sum_in,
        4: encoder_attention,
        5: decoder_attention,
        6: lambda made: encoder_hidden(made) | last_in(made),
        7: encoder_branch,
        8: cross_attention,
    }
    late = len(x_bits + y_bits) - 2
    extras = {turn + (late if turn > 3 else 0): value for turn, value in extras.items()}
    if late:
        extras[4] = linear_in
    else:
        attention_first = extras[4]
        extras[4] = lambda made: attention_first(made) | linear_in(made)
    gathered, made = run_rounds(starts, extras)
    table, linear = made["table"], made["linear"]
    x0, cache0, enc_pair, _ = made["enc"]
    x1, cache1 = made["x1"]
    y0, cache3, self_pair, _ = made["dec"]
    y1, cache4 = made["y1"]
    cache2, cross_query, cross_pair, part = made["cross"]
    down_all, up_all = made["adapters"]
    enc_feed = made["feed0"][1]
    attn_w = [made["enc_w"], made["dec_w"], made["cross_w"]]
    y2, cache5 = norm_forward(y1 + core_sum(part), gains[5], biases[5])
    first_w = [made["first0"], place(gathered, 6)[0].reshape(width, hidden // 2)]
    labels, stack = gathered[len(groups) - 1]
    stack = lax.all_gather(after(stack, made["last"]), "kv", axis=1)
    second_w = place({7: [(labels, 0, stack)]}, 7)[0].reshape(hidden // 2, width)
    second_w = [made["second0"], second_w]
    branch, dec_feed = feed_forward(bfloat(y2), first_w[1], second_w[1], down_all[1], up_all[1])
    y3, cache6 = norm_forward(y2 + core_sum(branch), gains[6], biases[6])

    down_orders = [[1] + list(bits) for bits in orders]
    linear_sum = halved_sum(
        [
            {key: after(linear[h, key], made["tie"]) for key in range(seq_count)}
            for h in range(2)
        ],
        down_orders,
    )
    y3_low = bfloat(y3)
    near = [
        lax.dynamic_slice_in_dim(y3_low, place * own_rows + h * half, half)
        for h in range(2)
        for place in (core, 1 - core)
    ]
    far = spread([near[0], near[2]], [list(bits) + [1] for bits in orders])
    near = jnp.concatenate(near)
    far = jnp.concatenate([half_far[key] for half_far in far for key in range(2, seq_count)])
    blocks = [{}, {}]
    loss_part = 0.0
    for rows, first, last in ((near, 0, 2), (far, 2, seq_count)):
        flags = jnp.any(alive[:, first:last].reshape(-1, LIVE_ROWS), 1)
        mixed, stats = vocab_pass(rows, flags, table, vocab_rows, 256, tile)
        mixed = mixed.reshape(2, last - first, half, width)
        tops = stats[:, 0].reshape(2, last - first, half)
        totals = stats[:, 64].reshape(2, last - first, half)
        for h in range(2):
            for key in range(first, last):
                pair = jnp.stack([tops[h, key - first], totals[h, key - first]])
                blocks[h][key] = (mixed[h, key - first], pair)
        rows_alive = alive[:, first:last].astype(jnp.float32)[..., None]
        rows = rows.astype(jnp.float32).reshape(mixed.shape)
        loss_part = loss_part - jnp.sum(rows_alive * rows * linear[:, first:last].astype(jnp.float32))
    merged = merged_sum(blocks, down_orders)
    final_grad = []
    for h, (mix, (top, total)) in enumerate(merged):
        row_grad = (mix / total[:, None] - linear_sum[h]) * live[h, 0][:, None]
        final_grad.append(jnp.where(alive[h, 0][:, None], row_grad, 0.0))
        loss_part = loss_part + jnp.sum(jnp.where(alive[h, 0], top + jnp.log(total), 0.0))
    final_grad = bfloat(jnp.concatenate(final_grad))
    final_grad = jnp.concatenate(in_order(core, final_grad, swap(final_grad, 1, 0)))
    final_grad = final_grad.astype(jnp.float32)

    grad, grad6 = norm_backward(final_grad, cache6, gains[6])
    inner_grad, down_grad, up_grad = feed_backward(
        grad, dec_feed, first_w[1], second_w[1], down_all[1], up_all[1]
    )
    dec_steps = Steps(adapter_steps(down_grad, up_grad, kind, tasks, lead))
    grad, grad5 = norm_backward(grad + core_sum(inner_grad), cache5, gains[5])
    out_grad = bfloat(times_second(bfloat(grad), attn_w[2][1]))
    dec_steps.after(out_grad)
    dq, dk, dv = attend_back(source_length, False, (cross_query, 0), (cross_pair, 0), out_grad)
    enc_grad = times_second(jnp.concatenate([dk, dv], 1), attn_w[2][0][:, half_w:])
    query_grad = times_second(dq, attn_w[2][0][:, :half_w])
    dec_steps.after(dq)
    summed = core_sum(jnp.concatenate([enc_grad, query_grad]))
    enc_rows = x0.shape[0]
    dec_grad, grad4 = norm_backward(grad + summed[enc_rows:], cache4, gains[4])
    grad, grad2 = norm_backward(summed[:enc_rows], cache2, gains[2])
    inner_grad, down_grad, up_grad = feed_backward(
        grad, enc_feed, first_w[0], second_w[0], down_all[0], up_all[0]
    )
    dec_steps.after(inner_grad)
    enc_steps = Steps(adapter_steps(down_grad, up_grad, kind, tasks, lead))
    out_grad = bfloat(times_second(bfloat(dec_grad), attn_w[1][1]))
    parts = attend_back(target_length, True, (self_pair, 0), (self_pair, half_w), out_grad)
    enc_steps.after(out_grad)
    dec_steps.after(parts[0])
    self_grad = times_second(jnp.concatenate(parts, 1), attn_w[1][0])
    enc_steps.after(parts[0])
    _, grad3 = norm_backward(dec_grad + core_sum(self_grad), cache3, gains[3])
    grad, grad1 = norm_backward(grad + core_sum(inner_grad), cache1, gains[1])
    out_grad = bfloat(times_second(bfloat(grad), attn_w[0][1]))
    parts = attend_back(source_length, False, (enc_pair, 0), (enc_pair, half_w), out_grad)
    enc_steps.after(parts[0])
    enc_grad = times_second(jnp.concatenate(parts, 1), attn_w[0][0])
    _, grad0 = norm_backward(grad + core_sum(enc_grad), cache0, gains[0])
    enc_sums, dec_sums = enc_steps.finish(), dec_steps.finish()

    norm_grad = 0.5 * jnp.stack([grad0, grad1, grad2, grad3, grad4, grad5, grad6], 1)
    down_part = jnp.stack([enc_sums[0], dec_sums[0]])
    up_part = jnp.stack([enc_sums[1], dec_sums[1]])
    square = jnp.sum(down_part * down_part) + jnp.sum(up_part * up_part)
    scalars = jnp.zeros((1, width), jnp.float32).at[0, 0].set(loss_part).at[0, 1].set(square)
    summed = total_sum(jnp.concatenate([norm_grad.reshape(-1, width), scalars]))
    norm_sum = summed[:-1].reshape(norm_grad.shape)
    loss_sum = summed[-1, 0]
    grad_norm = jnp.sqrt(summed[-1, 1] + jnp.sum(norm_sum * norm_sum))
    factor = clip_limit / jnp.maximum(grad_norm, clip_limit)
    count_step = step[0].astype(jnp.float32)
    down_new = adam_update(
        down_w, down_m, down_v, factor * down_part, rate_adapter, weight_decay, count_step
    )
    up_new = adam_update(up_w, up_m, up_v, factor * up_part, rate_adapter, weight_decay, count_step)
    norm_grad_out = factor * norm_sum
    norm_new = adam_update(norm_params, norm_m, norm_v, norm_grad_out, rate_norm, 0.0, count_step)
    return (
        loss_sum,
        count,
        grad_norm,
        down_new[0],
        down_new[1],
        down_new[2],
        up_new[0],
        up_new[1],
        up_new[2],
        norm_new[0],
        norm_new[1],
        norm_new[2],
        norm_grad_out,
    )


def solution(mesh):
    placed = (
        P(None, "seq", "kv", None),
        P(None, "seq", "kv", None),
        P(None, None, "kv"),
        P(),
        P(),
        P(),
        P(),
        P(None, ("seq", "kv"), None),
        P(None, ("seq", "kv"), None),
        P(None, ("seq", "kv"), None),
        P(None, ("seq", "kv"), None),
        P("seq", None),
        P(None, None, ("seq", "kv"), None),
        P(None, None, ("seq", "kv"), None),
        P(None, None, ("seq", "kv"), None),
        P(None, None, ("seq", "kv"), None),
        P(None, None, ("seq", "kv"), None),
        P(None, None, ("seq", "kv"), None),
        P(),
        P(),
        P(),
    )
    return jax.shard_map(
        per_device,
        mesh=mesh,
        in_specs=placed,
        out_specs=(
            P(),
            P(),
            P(),
            P(None, None, ("seq", "kv"), None),
            P(None, None, ("seq", "kv"), None),
            P(None, None, ("seq", "kv"), None),
            P(None, None, ("seq", "kv"), None),
            P(None, None, ("seq", "kv"), None),
            P(None, None, ("seq", "kv"), None),
            P(),
            P(),
            P(),
            P(),
        ),
        check_vma=False,
    )
```

time: 1790 us -> 803 us (0.45)
  waiting for transfers between devices: 1160 us -> 151 us
  matrix products: 361 us -> 61.7 us
  Pallas kernels: 0 us -> 162 us
  starting transfers between devices: 2.3 us -> 106 us
  local copies, waits for them, and re-layouts: 65.7 us -> 158 us
  blocking collectives: 74.3 us -> 0 us
  other arithmetic: 82.5 us -> 123 us
    all_gather x14 -> x8, waiting for transfers between devices: 697 us -> 4.01 us  [the longest x7 4.01 us: column_first_steps(): column, = (yield [lax.all_gather(own, 'kv')])]
    reduce_scatter x4 -> x0, waiting for transfers between devices: 426 us -> none  [the longest x1 184 us: reduce_grads(): lax.psum_scatter(up_grad, ('seq', 'kv'), scatter_dimension=2, tiled=True)]
    pallas_call x0 -> x16, Pallas kernels: none -> 162 us  [the longest x2 66.1 us: vocab_pass(): pl.pallas_call(functools.partial(vocab_kernel, count, tile, step), grid_s...]
    ppermute x0 -> x98, waiting for transfers between devices: none -> 147 us  [the longest x94 141 us: swap(): return lax.ppermute(value, AXES, pairs)]
    dot_general x32 -> x13, matrix products: 161 us -> 33.4 us  [times_second(): lax.dot_general(left, right, (((1,), (1,)), ((), ())), preferred_element_...]
    dot_general x36 -> x15, matrix products: 149 us -> 24.4 us  [times_plain(): return jnp.dot(left, right, preferred_element_type=jnp.float32)]
    ppermute x0 -> x98, starting transfers between devices: none -> 105 us  [the longest x94 97.7 us: swap(): return lax.ppermute(value, AXES, pairs)]
    psum x2 -> x0, blocking collectives: 60.9 us -> none  [the longest x1 38.4 us: reduce_grads(): norm_sum, loss_sum = lax.psum((norm_grad, loss_part), ('seq', 'kv'))]
  transfers between devices with their start and end apart: 24 -> 106, of which waited for: 20 -> 33; matrix products, arithmetic and copies ran while one was open for 17% -> 32% of each run, Pallas kernels for 0% -> 15%
where the time goes in v2:
time: 803 us; the launch traced here: 791 us
  Pallas kernels  162 us (20%)
  local copies, waits for them, and re-layouts  158 us (20%)
  waiting for transfers between devices  151 us (19%)
  other arithmetic  123 us (15%)
  starting transfers between devices  106 us (13%)
  matrix products  61.7 us (8%)
  between operations  29.9 us (4%)
    ppermute x94, waiting for transfers between devices, swap(): return lax.ppermute(value, AXES, pairs)  141 us
    ppermute x94, starting transfers between devices, swap(): return lax.ppermute(value, AXES, pairs)  97.7 us
    pallas_call x2, Pallas kernels, vocab_pass(): pl.pallas_call(functools.partial(vocab_kernel, count, tile, step), grid_s...  66.1 us
    pallas_call x8, Pallas kernels, place_blocks(): pl.pallas_call(functools.partial(place_kernel, plan, form), grid_spec=plt...  57.3 us
    unnamed x477, local copies, waits for them, and re-layouts  44.6 us
    pallas_call x6, Pallas kernels, attention_call(): pl.pallas_call(functools.partial(kernel, causal), grid_spec=pltpu.Prefetc...  38.9 us
    dot_general x13, matrix products, times_second(): lax.dot_general(left, right, (((1,), (1,)), ((), ())), preferred_element_...  33.4 us
    dot_general x15, matrix products, times_plain(): return jnp.dot(left, right, preferred_element_type=jnp.float32)  24.4 us
  transfers between devices with their start and end apart: 106, of which 33 were waited for; matrix products, arithmetic and copies ran while one was open for 32% of the time, Pallas kernels for 15%

profile of v2, /device:TPU:0, one launch (start us, length us, event | category | flops | bytes accessed | tf_op | source)
XLA Modules:
  0.0 790.8 jit_solution(17926203111580081284)
XLA Ops:
  59.6 7.0 collective-permute-start.4
  86.0 9.1 %collective-permute-done.10 = bf16[1,2,1,128,1024]{4,3,1,2,0:T(8,128)(2,1)S(1)} collective-permute-done((bf16[1,2,1,128,1024]{4,3,1,2,0:T(8,128)(2,1)S(1)}, bf16[1,2,1,128,1024]{4,3,1,2,0:T(8,128)(2,1)S(1)}, u32[]{:S(2)}, u32[]{:S(2)}) %collective-permute-start.10) | collective-permute-done | bytes 524320 | tf_op jit(solution)/shard_map/ppermute | solution.py:83
  104.5 13.1 %pad.14.table_ref = bf16[6400,1024]{1,0:T(8,128)(2,1)} pad(bf16[6284,1024]{1,0:T(8,128)(2,1)} %param.36, bf16[]{:T(256)} %constant.407.clone.1), padding=0_116x0_0 | pad | bytes 25976834 | tf_op jit(solution)/shard_map/jit(_pad)/pad | solution.py:832
  121.6 11.5 %collective-permute-done.18 = bf16[1,2,2,32,2048]{4,3,2,1,0:T(8,128)(2,1)} collective-permute-done((bf16[1,2,2,32,2048]{4,3,2,1,0:T(8,128)(2,1)}, bf16[1,2,2,32,2048]{4,3,2,1,0:T(8,128)(2,1)}, u32[]{:S(2)}, u32[]{:S(2)}) %collective-permute-start.18) | collective-permute-done | bytes 524320 | tf_op jit(solution)/shard_map/ppermute | solution.py:83
  147.7 6.5 convert_reduce_fusion
  154.2 18.3 %collective-permute-done.22 = bf16[1,2,2,32,2048]{4,3,2,1,0:T(8,128)(2,1)} collective-permute-done((bf16[1,2,2,32,2048]{4,3,2,1,0:T(8,128)(2,1)}, bf16[1,2,2,32,2048]{4,3,2,1,0:T(8,128)(2,1)}, u32[]{:S(2)}, u32[]{:S(2)}) %collective-permute-start.22) | collective-permute-done | bytes 524320 | tf_op jit(solution)/shard_map/ppermute | solution.py:83
  182.7 8.1 %shard_map.300 = (bf16[4,2,4,32,1536]{4,3,2,1,0:T(8,128)(2,1)S(1)}, bf16[2,4,4,32,512]{4,3,2,1,0:T(8,128)(2,1)S(1)}) custom-call(s32[2]{0:T(128)S(1)} %pad_add_fusion.1.where_ref, bf16[2,2,2,32,2048]{4,3,2,1,0:T(8,128)(2,1)} %constant_dynamic-update-slice_fusion.26.refs_0_, bf16[2,2,2,32,2048]{4,3,2,1,0:T(8,128)(2,1)} %collective-permute-done.20.refs_1_, ...), custom_call_target="tpu_custom_call" | custom-call | flops 1 | bytes 1 | tf_op jit(solution)/shard_map/pallas_call | solution.py:259
  192.6 17.4 %gather_fusion = bf16[2048,1024]{1,0:T(8,128)(2,1)} fusion(bf16[6284,1024]{1,0:T(8,128)(2,1)} %param.36, s32[2048]{0:T(1024)S(1)} %fusion.207), kind=kCustom, calls=%fused_computation | custom fusion | bytes 8396800 | tf_op jit(solution)/shard_map/jit(_take)/gather | solution.py:862
  233.1 8.1 %shard_map.302 = (bf16[4,2,4,32,1536]{4,3,2,1,0:T(8,128)(2,1)S(1)}, bf16[2,4,4,32,512]{4,3,2,1,0:T(8,128)(2,1)S(1)}) custom-call(s32[2]{0:T(128)S(1)} %pad_add_fusion.1.where_ref, bf16[2,2,2,32,2048]{4,3,2,1,0:T(8,128)(2,1)} %constant_dynamic-update-slice_fusion.30.refs_0_, bf16[2,2,2,32,2048]{4,3,2,1,0:T(8,128)(2,1)} %collective-permute-done.24.refs_1_, ...), custom_call_target="tpu_custom_call" | custom-call | flops 1 | bytes 1 | tf_op jit(solution)/shard_map/pallas_call | solution.py:259
  243.3 7.1 shard_map.303
  270.2 8.0 %shard_map.304 = bf16[4,2,4,32,2048]{4,3,2,1,0:T(8,128)(2,1)S(1)} custom-call(s32[2]{0:T(128)S(1)} %pad_add_fusion.1.where_ref, bf16[2,2,2,32,2048]{4,3,2,1,0:T(8,128)(2,1)} %constant_dynamic-update-slice_fusion.39.refs_0_, bf16[2,2,2,32,2048]{4,3,2,1,0:T(8,128)(2,1)} %collective-permute-done.28.refs_1_, ...), custom_call_target="tpu_custom_call" | custom-call | flops 1 | bytes 1 | tf_op jit(solution)/shard_map/pallas_call | solution.py:259
  285.2 18.0 %collective-permute-done.35 = bf16[1,2,2,32,2048]{4,3,2,1,0:T(8,128)(2,1)} collective-permute-done((bf16[1,2,2,32,2048]{4,3,2,1,0:T(8,128)(2,1)}, bf16[1,2,2,32,2048]{4,3,2,1,0:T(8,128)(2,1)}, u32[]{:S(2)}, u32[]{:S(2)}) %collective-permute-start.35) | collective-permute-done | bytes 524320 | tf_op jit(solution)/shard_map/ppermute | solution.py:83
  310.9 8.4 %shard_map.305 = (bf16[2,4,2,4,2,16,256]{6,5,4,3,2,1,0:T(8,128)(2,1)S(1)}, bf16[2,4,4,4,16,256]{5,4,3,2,1,0:T(8,128)(2,1)S(1)}) custom-call(s32[2]{0:T(128)S(1)} %pad_add_fusion.1.where_ref, bf16[2,2,8,2,2,16,256]{6,5,4,3,2,1,0:T(8,128)(2,1)} %constant_dynamic-update-slice_fusion.43.refs_0_, ...), custom_call_target="tpu_custom_call" | custom-call | flops 1 | bytes 1 | tf_op jit(solution)/shard_map/pallas_call | solution.py:259
  324.6 18.9 %collective-permute-done.40 = bf16[1,2,2,32,2048]{4,3,2,1,0:T(8,128)(2,1)S(1)} collective-permute-done((bf16[1,2,2,32,2048]{4,3,2,1,0:T(8,128)(2,1)S(1)}, bf16[1,2,2,32,2048]{4,3,2,1,0:T(8,128)(2,1)S(1)}, u32[]{:S(2)}, u32[]{:S(2)}) %collective-permute-start.40) | collective-permute-done | bytes 524320 | tf_op jit(solution)/shard_map/ppermute | solution.py:83
  345.9 8.7 %shard_map.307 = (bf16[4,2,4,32,1536]{4,3,2,1,0:T(8,128)(2,1)S(1)}, bf16[2,4,4,32,512]{4,3,2,1,0:T(8,128)(2,1)S(1)}) custom-call(s32[2]{0:T(128)S(1)} %pad_add_fusion.1.where_ref, bf16[2,2,2,32,2048]{4,3,2,1,0:T(8,128)(2,1)S(1)} %constant_dynamic-update-slice_fusion.47.refs_0_, bf16[2,2,2,32,2048]{4,3,2,1,0:T(8,128)(2,1)S(1)} %collective-permute-done.38.refs_1_, ...), custom_call_target="tpu_custom_call" | custom-call | flops 1 | bytes 1 | tf_op jit(solution)/shard_map/pallas_call | solution.py:259
  381.6 12.0 %shard_map.309 = bf16[4,2,4,32,2048]{4,3,2,1,0:T(8,128)(2,1)S(1)} custom-call(s32[2]{0:T(128)S(1)} %pad_add_fusion.1.where_ref, bf16[2,2,2,32,2048]{4,3,2,1,0:T(8,128)(2,1)S(1)} %constant_dynamic-update-slice_fusion.51.refs_0_, bf16[2,2,2,32,2048]{4,3,2,1,0:T(8,128)(2,1)S(1)} %copy-done.17, bf16[2,2,2,32,2048]{4,3,2,1,0:T(8,128)(2,1)S(1)} %copy-done.11, ...), custom_call_target="tpu_custom_call" | custom-call | flops 1 | bytes 1 | tf_op jit(solution)/shard_map/pallas_call | solution.py:259
  432.4 24.4 %shard_map.311 = (f32[512,1024]{1,0:T(8,128)}, f32[512,128]{1,0:T(8,128)}) custom-call(s32[9]{0:T(128)} %pad_add_fusion.2.order_ref, bf16[512,1024]{1,0:T(8,128)(2,1)} %pad_maximum_fusion.8.rows_ref, bf16[6400,1024]{1,0:T(8,128)(2,1)} %pad.14.table_ref), custom_call_target="tpu_custom_call" | custom-call | flops 10066329600 | bytes 16252928 | tf_op jit(solution)/shard_map/pallas_call | solution.py:480
  465.3 41.6 %shard_map.312 = (f32[1536,1024]{1,0:T(8,128)}, f32[1536,128]{1,0:T(8,128)}) custom-call(s32[25]{0:T(128)} %pad_add_fusion.3.order_ref, bf16[1536,1024]{1,0:T(8,128)(2,1)} %copy-done.70, bf16[6400,1024]{1,0:T(8,128)(2,1)} %pad.14.table_ref), custom_call_target="tpu_custom_call" | custom-call | flops 30198988800 | bytes 22544384 | tf_op jit(solution)/shard_map/pallas_call | solution.py:480
  526.7 8.9 %collective-permute-start.57 = (bf16[2,128,1024]{2,1,0:T(8,128)(2,1)S(1)}, bf16[2,128,1024]{2,1,0:T(8,128)(2,1)S(1)}, u32[]{:S(2)}, u32[]{:S(2)}) collective-permute-start(bf16[2,128,1024]{2,1,0:T(8,128)(2,1)S(1)} %pad_maximum_fusion.20), channel_id=1, source_target_pairs={{0,8},{1,9},{2,10},{3,11},{4,12},{5,13},{6,14},{7,15},{8,0},{9,1},... | collective-permute-start | bytes 1572872 | tf_op jit(solution)/shard_map/ppermute | solution.py:83
  538.1 9.9 %collective-permute-done.58 = f32[2,2,128]{2,1,0:T(2,128)S(1)} collective-permute-done((f32[2,2,128]{2,1,0:T(2,128)S(1)}, f32[2,2,128]{2,1,0:T(2,128)S(1)}, u32[]{:S(2)}, u32[]{:S(2)}) %collective-permute-start.58) | collective-permute-done | bytes 2080 | tf_op jit(solution)/shard_map/ppermute | solution.py:83
  574.4 11.2 %fusion.55 = f32[512,1024]{1,0:T(8,128)} fusion(bf16[1024,2048]{1,0:T(8,128)(2,1)} %bitcast.1134, f32[512,2048]{1,0:T(8,128)} %get-tuple-element.404, bf16[2048,1024]{1,0:T(8,128)(2,1)} %bitcast.1132, f32[512,1024]{1,0:T(8,128)} %fusion.15), kind=kOutput, calls=%fused_computation.194 | convolution fusion | flops 4297588736 | bytes 16777216 | tf_op jit(solution)/shard_map/dot_general | solution.py:39
  610.5 7.0 shard_map.313
  657.2 7.8 fusion.316
  677.7 11.1 %shard_map.315 = (bf16[512,512]{1,0:T(8,128)(2,1)S(1)}, bf16[512,512]{1,0:T(8,128)(2,1)S(1)}, bf16[512,512]{1,0:T(8,128)(2,1)S(1)}) custom-call(s32[1]{0:T(128)} %bitcast.59.length_ref, bf16[512,1536]{1,0:T(8,128)(2,1)S(1)} %copy-done.1, bf16[512,1536]{1,0:T(8,128)(2,1)S(1)} %copy-done.1, bf16[512,1536]{1,0:T(8,128)(2,1)S(1)} %copy-done.1, ...), custom_call_target="tpu_custom_call" | custom-call | flops 1 | bytes 1 | tf_op jit(solution)/shard_map/pallas_call | solution.py:332
  (1114 shorter events, 459.0 us)
Async XLA Ops:
  7.2 65.1 %all-gather.17.cloned.1.call-start = ((), (), s32[]{:S(2)}) async-start(), calls=%async_computation | async-start | bytes 1310720 | tf_op jit(solution)/shard_map/all_gather | solution.py:147
  19.7 76.1 %all-gather.19.cloned.1.call-start = ((), (), s32[]{:S(2)}) async-start(), calls=%async_computation.1 | async-start | bytes 1310720 | tf_op jit(solution)/shard_map/all_gather | solution.py:147
  21.8 99.8 %all-gather.21.cloned.1.call-start = ((), (), s32[]{:S(2)}) async-start(), calls=%async_computation.2 | async-start | bytes 1310720 | tf_op jit(solution)/shard_map/all_gather | solution.py:147
  21.9 44.8 %collective-permute-start.15 = (s32[8,128]{1,0:T(8,128)S(1)}, s32[8,128]{1,0:T(8,128)S(1)}, u32[]{:S(2)}, u32[]{:S(2)}) collective-permute-start(s32[8,128]{1,0:T(8,128)S(1)} %get-tuple-element.805), channel_id=1, source_target_pairs={{0,3},{1,2},{2,1},{3,0},{4,7},{5,6},{6,5},{7,4},{8,11},{9,10},{10,... | collective-permute-start | bytes 12296 | tf_op jit(solution)/shard_map/ppermute | solution.py:83
  26.8 41.5 %collective-permute-start.14 = (s32[8,128]{1,0:T(8,128)S(1)}, s32[8,128]{1,0:T(8,128)S(1)}, u32[]{:S(2)}, u32[]{:S(2)}) collective-permute-start(s32[8,128]{1,0:T(8,128)S(1)} %get-tuple-element.805), channel_id=1, source_target_pairs={{0,2},{1,3},{2,0},{3,1},{4,6},{5,7},{6,4},{7,5},{8,10},{9,11},{10,... | collective-permute-start | bytes 12296 | tf_op jit(solution)/shard_map/ppermute | solution.py:83
  27.5 43.1 %collective-permute-start = (bf16[1,1,1,64,1024]{4,3,2,1,0:T(8,128)(2,1)}, bf16[1,1,1,64,1024]{4,3,2,1,0:T(8,128)(2,1)}, u32[]{:S(2)}, u32[]{:S(2)}) collective-permute-start(bf16[1,1,1,64,1024]{4,3,2,1,0:T(8,128)(2,1)} %get-tuple-element.249), channel_id=1, source_target_pairs={{0,8},{1,9},{2,10},{3,11},{4,12},{5,13},{6,14},{7,15},{8,0},{9,1},... | collective-permute-start | bytes 393224 | tf_op jit(solution)/shard_map/ppermute | solution.py:83
  34.1 120.1 %all-gather.23.cloned.1.call-start = ((), (), s32[]{:S(2)}) async-start(), calls=%async_computation.3 | async-start | bytes 1310720 | tf_op jit(solution)/shard_map/all_gather | solution.py:147
  37.3 184.5 %all-gather.25.cloned.1.call-start = ((), (), s32[]{:S(2)}) async-start(), calls=%async_computation.4 | async-start | bytes 1310720 | tf_op jit(solution)/shard_map/all_gather | solution.py:147
  41.0 214.9 %all-gather.27.cloned.1.call-start = ((), (), s32[]{:S(2)}) async-start(), calls=%async_computation.5 | async-start | bytes 1310720 | tf_op jit(solution)/shard_map/all_gather | solution.py:147
  43.7 241.5 %all-gather.29.cloned.1.call-start = ((), (), s32[]{:S(2)}) async-start(), calls=%async_computation.6 | async-start | bytes 1310720 | tf_op jit(solution)/shard_map/all_gather | solution.py:147
  69.2 305.0 %all-gather.31.cloned.1.call-start = ((), (), s32[]{:S(2)}) async-start(), calls=%async_computation.7 | async-start | bytes 5242880 | tf_op jit(solution)/shard_map/all_gather | solution.py:973
  97.0 36.0 %collective-permute-start.16 = (bf16[2,2,1,128,1024]{4,3,1,2,0:T(8,128)(2,1)S(1)}, bf16[2,2,1,128,1024]{4,3,1,2,0:T(8,128)(2,1)}, u32[]{:S(2)}, u32[]{:S(2)}) collective-permute-start(bf16[2,2,1,128,1024]{4,3,1,2,0:T(8,128)(2,1)S(1)} %constant_dynamic-update-slice_fusion.22), channel_id=1, source_target_pairs={{0,16},{1,17},{2,18},{3,19},{4,20},{5,21},{6,22},{7,23},{8,24},{9,... | collective-permute-start | bytes 3145736 | tf_op jit(solution)/shard_map/ppermute | solution.py:83
  137.1 35.4 %collective-permute-start.20 = (bf16[2,2,2,32,2048]{4,3,2,1,0:T(8,128)(2,1)}, bf16[2,2,2,32,2048]{4,3,2,1,0:T(8,128)(2,1)}, u32[]{:S(2)}, u32[]{:S(2)}) collective-permute-start(bf16[2,2,2,32,2048]{4,3,2,1,0:T(8,128)(2,1)} %constant_dynamic-update-slice_fusion.26.refs_0_), channel_id=1, source_target_pairs={{0,16},{1,17},{2,18},{3,19},{4,20},{5,21},{6,22},{7,23},{8,24},{9,... | collective-permute-start | bytes 3145736 | tf_op jit(solution)/shard_map/ppermute | solution.py:83
  176.5 45.3 %collective-permute-start.24 = (bf16[2,2,2,32,2048]{4,3,2,1,0:T(8,128)(2,1)}, bf16[2,2,2,32,2048]{4,3,2,1,0:T(8,128)(2,1)}, u32[]{:S(2)}, u32[]{:S(2)}) collective-permute-start(bf16[2,2,2,32,2048]{4,3,2,1,0:T(8,128)(2,1)} %constant_dynamic-update-slice_fusion.30.refs_0_), channel_id=1, source_target_pairs={{0,16},{1,17},{2,18},{3,19},{4,20},{5,21},{6,22},{7,23},{8,24},{9,... | collective-permute-start | bytes 3145736 | tf_op jit(solution)/shard_map/ppermute | solution.py:83
  178.4 43.4 %collective-permute-start.25 = (bf16[2,2,2,32,2048]{4,3,2,1,0:T(8,128)(2,1)S(1)}, bf16[2,2,2,32,2048]{4,3,2,1,0:T(8,128)(2,1)}, u32[]{:S(2)}, u32[]{:S(2)}) collective-permute-start(bf16[2,2,2,32,2048]{4,3,2,1,0:T(8,128)(2,1)S(1)} %constant_dynamic-update-slice_fusion.32.refs_2_), channel_id=1, source_target_pairs={{0,8},{1,9},{2,10},{3,11},{4,12},{5,13},{6,14},{7,15},{8,0},{9,1},... | collective-permute-start | bytes 3145736 | tf_op jit(solution)/shard_map/ppermute | solution.py:83
  180.4 41.4 %collective-permute-start.26 = (bf16[1,2,2,32,2048]{4,3,2,1,0:T(8,128)(2,1)}, bf16[1,2,2,32,2048]{4,3,2,1,0:T(8,128)(2,1)}, u32[]{:S(2)}, u32[]{:S(2)}) collective-permute-start(bf16[1,2,2,32,2048]{4,3,2,1,0:T(8,128)(2,1)} %get-tuple-element.283), channel_id=1, source_target_pairs={{0,8},{1,9},{2,10},{3,11},{4,12},{5,13},{6,14},{7,15},{8,0},{9,1},... | collective-permute-start | bytes 1572872 | tf_op jit(solution)/shard_map/ppermute | solution.py:83
  181.6 40.2 %collective-permute-start.27 = (bf16[1,2,2,32,2048]{4,3,2,1,0:T(8,128)(2,1)}, bf16[1,2,2,32,2048]{4,3,2,1,0:T(8,128)(2,1)}, u32[]{:S(2)}, u32[]{:S(2)}) collective-permute-start(bf16[1,2,2,32,2048]{4,3,2,1,0:T(8,128)(2,1)} %get-tuple-element.285), channel_id=1, source_target_pairs={{0,16},{1,17},{2,18},{3,19},{4,20},{5,21},{6,22},{7,23},{8,24},{9,... | collective-permute-start | bytes 1572872 | tf_op jit(solution)/shard_map/ppermute | solution.py:83
  263.8 39.3 %collective-permute-start.33 = (bf16[2,2,8,2,2,16,256]{6,5,4,3,2,1,0:T(8,128)(2,1)}, bf16[2,2,8,2,2,16,256]{6,5,4,3,2,1,0:T(8,128)(2,1)}, u32[]{:S(2)}, u32[]{:S(2)}) collective-permute-start(bf16[2,2,8,2,2,16,256]{6,5,4,3,2,1,0:T(8,128)(2,1)} %constant_dynamic-update-slice_fusion.43.refs_0_), channel_id=1, source_target_pairs={{0,16},{1,17},{2,18},{3,19},{4,20},{5,21},{6,22},{7,23},{8,24},{9,... | collective-permute-start | bytes 3145736 | tf_op jit(solution)/shard_map/ppermute | solution.py:83
  266.1 37.0 %collective-permute-start.34 = (bf16[2,2,8,2,2,16,256]{6,5,4,3,2,1,0:T(8,128)(2,1)S(1)}, bf16[2,2,8,2,2,16,256]{6,5,4,3,2,1,0:T(8,128)(2,1)}, u32[]{:S(2)}, u32[]{:S(2)}) collective-permute-start(bf16[2,2,8,2,2,16,256]{6,5,4,3,2,1,0:T(8,128)(2,1)S(1)} %constant_dynamic-update-slice_fusion.45.refs_2_), channel_id=1, source_target_pairs={{0,8},{1,9},{2,10},{3,11},{4,12},{5,13},{6,14},{7,15},{8,0},{9,1},... | collective-permute-start | bytes 3145736 | tf_op jit(solution)/shard_map/ppermute | solution.py:83
  305.5 38.0 %collective-permute-start.38 = (bf16[2,2,2,32,2048]{4,3,2,1,0:T(8,128)(2,1)S(1)}, bf16[2,2,2,32,2048]{4,3,2,1,0:T(8,128)(2,1)S(1)}, u32[]{:S(2)}, u32[]{:S(2)}) collective-permute-start(bf16[2,2,2,32,2048]{4,3,2,1,0:T(8,128)(2,1)S(1)} %constant_dynamic-update-slice_fusion.47.refs_0_), channel_id=1, source_target_pairs={{0,16},{1,17},{2,18},{3,19},{4,20},{5,21},{6,22},{7,23},{8,24},{9,... | collective-permute-start | bytes 3145736 | tf_op jit(solution)/shard_map/ppermute | solution.py:83
  307.7 35.8 %collective-permute-start.39 = (bf16[2,2,2,32,2048]{4,3,2,1,0:T(8,128)(2,1)S(1)}, bf16[2,2,2,32,2048]{4,3,2,1,0:T(8,128)(2,1)S(1)}, u32[]{:S(2)}, u32[]{:S(2)}) collective-permute-start(bf16[2,2,2,32,2048]{4,3,2,1,0:T(8,128)(2,1)S(1)} %constant_dynamic-update-slice_fusion.49.refs_2_), channel_id=1, source_target_pairs={{0,8},{1,9},{2,10},{3,11},{4,12},{5,13},{6,14},{7,15},{8,0},{9,1},... | collective-permute-start | bytes 3145736 | tf_op jit(solution)/shard_map/ppermute | solution.py:83
  652.8 50.1 %collective-permute-start.77 = (bf16[4,4,32,256]{3,2,1,0:T(8,128)(2,1)}, bf16[4,4,32,256]{3,2,1,0:T(8,128)(2,1)}, u32[]{:S(2)}, u32[]{:S(2)}) collective-permute-start(bf16[4,4,32,256]{3,2,1,0:T(8,128)(2,1)} %fusion.154), channel_id=1, source_target_pairs={{0,4},{1,5},{2,6},{3,7},{4,0},{5,1},{6,2},{7,3},{8,12},{9,13},{10,... | collective-permute-start | bytes 786440 | tf_op jit(solution)/shard_map/ppermute | solution.py:83
  666.7 42.9 %collective-permute-start.74 = (bf16[256,1024]{1,0:T(8,128)(2,1)}, bf16[256,1024]{1,0:T(8,128)(2,1)}, u32[]{:S(2)}, u32[]{:S(2)}) collective-permute-start(bf16[256,1024]{1,0:T(8,128)(2,1)} %get-tuple-element.831), channel_id=1, source_target_pairs={{0,4},{1,5},{2,6},{3,7},{4,0},{5,1},{6,2},{7,3},{8,12},{9,13},{10,... | collective-permute-start | bytes 1572872 | tf_op jit(solution)/shard_map/ppermute | solution.py:83
  692.5 45.7 %collective-permute-start.76 = (bf16[512,1024]{1,0:T(8,128)(2,1)}, bf16[512,1024]{1,0:T(8,128)(2,1)}, u32[]{:S(2)}, u32[]{:S(2)}) collective-permute-start(bf16[512,1024]{1,0:T(8,128)(2,1)} %get-tuple-element.835), channel_id=1, source_target_pairs={{0,4},{1,5},{2,6},{3,7},{4,0},{5,1},{6,2},{7,3},{8,12},{9,13},{10,... | collective-permute-start | bytes 3145736 | tf_op jit(solution)/shard_map/ppermute | solution.py:83
  (292 other events, 2876.3 us)
Sparse Core Ops, SparseCore 0:
  19.9 42.2 all-gather.16
  64.3 27.6 all-gather.18
  94.1 27.4 all-gather.20
  123.6 27.4 all-gather.22
  153.0 27.4 all-gather.24
  182.5 27.4 all-gather.26
  212.1 27.4 all-gather.28
  241.1 80.2 all-gather.30

commit v3 on v2

--- a/solution.py
+++ b/solution.py
@@ -212,39 +212,36 @@
     for source, (labels, first) in zip(sources, plan):
         for place, label in enumerate(labels):
             chip = own ^ (label // 2)
-            for step in range(source.shape[1]):
-                block = source.at[place, step]
-                z = first + step
-                if form == "attention":
-                    split = staged[0].shape[-1]
-                    half = staged[1].shape[-1]
+            block = source.at[place]
+            span = slice(first, first + source.shape[1])
+            if form == "attention":
+                split = staged[0].shape[-1]
+                for side in range(2):
+                    copies.append((block.at[:, side, :, :split], 0, (chip, side, span)))
+                    copies.append((block.at[:, side, :, split:], 1, (side, chip, span)))
+            elif form == "first":
+                for side in range(2):
+                    copies.append((block.at[:, side], 0, (chip, side, span)))
+            elif form == "second":
+                copies.append((block.at[:, 0], 0, (chip, span)))
+            else:
+                for layer in range(2):
                     for side in range(2):
-                        copies.append((block.at[side, :, :split], 0, (chip, side, z)))
-                        copies.append((block.at[side, :, split:], 1, (side, chip, z)))
-                elif form == "first":
-                    for side in range(2):
-                        copies.append((block.at[side], 0, (chip, side, z)))
-                elif form == "second":
-                    copies.append((block.at[0], 0, (chip, z)))
-                else:
-                    for layer in range(2):
-                        down = block.at[2 * layer + kind]
-                        for side in range(2):
-                            copies.append((down.at[side], 0, (layer, chip, side, z)))
-                        up = block.at[4 + 2 * layer + kind]
-                        for fold in range(4):
-                            copies.append((up.at[fold // 2, fold % 2], 1, (layer, fold, chip, z)))
+                        down = block.at[:, 2 * layer + kind, side]
+                        copies.append((down, 0, (layer, chip, side, span)))
+                    for fold in range(4):
+                        up = block.at[:, 4 + 2 * layer + kind, fold // 2, fold % 2]
+                        copies.append((up, 1, (layer, fold, chip, span)))
     started = []
     for place, (origin, turn, index) in enumerate(copies):
         copy = pltpu.make_async_copy(origin, staged[turn].at[index], in_sems.at[place])
         copy.start()
         started.append(copy)
+    for copy in started:
+        copy.wait()
     ended = []
-    for place, (origin, turn, index) in enumerate(copies):
-        started[place].wait()
-        copy = pltpu.make_async_copy(
-            staged[turn].at[index], targets[turn].at[index], out_sems.at[place]
-        )
+    for turn, (origin, target) in enumerate(zip(staged, targets)):
+        copy = pltpu.make_async_copy(origin, target, out_sems.at[turn])
         copy.start()
         ended.append(copy)
     for copy in ended:
@@ -253,7 +250,7 @@
 
 def place_blocks(pieces, where, form, shapes):
     plan = [(labels, first) for labels, first, _ in pieces]
-    blocks = sum(len(labels) * stack.shape[1] for labels, _, stack in pieces)
+    blocks = sum(len(labels) for labels, _, _ in pieces)
     copies = blocks * {"attention": 4, "first": 2, "second": 1, "adapter": 12}[form]
     anywhere = pl.BlockSpec(memory_space=pl.ANY)
     return pl.pallas_call(
@@ -264,7 +261,7 @@
             in_specs=[anywhere] * len(pieces),
             out_specs=[anywhere] * len(shapes),
             scratch_shapes=[pltpu.VMEM(shape, jnp.bfloat16) for shape in shapes]
-            + [pltpu.SemaphoreType.DMA((copies,))] * 2,
+            + [pltpu.SemaphoreType.DMA((copies,)), pltpu.SemaphoreType.DMA((len(shapes),))],
         ),
         out_shape=[jax.ShapeDtypeStruct(shape, jnp.bfloat16) for shape in shapes],
         compiler_params=pltpu.CompilerParams(vmem_limit_bytes=24 * MEBI),
@@ -375,14 +372,47 @@
     return (branch, (low_in, slope, inner_slope, inner_low))
 
 
+def feed_grad_kernel(grad_ref, second_ref, slope_ref, first_ref, out_ref):
+    hidden_grad = bfloat(times_second(grad_ref[...], second_ref[...]) * slope_ref[...])
+    part = times_second(hidden_grad, first_ref[...])
+
+    @pl.when(pl.program_id(0) == 0)
+    def _():
+        out_ref[...] = part
+
+    @pl.when(pl.program_id(0) > 0)
+    def _():
+        out_ref[...] += part
+
+
+def feed_grad(grad, w_second, slope, w_first):
+    rows, width = grad.shape
+    units = w_second.shape[0]
+    tile = min(units, 512)
+    return pl.pallas_call(
+        feed_grad_kernel,
+        grid=(units // tile,),
+        in_specs=[
+            pl.BlockSpec((rows, width), lambda i: (0, 0)),
+            pl.BlockSpec((tile, width), lambda i: (i, 0)),
+            pl.BlockSpec((rows, tile), lambda i: (0, i)),
+            pl.BlockSpec((width, tile), lambda i: (0, i)),
+        ],
+        out_specs=pl.BlockSpec((rows, width), lambda i: (0, 0)),
+        out_shape=jax.ShapeDtypeStruct((rows, width), jnp.float32),
+        compiler_params=pltpu.CompilerParams(vmem_limit_bytes=40 * MEBI),
+        cost_estimate=LIGHT,
+    )(grad, w_second, slope, w_first)
+
+
 def feed_backward(grad, cache, w_first, w_second, down, upward):
     low_in, slope, inner_slope, inner_low = cache
-    hidden_grad = bfloat(times_second(bfloat(grad), w_second) * slope)
+    hidden_part = feed_grad(bfloat(grad), w_second, slope, w_first)
     adapter_grad = bfloat(4.0 * grad)
     upward_grad = times_first(inner_low, adapter_grad)
     inner_grad = bfloat(times_second(adapter_grad, upward) * inner_slope)
     down_grad = times_first(low_in, inner_grad)
-    value_grad = times_second(hidden_grad, w_first) + times_second(inner_grad, down)
+    value_grad = hidden_part + times_second(inner_grad, down)
     return (value_grad, down_grad, upward_grad)
 
 
@@ -529,17 +559,21 @@
     return halves
 
 
-def halved_sum(halves, orders):
+def halved_steps(halves, orders):
     for turn in range(len(orders[0])):
         sent, kept = [], []
         for half, bits in zip(halves, orders):
             keep = [key for key in sorted(half) if not key & bits[turn]]
             kept.append(keep)
-            sent.append(jnp.stack([bfloat(half[key | bits[turn]]) for key in keep]))
-        got = exchange(sent, [bits[turn] for bits in orders])
+            away = jnp.stack([bfloat(half[key | bits[turn]]) for key in keep])
+            sent += [swap(away, bits[turn], 0), jnp.stack([half[key] for key in keep])]
+        done = yield sent
         halves = [
-            {key: half[key] + other[place].astype(jnp.float32) for place, key in enumerate(keep)}
-            for half, keep, other in zip(halves, kept, got)
+            {
+                key: own[place].astype(jnp.float32) + got[place].astype(jnp.float32)
+                for place, key in enumerate(keep)
+            }
+            for keep, got, own in zip(kept, done[::2], done[1::2])
         ]
     return [half[0] for half in halves]
 
@@ -572,6 +606,63 @@
     return [half[0] for half in halves]
 
 
+def fold_kernel(
+    orders, where_ref, down_ref, other_ref, up_ref, *outs
+):
+    core, kind = where_ref[0], where_ref[1]
+    chips, _, kv_count, _, lanes = down_ref.shape
+    folds = up_ref.shape[-1] // lanes
+    for task, bit in enumerate(orders):
+        gate = (kind == task).astype(jnp.float32)
+        place = where_ref[2 + task]
+        keep_ref, send_ref = outs[2 * task], outs[2 * task + 1]
+        pairs = [(high, low) for high in range(chips // (2 * bit)) for low in range(bit)]
+        for index, (high, low) in enumerate(pairs):
+            for side, out_ref in ((place, keep_ref), (1 - place, send_ref)):
+                chip = (2 * high + side) * bit + low
+                for z in range(kv_count):
+                    up = up_ref[chip, z]
+                    parts = [down_ref[chip, core, z], other_ref[chip, z].astype(jnp.float32)]
+                    parts += [up[:, fold * lanes : (fold + 1) * lanes] for fold in range(folds)]
+                    out_ref[index, z] = (jnp.concatenate(parts) * gate).astype(out_ref.dtype)
+
+
+def halve_kernel(posts, where_ref, *refs):
+    tasks = len(posts)
+    for task, post in enumerate(posts):
+        keep_ref, got_ref = refs[2 * task], refs[2 * task + 1]
+        out_ref, send_ref = refs[2 * tasks + 2 * task], refs[2 * tasks + 2 * task + 1]
+        place = where_ref[task]
+        for high in range(keep_ref.shape[0] // (2 * post)):
+            for low in range(post):
+                for side, target in ((place, out_ref), (1 - place, send_ref)):
+                    index = (2 * high + side) * post + low
+                    total = keep_ref[index] + got_ref[index].astype(jnp.float32)
+                    target[high * post + low] = total.astype(target.dtype)
+
+
+def column_kernel(tasks, where_ref, *refs):
+    own_ref, sends = refs[2 * tasks], refs[2 * tasks + 1 :]
+    for task in range(tasks):
+        keep_ref, got_ref = refs[2 * task], refs[2 * task + 1]
+        for step, target in enumerate((own_ref,) + sends):
+            z = where_ref[0] ^ step
+            total = keep_ref[0, z] + got_ref[0, z].astype(jnp.float32)
+            target[task] = total.astype(target.dtype)
+
+
+def in_vmem(kernel, where, arrays, outs):
+    whole = pl.BlockSpec(memory_space=pltpu.VMEM)
+    return pl.pallas_call(
+        kernel,
+        in_specs=[pl.BlockSpec(memory_space=pltpu.SMEM)] + [whole] * len(arrays),
+        out_specs=[whole] * len(outs),
+        out_shape=[jax.ShapeDtypeStruct(shape, dtype) for shape, dtype in outs],
+        compiler_params=pltpu.CompilerParams(vmem_limit_bytes=40 * MEBI),
+        cost_estimate=LIGHT,
+    )(jnp.stack(where).astype(jnp.int32), *arrays)
+
+
 def adapter_steps(down_grad, up_grad, kind, tasks, lead):
     seq_count, kv_count = lax.axis_size("seq"), lax.axis_size("kv")
     seq_index, kv_index = lax.axis_index("seq"), lax.axis_index("kv")
@@ -582,42 +673,54 @@
     down_rows = down_grad.shape[0] // devices
     up_rows = up_grad.shape[0] // (chips * kv_count)
     folds = up_grad.shape[1] // lanes
+    height = 2 * down_rows + folds * up_rows
     down_part = down_grad.reshape(chips, 2, kv_count, down_rows, lanes)
-    up_part = up_grad.reshape(chips, kv_count, up_rows, folds, lanes).transpose(0, 1, 3, 2, 4)
-    up_part = up_part.reshape(chips, kv_count, folds * up_rows, lanes)
-    mine, other, up_part = yield [
-        pick(down_part, 1, core),
+    up_part = up_grad.reshape(chips, kv_count, up_rows, folds * lanes)
+    down_part, other, up_part = yield [
+        down_part,
         swap(bfloat(pick(down_part, 1, 1 - core)), 1, 0),
         up_part,
     ]
-    grad = jnp.concatenate([mine, other.astype(jnp.float32), up_part], 2)
-    height = grad.shape[2]
     x_bits, y_bits = plane_bits()
     orders = [(x_bits + y_bits, y_bits + x_bits)[task % 2] for task in range(tasks)]
-    lefts = [list(reversed(x_bits + y_bits)) for _ in range(tasks)]
-    parts = []
-    for task in range(tasks):
-        part = grad * (kind == task).astype(jnp.float32)
-        parts.append(
-            part.reshape([2] * (len(x_bits) + len(y_bits)) + [kv_count, height, lanes])
-        )
+    lefts = [sorted(x_bits + y_bits) for _ in range(tasks)]
+
+    def shapes(count):
+        shape = (count, kv_count, height, lanes)
+        return [(shape, dtype) for _ in range(tasks) for dtype in (jnp.float32, jnp.bfloat16)]
+
+    count = chips // 2
+    parts = in_vmem(
+        functools.partial(fold_kernel, [bits[0] // 2 for bits in orders]),
+        [core, kind] + [(seq_index // bits[0]) % 2 for bits in orders],
+        [down_part, other, up_part],
+        shapes(count),
+    )
     for turn in range(len(orders[0])):
-        kept, got = [], []
-        for part, bits, left in zip(parts, orders, lefts):
-            bit = bits[turn]
-            axis = left.index(bit)
-            left.remove(bit)
-            place = (seq_index // bit) % 2
-            kept.append(pick(part, axis, place))
-            got.append(swap(bfloat(pick(part, axis, 1 - place)), bit, 0))
-        done = yield kept + got
-        parts = [
-            part + other.astype(jnp.float32) for part, other in zip(done[:tasks], done[tasks:])
-        ]
-    part = jnp.stack(parts, 1)
-    done = yield [pick(part, 0, kv_index)] + [
-        swap(bfloat(pick(part, 0, kv_index ^ step)), 0, step) for step in range(1, kv_count)
-    ]
+        parts = list(parts)
+        for task, bits in enumerate(orders):
+            lefts[task].remove(bits[turn])
+            parts[2 * task + 1] = swap(parts[2 * task + 1], bits[turn], 0)
+        parts = yield parts
+        if turn + 1 < len(orders[0]):
+            count //= 2
+            bits = [order[turn + 1] for order in orders]
+            parts = in_vmem(
+                functools.partial(
+                    halve_kernel, [2 ** left.index(bit) for left, bit in zip(lefts, bits)]
+                ),
+                [(seq_index // bit) % 2 for bit in bits],
+                parts,
+                shapes(count),
+            )
+    shape = (tasks, height, lanes)
+    outs = in_vmem(
+        functools.partial(column_kernel, tasks),
+        [kv_index],
+        parts,
+        [(shape, jnp.float32)] + [(shape, jnp.bfloat16)] * (kv_count - 1),
+    )
+    done = yield [outs[0]] + [swap(outs[step], 0, step) for step in range(1, kv_count)]
     total = done[0]
     for other in done[1:]:
         total = total + other.astype(jnp.float32)
@@ -651,6 +754,16 @@
         except StopIteration as stop:
             self.result = stop.value
 
+    def along(self, values):
+        count = len(self.sent)
+        done = lax.optimization_barrier(tuple(self.sent) + tuple(values))
+        if self.result is None:
+            try:
+                self.sent = self.steps.send(list(done[:count]))
+            except StopIteration as stop:
+                self.result, self.sent = stop.value, []
+        return list(done[count:])
+
     def finish(self):
         while self.result is None:
             try:
@@ -661,20 +774,20 @@
 
 
 def total_sum(value):
-    step = 1
-    while step < lax.axis_size("seq"):
-        value = value + swap(value, step, 0)
-        step *= 2
-    step = 1
-    while step < lax.axis_size("kv"):
-        value = value + swap(value, 0, step)
-        step *= 2
+    seq_count, kv_count = lax.axis_size("seq"), lax.axis_size("kv")
+    value = value + swap(value, 1, 0)
+    masks = [(bit, 0) for bit in sum(plane_bits(), [])]
+    masks += [(0, 1 << place) for place in range(kv_count.bit_length() - 1)]
+    for first, second in zip(masks[::2], masks[1::2]):
+        both = (first[0] | second[0], first[1] | second[1])
+        got = [swap(value, *mask) for mask in (first, second, both)]
+        value = (value + got[0]) + (got[1] + got[2])
     return value
 
 
-def item_rows(embeds):
+def half_rows(embeds):
     seq_count, kv_count = lax.axis_size("seq"), lax.axis_size("kv")
-    seq_index, kv_index = lax.axis_index("seq"), lax.axis_index("kv")
+    kv_index = lax.axis_index("kv")
     got = []
     for turn in range(2):
         pairs = []
@@ -685,10 +798,9 @@
         sent = pick(embeds[:, 0], 0, (kv_index % 2) ^ turn)
         got.append(lax.ppermute(sent, AXES, pairs))
     swapped = kv_index // 2 == 1
-    mine = jnp.concatenate(
+    return jnp.concatenate(
         [jnp.where(swapped, got[1], got[0]), jnp.where(swapped, got[0], got[1])]
     )
-    return jnp.concatenate(in_order(seq_index % 2, mine, swap(mine, 1, 0)))
 
 
 def adam_update(weight, first, second, grad, rate, decay, count_step):
@@ -808,24 +920,30 @@
 
     def with_last(made):
         return [
-            (len(groups) - 1, plane_first_steps(groups[-1][0])),
-            (0, column_first_steps(groups[0][0])),
+            (len(groups) - 1, plane_first_steps(after(groups[-1][0], made["tie"]))),
+            (2, column_first_steps(groups[2][0])),
         ]
 
     def ids_in(made):
-        parts = [pick(targets, 0, batch)]
+        ids = after(targets, made["tie"])
+        parts = [pick(ids, 0, batch)]
         for turn in range(1, kv_count):
-            parts.append(swap(pick(targets, 0, batch ^ (turn // 2)), 0, turn))
+            parts.append(swap(pick(ids, 0, batch ^ (turn // 2)), 0, turn))
         order = kv_index ^ jnp.arange(kv_count, dtype=jnp.int32)
         chosen = order[:, None] == jnp.arange(kv_count, dtype=jnp.int32)[None, :]
         parts = jnp.sum(jnp.where(chosen[:, :, None, None], jnp.stack(parts)[:, None], 0), 0)
         return {"ids": parts.transpose(1, 0, 2)}
 
     def rows_in(made):
-        return {
-            "source": item_rows(src_embed),
-            "target": item_rows(tgt_embed),
-        }
+        source, target = half_rows(src_embed), half_rows(tgt_embed)
+        return {"half_rows": (source, target)}
+
+    def whole_rows(made):
+        source, target = [
+            jnp.concatenate(in_order(core, half_item, swap(half_item, 1, 0)))
+            for half_item in made["half_rows"]
+        ]
+        return {"source": source, "target": target}
 
     def table_in(made):
         low = after(embed, made["tie"])
@@ -869,7 +987,8 @@
     def last_in(made):
         return {"last": step + 0}
 
-    starts = [with_last] + [column_start(place) for place in range(1, len(groups) - 1)]
+    starts = [column_start(place) for place in range(len(groups) - 1)]
+    starts[2] = with_last
     def place(made, group):
         _, form, shape = groups[group]
         return place_blocks(made[group], where, form, shape)
@@ -941,9 +1060,9 @@
 
     extras = {
         0: rows_in,
-        1: ids_in,
+        1: whole_rows,
         2: table_in,
-        3: sum_in,
+        3: lambda made: sum_in(made) | ids_in(made),
         4: encoder_attention,
         5: decoder_attention,
         6: lambda made: encoder_hidden(made) | last_in(made),
@@ -967,6 +1086,16 @@
     down_all, up_all = made["adapters"]
     enc_feed = made["feed0"][1]
     attn_w = [made["enc_w"], made["dec_w"], made["cross_w"]]
+    down_orders = [[1] + list(bits) for bits in orders]
+    linear_steps = Steps(
+        halved_steps(
+            [
+                {key: after(linear[h, key], made["tie"]) for key in range(seq_count)}
+                for h in range(2)
+            ],
+            down_orders,
+        )
+    )
     y2, cache5 = norm_forward(y1 + core_sum(part), gains[5], biases[5])
     first_w = [made["first0"], place(gathered, 6)[0].reshape(width, hidden // 2)]
     labels, stack = gathered[len(groups) - 1]
@@ -976,20 +1105,14 @@
     branch, dec_feed = feed_forward(bfloat(y2), first_w[1], second_w[1], down_all[1], up_all[1])
     y3, cache6 = norm_forward(y2 + core_sum(branch), gains[6], biases[6])
 
-    down_orders = [[1] + list(bits) for bits in orders]
-    linear_sum = halved_sum(
-        [
-            {key: after(linear[h, key], made["tie"]) for key in range(seq_count)}
-            for h in range(2)
-        ],
-        down_orders,
-    )
+    linear_steps.after(y2)
     y3_low = bfloat(y3)
     near = [
         lax.dynamic_slice_in_dim(y3_low, place * own_rows + h * half, half)
         for h in range(2)
         for place in (core, 1 - core)
     ]
+    linear_steps.after(near[0])
     far = spread([near[0], near[2]], [list(bits) + [1] for bits in orders])
     near = jnp.concatenate(near)
     far = jnp.concatenate([half_far[key] for half_far in far for key in range(2, seq_count)])
@@ -1005,9 +1128,7 @@
             for key in range(first, last):
                 pair = jnp.stack([tops[h, key - first], totals[h, key - first]])
                 blocks[h][key] = (mixed[h, key - first], pair)
-        rows_alive = alive[:, first:last].astype(jnp.float32)[..., None]
-        rows = rows.astype(jnp.float32).reshape(mixed.shape)
-        loss_part = loss_part - jnp.sum(rows_alive * rows * linear[:, first:last].astype(jnp.float32))
+    linear_sum = linear_steps.finish()
     merged = merged_sum(blocks, down_orders)
     final_grad = []
     for h, (mix, (top, total)) in enumerate(merged):
@@ -1022,37 +1143,50 @@
     inner_grad, down_grad, up_grad = feed_backward(
         grad, dec_feed, first_w[1], second_w[1], down_all[1], up_all[1]
     )
+    tied = lax.optimization_barrier
+    inner_grad, down_grad, up_grad = tied((inner_grad, down_grad, up_grad))
     dec_steps = Steps(adapter_steps(down_grad, up_grad, kind, tasks, lead))
     grad, grad5 = norm_backward(grad + core_sum(inner_grad), cache5, gains[5])
     out_grad = bfloat(times_second(bfloat(grad), attn_w[2][1]))
-    dec_steps.after(out_grad)
     dq, dk, dv = attend_back(source_length, False, (cross_query, 0), (cross_pair, 0), out_grad)
     enc_grad = times_second(jnp.concatenate([dk, dv], 1), attn_w[2][0][:, half_w:])
     query_grad = times_second(dq, attn_w[2][0][:, :half_w])
-    dec_steps.after(dq)
-    summed = core_sum(jnp.concatenate([enc_grad, query_grad]))
+    (part,) = dec_steps.along([jnp.concatenate([enc_grad, query_grad])])
+    summed = core_sum(part)
     enc_rows = x0.shape[0]
     dec_grad, grad4 = norm_backward(grad + summed[enc_rows:], cache4, gains[4])
     grad, grad2 = norm_backward(summed[:enc_rows], cache2, gains[2])
     inner_grad, down_grad, up_grad = feed_backward(
         grad, enc_feed, first_w[0], second_w[0], down_all[0], up_all[0]
     )
-    dec_steps.after(inner_grad)
+    inner_grad, down_grad, up_grad, dec_grad, grad = dec_steps.along(
+        [inner_grad, down_grad, up_grad, dec_grad, grad]
+    )
     enc_steps = Steps(adapter_steps(down_grad, up_grad, kind, tasks, lead))
+    inner_sum = core_sum(inner_grad)
     out_grad = bfloat(times_second(bfloat(dec_grad), attn_w[1][1]))
     parts = attend_back(target_length, True, (self_pair, 0), (self_pair, half_w), out_grad)
-    enc_steps.after(out_grad)
-    dec_steps.after(parts[0])
-    self_grad = times_second(jnp.concatenate(parts, 1), attn_w[1][0])
-    enc_steps.after(parts[0])
-    _, grad3 = norm_backward(dec_grad + core_sum(self_grad), cache3, gains[3])
-    grad, grad1 = norm_backward(grad + core_sum(inner_grad), cache1, gains[1])
+    part = times_second(jnp.concatenate(parts, 1), attn_w[1][0])
+    part, inner_sum, *sent = dec_steps.along([part, inner_sum] + enc_steps.sent)
+    enc_steps.sent = sent
+    part, inner_sum = enc_steps.along([part, inner_sum])
+    self_sum = core_sum(part)
+    grad, grad1 = norm_backward(grad + inner_sum, cache1, gains[1])
     out_grad = bfloat(times_second(bfloat(grad), attn_w[0][1]))
     parts = attend_back(source_length, False, (enc_pair, 0), (enc_pair, half_w), out_grad)
-    enc_steps.after(parts[0])
-    enc_grad = times_second(jnp.concatenate(parts, 1), attn_w[0][0])
-    _, grad0 = norm_backward(grad + core_sum(enc_grad), cache0, gains[0])
+    part = times_second(jnp.concatenate(parts, 1), attn_w[0][0])
+    part, self_sum, grad = enc_steps.along([part, self_sum, grad])
+    enc_sum = core_sum(part)
+    _, grad3 = norm_backward(dec_grad + self_sum, cache3, gains[3])
+    (enc_sum,) = enc_steps.along([enc_sum])
+    _, grad0 = norm_backward(grad + enc_sum, cache0, gains[0])
     enc_sums, dec_sums = enc_steps.finish(), dec_steps.finish()
+
+    linear = after(linear, enc_sum)
+    for rows, first, last in ((near, 0, 2), (far, 2, seq_count)):
+        rows = rows.astype(jnp.float32).reshape(2, last - first, half, width)
+        rows_alive = alive[:, first:last].astype(jnp.float32)[..., None]
+        loss_part = loss_part - jnp.sum(rows_alive * rows * linear[:, first:last].astype(jnp.float32))
 
     norm_grad = 0.5 * jnp.stack([grad0, grad1, grad2, grad3, grad4, grad5, grad6], 1)
     down_part = jnp.stack([enc_sums[0], dec_sums[0]])

time: 803 us -> 796 us (level)
  waiting for transfers between devices: 151 us -> 192 us
  Pallas kernels: 162 us -> 133 us
  matrix products: 61.7 us -> 37.2 us
  starting transfers between devices: 106 us -> 124 us
  local copies, waits for them, and re-layouts: 158 us -> 146 us
    ppermute x94 -> x96, waiting for transfers between devices: 141 us -> 180 us  [swap(): return lax.ppermute(value, AXES, pairs)]
    pallas_call x8, Pallas kernels: 57.3 us -> 19.4 us  [place_blocks(): pl.pallas_call(functools.partial(place_kernel, plan, form), grid_spec=plt...]
    dot_general x13 -> x11, matrix products: 33.4 us -> 10.1 us  [times_second(): lax.dot_general(left, right, (((1,), (1,)), ((), ())), preferred_element_...]
    pallas_call x0 -> x8, Pallas kernels: none -> 16.3 us  [the longest x2 12.1 us: feed_grad(): pl.pallas_call(feed_grad_kernel, grid=(units // tile,), in_specs=[pl.Bloc...]
    all_gather x7, starting transfers between devices: 0.63 us -> 11.3 us  [column_first_steps(): column, = (yield [lax.all_gather(own, 'kv')])]
    unnamed x477 -> x495, local copies, waits for them, and re-layouts: 44.6 us -> 49.8 us
    ppermute x94 -> x96, starting transfers between devices: 97.7 us -> 101 us  [swap(): return lax.ppermute(value, AXES, pairs)]
    convert_element_type x14 -> x19, other arithmetic: 14.2 us -> 17.3 us  [bfloat(): return value.astype(jnp.bfloat16)]
  transfers between devices with their start and end apart: 106 -> 108, of which waited for: 33 -> 35; matrix products, arithmetic and copies ran while one was open for 32% -> 30% of each run, Pallas kernels for 15% -> 16%
where the time goes in v3:
time: 796 us; the launch traced here: 789 us
  waiting for transfers between devices  192 us (24%)
  local copies, waits for them, and re-layouts  146 us (18%)
  Pallas kernels  133 us (17%)
  other arithmetic  129 us (16%)
  starting transfers between devices  124 us (16%)
  matrix products  37.2 us (5%)
  between operations  28.4 us (4%)
    ppermute x96, waiting for transfers between devices, swap(): return lax.ppermute(value, AXES, pairs)  180 us
    ppermute x96, starting transfers between devices, swap(): return lax.ppermute(value, AXES, pairs)  101 us
    pallas_call x2, Pallas kernels, vocab_pass(): pl.pallas_call(functools.partial(vocab_kernel, count, tile, step), grid_s...  58.2 us
    unnamed x495, local copies, waits for them, and re-layouts  49.8 us
    pallas_call x6, Pallas kernels, attention_call(): pl.pallas_call(functools.partial(kernel, causal), grid_spec=pltpu.Prefetc...  38.8 us
    dot_general x15, matrix products, times_plain(): return jnp.dot(left, right, preferred_element_type=jnp.float32)  25.5 us
    pallas_call x8, Pallas kernels, place_blocks(): pl.pallas_call(functools.partial(place_kernel, plan, form), grid_spec=plt...  19.4 us
    gather x1, local copies, waits for them, and re-layouts, linear_in(): jnp.take(embed, jnp.clip(local_ids, 0, vocab_rows - 1), axis=0)  17.4 us
  transfers between devices with their start and end apart: 108, of which 35 were waited for; matrix products, arithmetic and copies ran while one was open for 30% of the time, Pallas kernels for 16%

profile of v3, /device:TPU:0, one launch (start us, length us, event | category | flops | bytes accessed | tf_op | source)
XLA Modules:
  0.0 789.0 jit_solution(15113593640363646899)
XLA Ops:
  40.8 11.1 %all-gather.27.cloned.1.call-start = ((), (), s32[]{:S(2)}) async-start(), calls=%async_computation.5 | async-start | bytes 1310720 | tf_op jit(solution)/shard_map/all_gather | solution.py:147
  70.3 8.9 %collective-permute-done.4 = bf16[1,2,1,128,1024]{4,3,1,2,0:T(8,128)(2,1)S(1)} collective-permute-done((bf16[1,2,1,128,1024]{4,3,1,2,0:T(8,128)(2,1)S(1)}, bf16[1,2,1,128,1024]{4,3,1,2,0:T(8,128)(2,1)S(1)}, u32[]{:S(2)}, u32[]{:S(2)}) %collective-permute-start.4) | collective-permute-done | bytes 524320 | tf_op jit(solution)/shard_map/ppermute | solution.py:83
  80.5 11.9 %all-gather.19.cloned.1.call-done = bf16[8,32,2048]{2,1,0:T(8,128)(2,1)} async-done(((bf16[2,32,2048]{2,1,0:T(8,128)(2,1)}), bf16[8,32,2048]{2,1,0:T(8,128)(2,1)}) %all-gather.19.cloned.1.call-update) | async-done | bytes 1048592 | tf_op jit(solution)/shard_map/all_gather | solution.py:147
  104.1 29.7 %collective-permute-done.13 = bf16[1,1,1,64,1024]{4,3,2,1,0:T(8,128)(2,1)S(1)} collective-permute-done((bf16[1,1,1,64,1024]{4,3,2,1,0:T(8,128)(2,1)S(1)}, bf16[1,1,1,64,1024]{4,3,2,1,0:T(8,128)(2,1)S(1)}, u32[]{:S(2)}, u32[]{:S(2)}) %collective-permute-start.13) | collective-permute-done | bytes 131104 | tf_op jit(solution)/shard_map/ppermute | solution.py:83
  136.3 13.0 %pad.14.table_ref = bf16[6400,1024]{1,0:T(8,128)(2,1)} pad(bf16[6284,1024]{1,0:T(8,128)(2,1)} %param.36, bf16[]{:T(256)} %constant.340.clone.1), padding=0_116x0_0 | pad | bytes 25976834 | tf_op jit(solution)/shard_map/jit(_pad)/pad | solution.py:950
  169.1 18.6 %collective-permute-done.17 = bf16[2,1,1,64,1024]{4,3,2,1,0:T(8,128)(2,1)S(1)} collective-permute-done((bf16[2,1,1,64,1024]{4,3,2,1,0:T(8,128)(2,1)S(1)}, bf16[2,1,1,64,1024]{4,3,2,1,0:T(8,128)(2,1)S(1)}, u32[]{:S(2)}, u32[]{:S(2)}) %collective-permute-start.17) | collective-permute-done | bytes 262176 | tf_op jit(solution)/shard_map/ppermute | solution.py:83
  189.3 7.1 convert_reduce_fusion
  221.7 17.4 %gather_fusion = bf16[2048,1024]{1,0:T(8,128)(2,1)} fusion(bf16[6284,1024]{1,0:T(8,128)(2,1)} %param.36, s32[2048]{0:T(1024)S(1)} %fusion.146), kind=kCustom, calls=%fused_computation | custom fusion | bytes 8396800 | tf_op jit(solution)/shard_map/jit(_take)/gather | solution.py:980
  270.8 7.0 shard_map.303
  283.4 9.7 %collective-permute-done.30 = bf16[1,2,8,2,2,16,256]{6,5,4,3,2,1,0:T(8,128)(2,1)} collective-permute-done((bf16[1,2,8,2,2,16,256]{6,5,4,3,2,1,0:T(8,128)(2,1)}, bf16[1,2,8,2,2,16,256]{6,5,4,3,2,1,0:T(8,128)(2,1)}, u32[]{:S(2)}, u32[]{:S(2)}) %collective-permute-start.30) | collective-permute-done | bytes 524320 | tf_op jit(solution)/shard_map/ppermute | solution.py:83
  312.6 23.0 %collective-permute-done.35 = bf16[1,2,2,32,2048]{4,3,2,1,0:T(8,128)(2,1)} collective-permute-done((bf16[1,2,2,32,2048]{4,3,2,1,0:T(8,128)(2,1)}, bf16[1,2,2,32,2048]{4,3,2,1,0:T(8,128)(2,1)}, u32[]{:S(2)}, u32[]{:S(2)}) %collective-permute-start.35) | collective-permute-done | bytes 524320 | tf_op jit(solution)/shard_map/ppermute | solution.py:83
  352.1 24.1 %collective-permute-done.40 = bf16[1,2,2,32,2048]{4,3,2,1,0:T(8,128)(2,1)S(1)} collective-permute-done((bf16[1,2,2,32,2048]{4,3,2,1,0:T(8,128)(2,1)S(1)}, bf16[1,2,2,32,2048]{4,3,2,1,0:T(8,128)(2,1)S(1)}, u32[]{:S(2)}, u32[]{:S(2)}) %collective-permute-start.40) | collective-permute-done | bytes 524320 | tf_op jit(solution)/shard_map/ppermute | solution.py:83
  393.6 6.3 collective-permute-done.42.refs_1_
  410.1 5.4 fusion.5
  439.4 8.2 %collective-permute-done.47 = bf16[1,128,1024]{2,1,0:T(8,128)(2,1)S(1)} collective-permute-done((bf16[1,128,1024]{2,1,0:T(8,128)(2,1)S(1)}, bf16[1,128,1024]{2,1,0:T(8,128)(2,1)S(1)}, u32[]{:S(2)}, u32[]{:S(2)}) %collective-permute-start.47) | collective-permute-done | bytes 262176 | tf_op jit(solution)/shard_map/ppermute | solution.py:83
  454.3 24.5 %shard_map.311 = (f32[512,1024]{1,0:T(8,128)}, f32[512,128]{1,0:T(8,128)}) custom-call(s32[9]{0:T(128)} %pad_add_fusion.4.order_ref, bf16[512,1024]{1,0:T(8,128)(2,1)} %pad_maximum_fusion.6.rows_ref, bf16[6400,1024]{1,0:T(8,128)(2,1)} %pad.14.table_ref), custom_call_target="tpu_custom_call" | custom-call | flops 10066329600 | bytes 16252928 | tf_op jit(solution)/shard_map/pallas_call | solution.py:510
  487.2 33.7 %shard_map.312 = (f32[1536,1024]{1,0:T(8,128)}, f32[1536,128]{1,0:T(8,128)}) custom-call(s32[25]{0:T(128)} %pad_add_fusion.5.order_ref, bf16[1536,1024]{1,0:T(8,128)(2,1)} %copy-done.86, bf16[6400,1024]{1,0:T(8,128)(2,1)} %pad.14.table_ref), custom_call_target="tpu_custom_call" | custom-call | flops 30198988800 | bytes 22544384 | tf_op jit(solution)/shard_map/pallas_call | solution.py:510
  547.0 8.0 %collective-permute-done.58 = f32[2,2,128]{2,1,0:T(2,128)S(1)} collective-permute-done((f32[2,2,128]{2,1,0:T(2,128)S(1)}, f32[2,2,128]{2,1,0:T(2,128)S(1)}, u32[]{:S(2)}, u32[]{:S(2)}) %collective-permute-start.58) | collective-permute-done | bytes 2080 | tf_op jit(solution)/shard_map/ppermute | solution.py:83
  583.1 7.6 shard_map.313
  603.0 7.2 shard_map.314
  647.1 11.1 %shard_map.318 = (bf16[512,512]{1,0:T(8,128)(2,1)S(1)}, bf16[512,512]{1,0:T(8,128)(2,1)S(1)}, bf16[512,512]{1,0:T(8,128)(2,1)S(1)}) custom-call(s32[1]{0:T(128)} %bitcast.62.length_ref, bf16[512,1536]{1,0:T(8,128)(2,1)S(1)} %copy-done.1, bf16[512,1536]{1,0:T(8,128)(2,1)S(1)} %copy-done.1, bf16[512,1536]{1,0:T(8,128)(2,1)S(1)} %copy-done.1, ...), custom_call_target="tpu_custom_call" | custom-call | flops 1 | bytes 1 | tf_op jit(solution)/shard_map/pallas_call | solution.py:329
  666.0 18.8 %collective-permute-start.92 = (bf16[2,128,256]{2,1,0:T(8,128)(2,1)S(1)}, bf16[2,128,256]{2,1,0:T(8,128)(2,1)S(1)}, u32[]{:S(2)}, u32[]{:S(2)}) collective-permute-start(bf16[2,128,256]{2,1,0:T(8,128)(2,1)S(1)} %get-tuple-element.554), channel_id=1, source_target_pairs={{0,3},{1,2},{2,1},{3,0},{4,7},{5,6},{6,5},{7,4},{8,11},{9,10},{10,... | collective-permute-start | bytes 393224 | tf_op jit(solution)/shard_map/ppermute | solution.py:83
  687.3 5.2 shard_map.320
  742.9 5.8 collective-permute-done.88
  (1120 shorter events, 437.4 us)
Async XLA Ops:
  7.2 56.2 %all-gather.17.cloned.1.call-start = ((), (), s32[]{:S(2)}) async-start(), calls=%async_computation | async-start | bytes 1310720 | tf_op jit(solution)/shard_map/all_gather | solution.py:147
  19.7 72.7 %all-gather.19.cloned.1.call-start = ((), (), s32[]{:S(2)}) async-start(), calls=%async_computation.1 | async-start | bytes 1310720 | tf_op jit(solution)/shard_map/all_gather | solution.py:147
  21.8 127.5 %all-gather.21.cloned.1.call-start = ((), (), s32[]{:S(2)}) async-start(), calls=%async_computation.2 | async-start | bytes 1310720 | tf_op jit(solution)/shard_map/all_gather | solution.py:147
  21.9 41.2 %collective-permute-start = (bf16[64,1024]{1,0:T(8,128)(2,1)S(1)}, bf16[64,1024]{1,0:T(8,128)(2,1)S(1)}, u32[]{:S(2)}, u32[]{:S(2)}) collective-permute-start(bf16[64,1024]{1,0:T(8,128)(2,1)S(1)} %get-tuple-element.837), channel_id=1, source_target_pairs={{1,0},{5,1},{0,2},{4,3},{3,4},{7,5},{2,6},{6,7},{9,8},{13,9},{8,10... | collective-permute-start | bytes 393224 | tf_op jit(solution)/shard_map/ppermute | solution.py:799
  34.9 166.2 %all-gather.23.cloned.1.call-start = ((), (), s32[]{:S(2)}) async-start(), calls=%async_computation.3 | async-start | bytes 1310720 | tf_op jit(solution)/shard_map/all_gather | solution.py:147
  38.0 215.6 %all-gather.25.cloned.1.call-start = ((), (), s32[]{:S(2)}) async-start(), calls=%async_computation.4 | async-start | bytes 1310720 | tf_op jit(solution)/shard_map/all_gather | solution.py:147
  40.8 242.7 %all-gather.27.cloned.1.call-start = ((), (), s32[]{:S(2)}) async-start(), calls=%async_computation.5 | async-start | bytes 1310720 | tf_op jit(solution)/shard_map/all_gather | solution.py:147
  55.2 257.4 %all-gather.29.cloned.1.call-start = ((), (), s32[]{:S(2)}) async-start(), calls=%async_computation.6 | async-start | bytes 1310720 | tf_op jit(solution)/shard_map/all_gather | solution.py:147
  63.3 353.6 %all-gather.31.cloned.1.call-start = ((), (), s32[]{:S(2)}) async-start(), calls=%async_computation.7 | async-start | bytes 5242880 | tf_op jit(solution)/shard_map/all_gather | solution.py:1102
  92.6 56.8 %collective-permute-start.9 = (bf16[2,2,1,128,1024]{4,3,1,2,0:T(8,128)(2,1)S(1)}, bf16[2,2,1,128,1024]{4,3,1,2,0:T(8,128)(2,1)S(1)}, u32[]{:S(2)}, u32[]{:S(2)}) collective-permute-start(bf16[2,2,1,128,1024]{4,3,1,2,0:T(8,128)(2,1)S(1)} %constant_dynamic-update-slice_fusion.18), channel_id=1, source_target_pairs={{0,16},{1,17},{2,18},{3,19},{4,20},{5,21},{6,22},{7,23},{8,24},{9,... | collective-permute-start | bytes 3145736 | tf_op jit(solution)/shard_map/ppermute | solution.py:83
  95.2 55.2 %collective-permute-start.10 = (bf16[2,2,1,128,1024]{4,3,2,1,0:T(8,128)(2,1)S(1)}, bf16[2,2,1,128,1024]{4,3,2,1,0:T(8,128)(2,1)}, u32[]{:S(2)}, u32[]{:S(2)}) collective-permute-start(bf16[2,2,1,128,1024]{4,3,2,1,0:T(8,128)(2,1)S(1)} %constant_dynamic-update-slice_fusion.20.refs_2_), channel_id=1, source_target_pairs={{0,8},{1,9},{2,10},{3,11},{4,12},{5,13},{6,14},{7,15},{8,0},{9,1},... | collective-permute-start | bytes 3145736 | tf_op jit(solution)/shard_map/ppermute | solution.py:83
  97.8 51.5 %collective-permute-start.11 = (bf16[1,2,2,32,2048]{4,3,2,1,0:T(8,128)(2,1)}, bf16[1,2,2,32,2048]{4,3,2,1,0:T(8,128)(2,1)}, u32[]{:S(2)}, u32[]{:S(2)}) collective-permute-start(bf16[1,2,2,32,2048]{4,3,2,1,0:T(8,128)(2,1)} %get-tuple-element.306), channel_id=1, source_target_pairs={{0,8},{1,9},{2,10},{3,11},{4,12},{5,13},{6,14},{7,15},{8,0},{9,1},... | collective-permute-start | bytes 1572872 | tf_op jit(solution)/shard_map/ppermute | solution.py:83
  98.4 51.0 %collective-permute-start.12 = (bf16[1,2,2,32,2048]{4,3,2,1,0:T(8,128)(2,1)}, bf16[1,2,2,32,2048]{4,3,2,1,0:T(8,128)(2,1)}, u32[]{:S(2)}, u32[]{:S(2)}) collective-permute-start(bf16[1,2,2,32,2048]{4,3,2,1,0:T(8,128)(2,1)} %get-tuple-element.308), channel_id=1, source_target_pairs={{0,16},{1,17},{2,18},{3,19},{4,20},{5,21},{6,22},{7,23},{8,24},{9,... | collective-permute-start | bytes 1572872 | tf_op jit(solution)/shard_map/ppermute | solution.py:83
  158.9 42.2 %collective-permute-start.15 = (bf16[2,2,2,32,2048]{4,3,2,1,0:T(8,128)(2,1)}, bf16[2,2,2,32,2048]{4,3,2,1,0:T(8,128)(2,1)}, u32[]{:S(2)}, u32[]{:S(2)}) collective-permute-start(bf16[2,2,2,32,2048]{4,3,2,1,0:T(8,128)(2,1)} %constant_dynamic-update-slice_fusion.22.refs_0_), channel_id=1, source_target_pairs={{0,16},{1,17},{2,18},{3,19},{4,20},{5,21},{6,22},{7,23},{8,24},{9,... | collective-permute-start | bytes 3145736 | tf_op jit(solution)/shard_map/ppermute | solution.py:83
  161.2 39.8 %collective-permute-start.16 = (bf16[2,2,2,32,2048]{4,3,2,1,0:T(8,128)(2,1)S(1)}, bf16[2,2,2,32,2048]{4,3,2,1,0:T(8,128)(2,1)}, u32[]{:S(2)}, u32[]{:S(2)}) collective-permute-start(bf16[2,2,2,32,2048]{4,3,2,1,0:T(8,128)(2,1)S(1)} %constant_dynamic-update-slice_fusion.24.refs_2_), channel_id=1, source_target_pairs={{0,8},{1,9},{2,10},{3,11},{4,12},{5,13},{6,14},{7,15},{8,0},{9,1},... | collective-permute-start | bytes 3145736 | tf_op jit(solution)/shard_map/ppermute | solution.py:83
  204.4 49.2 %collective-permute-start.24 = (bf16[2,2,2,32,2048]{4,3,2,1,0:T(8,128)(2,1)S(1)}, bf16[2,2,2,32,2048]{4,3,2,1,0:T(8,128)(2,1)}, u32[]{:S(2)}, u32[]{:S(2)}) collective-permute-start(bf16[2,2,2,32,2048]{4,3,2,1,0:T(8,128)(2,1)S(1)} %constant_dynamic-update-slice_fusion.30.refs_0_), channel_id=1, source_target_pairs={{0,16},{1,17},{2,18},{3,19},{4,20},{5,21},{6,22},{7,23},{8,24},{9,... | collective-permute-start | bytes 3145736 | tf_op jit(solution)/shard_map/ppermute | solution.py:83
  206.7 46.9 %collective-permute-start.25 = (bf16[2,2,2,32,2048]{4,3,2,1,0:T(8,128)(2,1)S(1)}, bf16[2,2,2,32,2048]{4,3,2,1,0:T(8,128)(2,1)}, u32[]{:S(2)}, u32[]{:S(2)}) collective-permute-start(bf16[2,2,2,32,2048]{4,3,2,1,0:T(8,128)(2,1)S(1)} %constant_dynamic-update-slice_fusion.32.refs_2_), channel_id=1, source_target_pairs={{0,8},{1,9},{2,10},{3,11},{4,12},{5,13},{6,14},{7,15},{8,0},{9,1},... | collective-permute-start | bytes 3145736 | tf_op jit(solution)/shard_map/ppermute | solution.py:83
  209.3 44.3 %collective-permute-start.26 = (bf16[1,2,2,32,2048]{4,3,2,1,0:T(8,128)(2,1)}, bf16[1,2,2,32,2048]{4,3,2,1,0:T(8,128)(2,1)}, u32[]{:S(2)}, u32[]{:S(2)}) collective-permute-start(bf16[1,2,2,32,2048]{4,3,2,1,0:T(8,128)(2,1)} %get-tuple-element.333), channel_id=1, source_target_pairs={{0,8},{1,9},{2,10},{3,11},{4,12},{5,13},{6,14},{7,15},{8,0},{9,1},... | collective-permute-start | bytes 1572872 | tf_op jit(solution)/shard_map/ppermute | solution.py:83
  209.8 43.8 %collective-permute-start.27 = (bf16[1,2,2,32,2048]{4,3,2,1,0:T(8,128)(2,1)}, bf16[1,2,2,32,2048]{4,3,2,1,0:T(8,128)(2,1)}, u32[]{:S(2)}, u32[]{:S(2)}) collective-permute-start(bf16[1,2,2,32,2048]{4,3,2,1,0:T(8,128)(2,1)} %get-tuple-element.335), channel_id=1, source_target_pairs={{0,16},{1,17},{2,18},{3,19},{4,20},{5,21},{6,22},{7,23},{8,24},{9,... | collective-permute-start | bytes 1572872 | tf_op jit(solution)/shard_map/ppermute | solution.py:83
  296.4 39.2 %collective-permute-start.33 = (bf16[2,2,8,2,2,16,256]{6,5,4,3,2,1,0:T(8,128)(2,1)S(1)}, bf16[2,2,8,2,2,16,256]{6,5,4,3,2,1,0:T(8,128)(2,1)}, u32[]{:S(2)}, u32[]{:S(2)}) collective-permute-start(bf16[2,2,8,2,2,16,256]{6,5,4,3,2,1,0:T(8,128)(2,1)S(1)} %constant_dynamic-update-slice_fusion.43.refs_0_), channel_id=1, source_target_pairs={{0,16},{1,17},{2,18},{3,19},{4,20},{5,21},{6,22},{7,23},{8,24},{9,... | collective-permute-start | bytes 3145736 | tf_op jit(solution)/shard_map/ppermute | solution.py:83
  338.0 38.2 %collective-permute-start.38 = (bf16[2,2,2,32,2048]{4,3,2,1,0:T(8,128)(2,1)S(1)}, bf16[2,2,2,32,2048]{4,3,2,1,0:T(8,128)(2,1)S(1)}, u32[]{:S(2)}, u32[]{:S(2)}) collective-permute-start(bf16[2,2,2,32,2048]{4,3,2,1,0:T(8,128)(2,1)S(1)} %constant_dynamic-update-slice_fusion.47.refs_0_), channel_id=1, source_target_pairs={{0,16},{1,17},{2,18},{3,19},{4,20},{5,21},{6,22},{7,23},{8,24},{9,... | collective-permute-start | bytes 3145736 | tf_op jit(solution)/shard_map/ppermute | solution.py:83
  427.4 108.6 %collective-permute-start.67 = (bf16[2,128,1024]{2,1,0:T(8,128)(2,1)}, bf16[2,128,1024]{2,1,0:T(8,128)(2,1)}, u32[]{:S(2)}, u32[]{:S(2)}) collective-permute-start(bf16[2,128,1024]{2,1,0:T(8,128)(2,1)} %pad_maximum_fusion.24), channel_id=1, source_target_pairs={{0,8},{1,9},{2,10},{3,11},{4,12},{5,13},{6,14},{7,15},{8,0},{9,1},... | collective-permute-start | bytes 1572872 | tf_op jit(solution)/shard_map/ppermute | solution.py:83
  432.3 104.2 %collective-permute-start.68 = (bf16[2,128,1024]{2,1,0:T(8,128)(2,1)}, bf16[2,128,1024]{2,1,0:T(8,128)(2,1)}, u32[]{:S(2)}, u32[]{:S(2)}) collective-permute-start(bf16[2,128,1024]{2,1,0:T(8,128)(2,1)} %pad_maximum_fusion.25), channel_id=1, source_target_pairs={{0,16},{1,17},{2,18},{3,19},{4,20},{5,21},{6,22},{7,23},{8,24},{9,... | collective-permute-start | bytes 1572872 | tf_op jit(solution)/shard_map/ppermute | solution.py:83
  662.5 41.7 %collective-permute-start.81 = (bf16[2,4,128,256]{3,2,1,0:T(8,128)(2,1)}, bf16[2,4,128,256]{3,2,1,0:T(8,128)(2,1)S(1)}, u32[]{:S(2)}, u32[]{:S(2)}) collective-permute-start(bf16[2,4,128,256]{3,2,1,0:T(8,128)(2,1)} %get-tuple-element.510), channel_id=1, source_target_pairs={{0,8},{1,9},{2,10},{3,11},{4,12},{5,13},{6,14},{7,15},{8,0},{9,1},... | collective-permute-start | bytes 1572872 | tf_op jit(solution)/shard_map/ppermute | solution.py:83
  (304 other events, 3568.6 us)
Sparse Core Ops, SparseCore 0:
  19.9 42.8 all-gather.16
  64.3 28.0 all-gather.18
  94.6 27.4 all-gather.20
  124.1 27.3 all-gather.22
  152.9 27.3 all-gather.24
  182.3 27.5 all-gather.26
  212.0 27.4 all-gather.28
  246.3 80.5 all-gather.30

commit v4 on v2

--- a/solution.py
+++ b/solution.py
@@ -212,39 +212,36 @@
     for source, (labels, first) in zip(sources, plan):
         for place, label in enumerate(labels):
             chip = own ^ (label // 2)
-            for step in range(source.shape[1]):
-                block = source.at[place, step]
-                z = first + step
-                if form == "attention":
-                    split = staged[0].shape[-1]
-                    half = staged[1].shape[-1]
+            block = source.at[place]
+            span = slice(first, first + source.shape[1])
+            if form == "attention":
+                split = staged[0].shape[-1]
+                for side in range(2):
+                    copies.append((block.at[:, side, :, :split], 0, (chip, side, span)))
+                    copies.append((block.at[:, side, :, split:], 1, (side, chip, span)))
+            elif form == "first":
+                for side in range(2):
+                    copies.append((block.at[:, side], 0, (chip, side, span)))
+            elif form == "second":
+                copies.append((block.at[:, 0], 0, (chip, span)))
+            else:
+                for layer in range(2):
                     for side in range(2):
-                        copies.append((block.at[side, :, :split], 0, (chip, side, z)))
-                        copies.append((block.at[side, :, split:], 1, (side, chip, z)))
-                elif form == "first":
-                    for side in range(2):
-                        copies.append((block.at[side], 0, (chip, side, z)))
-                elif form == "second":
-                    copies.append((block.at[0], 0, (chip, z)))
-                else:
-                    for layer in range(2):
-                        down = block.at[2 * layer + kind]
-                        for side in range(2):
-                            copies.append((down.at[side], 0, (layer, chip, side, z)))
-                        up = block.at[4 + 2 * layer + kind]
-                        for fold in range(4):
-                            copies.append((up.at[fold // 2, fold % 2], 1, (layer, fold, chip, z)))
+                        down = block.at[:, 2 * layer + kind, side]
+                        copies.append((down, 0, (layer, chip, side, span)))
+                    for fold in range(4):
+                        up = block.at[:, 4 + 2 * layer + kind, fold // 2, fold % 2]
+                        copies.append((up, 1, (layer, fold, chip, span)))
     started = []
     for place, (origin, turn, index) in enumerate(copies):
         copy = pltpu.make_async_copy(origin, staged[turn].at[index], in_sems.at[place])
         copy.start()
         started.append(copy)
+    for copy in started:
+        copy.wait()
     ended = []
-    for place, (origin, turn, index) in enumerate(copies):
-        started[place].wait()
-        copy = pltpu.make_async_copy(
-            staged[turn].at[index], targets[turn].at[index], out_sems.at[place]
-        )
+    for turn, (origin, target) in enumerate(zip(staged, targets)):
+        copy = pltpu.make_async_copy(origin, target, out_sems.at[turn])
         copy.start()
         ended.append(copy)
     for copy in ended:
@@ -253,7 +250,7 @@
 
 def place_blocks(pieces, where, form, shapes):
     plan = [(labels, first) for labels, first, _ in pieces]
-    blocks = sum(len(labels) * stack.shape[1] for labels, _, stack in pieces)
+    blocks = sum(len(labels) for labels, _, _ in pieces)
     copies = blocks * {"attention": 4, "first": 2, "second": 1, "adapter": 12}[form]
     anywhere = pl.BlockSpec(memory_space=pl.ANY)
     return pl.pallas_call(
@@ -264,7 +261,7 @@
             in_specs=[anywhere] * len(pieces),
             out_specs=[anywhere] * len(shapes),
             scratch_shapes=[pltpu.VMEM(shape, jnp.bfloat16) for shape in shapes]
-            + [pltpu.SemaphoreType.DMA((copies,))] * 2,
+            + [pltpu.SemaphoreType.DMA((copies,)), pltpu.SemaphoreType.DMA((len(shapes),))],
         ),
         out_shape=[jax.ShapeDtypeStruct(shape, jnp.bfloat16) for shape in shapes],
         compiler_params=pltpu.CompilerParams(vmem_limit_bytes=24 * MEBI),
@@ -375,14 +372,47 @@
     return (branch, (low_in, slope, inner_slope, inner_low))
 
 
+def feed_grad_kernel(grad_ref, second_ref, slope_ref, first_ref, out_ref):
+    hidden_grad = bfloat(times_second(grad_ref[...], second_ref[...]) * slope_ref[...])
+    part = times_second(hidden_grad, first_ref[...])
+
+    @pl.when(pl.program_id(0) == 0)
+    def _():
+        out_ref[...] = part
+
+    @pl.when(pl.program_id(0) > 0)
+    def _():
+        out_ref[...] += part
+
+
+def feed_grad(grad, w_second, slope, w_first):
+    rows, width = grad.shape
+    units = w_second.shape[0]
+    tile = min(units, 512)
+    return pl.pallas_call(
+        feed_grad_kernel,
+        grid=(units // tile,),
+        in_specs=[
+            pl.BlockSpec((rows, width), lambda i: (0, 0)),
+            pl.BlockSpec((tile, width), lambda i: (i, 0)),
+            pl.BlockSpec((rows, tile), lambda i: (0, i)),
+            pl.BlockSpec((width, tile), lambda i: (0, i)),
+        ],
+        out_specs=pl.BlockSpec((rows, width), lambda i: (0, 0)),
+        out_shape=jax.ShapeDtypeStruct((rows, width), jnp.float32),
+        compiler_params=pltpu.CompilerParams(vmem_limit_bytes=40 * MEBI),
+        cost_estimate=LIGHT,
+    )(grad, w_second, slope, w_first)
+
+
 def feed_backward(grad, cache, w_first, w_second, down, upward):
     low_in, slope, inner_slope, inner_low = cache
-    hidden_grad = bfloat(times_second(bfloat(grad), w_second) * slope)
+    hidden_part = feed_grad(bfloat(grad), w_second, slope, w_first)
     adapter_grad = bfloat(4.0 * grad)
     upward_grad = times_first(inner_low, adapter_grad)
     inner_grad = bfloat(times_second(adapter_grad, upward) * inner_slope)
     down_grad = times_first(low_in, inner_grad)
-    value_grad = times_second(hidden_grad, w_first) + times_second(inner_grad, down)
+    value_grad = hidden_part + times_second(inner_grad, down)
     return (value_grad, down_grad, upward_grad)
 
 

time: 803 us -> 802 us (level)
  Pallas kernels: 162 us -> 136 us
  matrix products: 61.7 us -> 37.7 us
  waiting for transfers between devices: 151 us -> 173 us
  starting transfers between devices: 106 us -> 126 us
  local copies, waits for them, and re-layouts: 158 us -> 167 us
    pallas_call x8, Pallas kernels: 57.3 us -> 19.6 us  [place_blocks(): pl.pallas_call(functools.partial(place_kernel, plan, form), grid_spec=plt...]
    dot_general x13 -> x11, matrix products: 33.4 us -> 9.86 us  [times_second(): lax.dot_general(left, right, (((1,), (1,)), ((), ())), preferred_element_...]
    ppermute x94, waiting for transfers between devices: 141 us -> 163 us  [swap(): return lax.ppermute(value, AXES, pairs)]
    pallas_call x0 -> x2, Pallas kernels: none -> 11.7 us  [feed_grad(): pl.pallas_call(feed_grad_kernel, grid=(units // tile,), in_specs=[pl.Bloc...]
    all_gather x7, starting transfers between devices: 0.63 us -> 11.8 us  [column_first_steps(): column, = (yield [lax.all_gather(own, 'kv')])]
    ppermute x94, starting transfers between devices: 97.7 us -> 107 us  [swap(): return lax.ppermute(value, AXES, pairs)]
    unnamed x477 -> x523, local copies, waits for them, and re-layouts: 44.6 us -> 52.5 us
    convert_element_type x14 -> x18, other arithmetic: 14.2 us -> 18.9 us  [bfloat(): return value.astype(jnp.bfloat16)]
  transfers between devices with their start and end apart: 106 -> 106, of which waited for: 33 -> 32; matrix products, arithmetic and copies ran while one was open for 32% -> 31% of each run, Pallas kernels for 15% -> 10%
where the time goes in v4:
time: 802 us; the launch traced here: 794 us
  waiting for transfers between devices  173 us (22%)
  local copies, waits for them, and re-layouts  167 us (21%)
  Pallas kernels  136 us (17%)
  starting transfers between devices  126 us (16%)
  other arithmetic  124 us (15%)
  matrix products  37.7 us (5%)
  between operations  29.9 us (4%)
    ppermute x94, waiting for transfers between devices, swap(): return lax.ppermute(value, AXES, pairs)  163 us
    ppermute x94, starting transfers between devices, swap(): return lax.ppermute(value, AXES, pairs)  107 us
    pallas_call x2, Pallas kernels, vocab_pass(): pl.pallas_call(functools.partial(vocab_kernel, count, tile, step), grid_s...  66.4 us
    unnamed x523, local copies, waits for them, and re-layouts  52.5 us
    pallas_call x6, Pallas kernels, attention_call(): pl.pallas_call(functools.partial(kernel, causal), grid_spec=pltpu.Prefetc...  38.5 us
    dot_general x15, matrix products, times_plain(): return jnp.dot(left, right, preferred_element_type=jnp.float32)  23.8 us
    pallas_call x8, Pallas kernels, place_blocks(): pl.pallas_call(functools.partial(place_kernel, plan, form), grid_spec=plt...  19.6 us
    convert_element_type x18, other arithmetic, bfloat(): return value.astype(jnp.bfloat16)  18.9 us
  transfers between devices with their start and end apart: 106, of which 32 were waited for; matrix products, arithmetic and copies ran while one was open for 31% of the time, Pallas kernels for 10%

profile of v4, /device:TPU:0, one launch (start us, length us, event | category | flops | bytes accessed | tf_op | source)
XLA Modules:
  0.0 793.5 jit_solution(5623481529752672933)
XLA Ops:
  40.9 11.6 %all-gather.27.cloned.1.call-start = ((), (), s32[]{:S(2)}) async-start(), calls=%async_computation.5 | async-start | bytes 1310720 | tf_op jit(solution)/shard_map/all_gather | solution.py:147
  66.3 9.6 %collective-permute-done.5 = bf16[128,1024]{1,0:T(8,128)(2,1)S(1)} collective-permute-done((bf16[128,1024]{1,0:T(8,128)(2,1)S(1)}, bf16[128,1024]{1,0:T(8,128)(2,1)S(1)}, u32[]{:S(2)}, u32[]{:S(2)}) %collective-permute-start.5) | collective-permute-done | bytes 262176 | tf_op jit(solution)/shard_map/ppermute | solution.py:716
  75.9 15.0 %collective-permute-start.4 = (bf16[128,1024]{1,0:T(8,128)(2,1)S(1)}, bf16[128,1024]{1,0:T(8,128)(2,1)S(1)}, u32[]{:S(2)}, u32[]{:S(2)}) collective-permute-start(bf16[128,1024]{1,0:T(8,128)(2,1)S(1)} %pad_maximum_fusion.26), channel_id=1, source_target_pairs={{0,4},{1,5},{2,6},{3,7},{4,0},{5,1},{6,2},{7,3},{8,12},{9,13},{10,... | collective-permute-start | bytes 786440 | tf_op jit(solution)/shard_map/ppermute | solution.py:83
  109.9 9.1 %collective-permute-done.10 = bf16[1,2,1,128,1024]{4,3,1,2,0:T(8,128)(2,1)S(1)} collective-permute-done((bf16[1,2,1,128,1024]{4,3,1,2,0:T(8,128)(2,1)S(1)}, bf16[1,2,1,128,1024]{4,3,1,2,0:T(8,128)(2,1)S(1)}, u32[]{:S(2)}, u32[]{:S(2)}) %collective-permute-start.10) | collective-permute-done | bytes 524320 | tf_op jit(solution)/shard_map/ppermute | solution.py:83
  128.6 13.0 %pad.14.table_ref = bf16[6400,1024]{1,0:T(8,128)(2,1)} pad(bf16[6284,1024]{1,0:T(8,128)(2,1)} %param.36, bf16[]{:T(256)} %constant.407.clone.1), padding=0_116x0_0 | pad | bytes 25976834 | tf_op jit(solution)/shard_map/jit(_pad)/pad | solution.py:862
  141.7 15.1 %collective-permute-done.18 = bf16[1,2,2,32,2048]{4,3,2,1,0:T(8,128)(2,1)} collective-permute-done((bf16[1,2,2,32,2048]{4,3,2,1,0:T(8,128)(2,1)}, bf16[1,2,2,32,2048]{4,3,2,1,0:T(8,128)(2,1)}, u32[]{:S(2)}, u32[]{:S(2)}) %collective-permute-start.18) | collective-permute-done | bytes 524320 | tf_op jit(solution)/shard_map/ppermute | solution.py:83
  173.5 6.5 convert_reduce_fusion
  180.1 18.4 %collective-permute-done.22 = bf16[1,2,2,32,2048]{4,3,2,1,0:T(8,128)(2,1)} collective-permute-done((bf16[1,2,2,32,2048]{4,3,2,1,0:T(8,128)(2,1)}, bf16[1,2,2,32,2048]{4,3,2,1,0:T(8,128)(2,1)}, u32[]{:S(2)}, u32[]{:S(2)}) %collective-permute-start.22) | collective-permute-done | bytes 524320 | tf_op jit(solution)/shard_map/ppermute | solution.py:83
  214.6 17.2 %gather_fusion = bf16[2048,1024]{1,0:T(8,128)(2,1)} fusion(bf16[6284,1024]{1,0:T(8,128)(2,1)} %param.36, s32[2048]{0:T(1024)S(1)} %fusion.201), kind=kCustom, calls=%fused_computation | custom fusion | bytes 8396800 | tf_op jit(solution)/shard_map/jit(_take)/gather | solution.py:892
  237.6 5.8 add_convert_fusion
  260.5 7.1 shard_map.303
  273.0 7.8 collective-permute-done.30
  300.5 23.5 %collective-permute-done.35 = bf16[1,2,2,32,2048]{4,3,2,1,0:T(8,128)(2,1)} collective-permute-done((bf16[1,2,2,32,2048]{4,3,2,1,0:T(8,128)(2,1)}, bf16[1,2,2,32,2048]{4,3,2,1,0:T(8,128)(2,1)}, u32[]{:S(2)}, u32[]{:S(2)}) %collective-permute-start.35) | collective-permute-done | bytes 524320 | tf_op jit(solution)/shard_map/ppermute | solution.py:83
  341.4 23.3 %collective-permute-done.40 = bf16[1,2,2,32,2048]{4,3,2,1,0:T(8,128)(2,1)S(1)} collective-permute-done((bf16[1,2,2,32,2048]{4,3,2,1,0:T(8,128)(2,1)S(1)}, bf16[1,2,2,32,2048]{4,3,2,1,0:T(8,128)(2,1)S(1)}, u32[]{:S(2)}, u32[]{:S(2)}) %collective-permute-start.40) | collective-permute-done | bytes 524320 | tf_op jit(solution)/shard_map/ppermute | solution.py:83
  381.6 6.8 collective-permute-done.42.refs_1_
  407.5 5.1 fusion.5
  428.3 5.7 collective-permute-done.67
  442.2 16.2 %shard_map.311 = (f32[512,1024]{1,0:T(8,128)}, f32[512,128]{1,0:T(8,128)}) custom-call(s32[9]{0:T(128)} %pad_add_fusion.2.order_ref, bf16[512,1024]{1,0:T(8,128)(2,1)} %pad_maximum_fusion.8.rows_ref, bf16[6400,1024]{1,0:T(8,128)(2,1)} %pad.14.table_ref), custom_call_target="tpu_custom_call" | custom-call | flops 10066329600 | bytes 16252928 | tf_op jit(solution)/shard_map/pallas_call | solution.py:510
  466.8 50.2 %shard_map.312 = (f32[1536,1024]{1,0:T(8,128)}, f32[1536,128]{1,0:T(8,128)}) custom-call(s32[25]{0:T(128)} %pad_add_fusion.3.order_ref, bf16[1536,1024]{1,0:T(8,128)(2,1)} %copy-done.85, bf16[6400,1024]{1,0:T(8,128)(2,1)} %pad.14.table_ref), custom_call_target="tpu_custom_call" | custom-call | flops 30198988800 | bytes 22544384 | tf_op jit(solution)/shard_map/pallas_call | solution.py:510
  537.5 9.3 %collective-permute-start.57 = (bf16[2,128,1024]{2,1,0:T(8,128)(2,1)S(1)}, bf16[2,128,1024]{2,1,0:T(8,128)(2,1)S(1)}, u32[]{:S(2)}, u32[]{:S(2)}) collective-permute-start(bf16[2,128,1024]{2,1,0:T(8,128)(2,1)S(1)} %pad_maximum_fusion.20), channel_id=1, source_target_pairs={{0,8},{1,9},{2,10},{3,11},{4,12},{5,13},{6,14},{7,15},{8,0},{9,1},... | collective-permute-start | bytes 1572872 | tf_op jit(solution)/shard_map/ppermute | solution.py:83
  549.3 9.5 %collective-permute-done.58 = f32[2,2,128]{2,1,0:T(2,128)S(1)} collective-permute-done((f32[2,2,128]{2,1,0:T(2,128)S(1)}, f32[2,2,128]{2,1,0:T(2,128)S(1)}, u32[]{:S(2)}, u32[]{:S(2)}) %collective-permute-start.58) | collective-permute-done | bytes 2080 | tf_op jit(solution)/shard_map/ppermute | solution.py:83
  587.0 7.6 shard_map.313
  617.0 7.1 shard_map.314
  681.9 11.3 %shard_map.317 = (bf16[512,512]{1,0:T(8,128)(2,1)S(1)}, bf16[512,512]{1,0:T(8,128)(2,1)S(1)}, bf16[512,512]{1,0:T(8,128)(2,1)S(1)}) custom-call(s32[1]{0:T(128)} %bitcast.59.length_ref, bf16[512,1536]{1,0:T(8,128)(2,1)S(1)} %copy-done.1, bf16[512,1536]{1,0:T(8,128)(2,1)S(1)} %copy-done.1, bf16[512,1536]{1,0:T(8,128)(2,1)S(1)} %copy-done.1, ...), custom_call_target="tpu_custom_call" | custom-call | flops 1 | bytes 1 | tf_op jit(solution)/shard_map/pallas_call | solution.py:329
  (1162 shorter events, 451.7 us)
Async XLA Ops:
  7.2 89.3 %all-gather.17.cloned.1.call-start = ((), (), s32[]{:S(2)}) async-start(), calls=%async_computation | async-start | bytes 1310720 | tf_op jit(solution)/shard_map/all_gather | solution.py:147
  19.7 100.1 %all-gather.19.cloned.1.call-start = ((), (), s32[]{:S(2)}) async-start(), calls=%async_computation.1 | async-start | bytes 1310720 | tf_op jit(solution)/shard_map/all_gather | solution.py:147
  22.4 119.3 %all-gather.21.cloned.1.call-start = ((), (), s32[]{:S(2)}) async-start(), calls=%async_computation.2 | async-start | bytes 1310720 | tf_op jit(solution)/shard_map/all_gather | solution.py:147
  23.1 67.9 %collective-permute-start.15 = (s32[8,128]{1,0:T(8,128)}, s32[8,128]{1,0:T(8,128)}, u32[]{:S(2)}, u32[]{:S(2)}) collective-permute-start(s32[8,128]{1,0:T(8,128)} %get-tuple-element.813), channel_id=1, source_target_pairs={{0,3},{1,2},{2,1},{3,0},{4,7},{5,6},{6,5},{7,4},{8,11},{9,10},{10,... | collective-permute-start | bytes 12296 | tf_op jit(solution)/shard_map/ppermute | solution.py:83
  27.9 64.7 %collective-permute-start.14 = (s32[8,128]{1,0:T(8,128)}, s32[8,128]{1,0:T(8,128)}, u32[]{:S(2)}, u32[]{:S(2)}) collective-permute-start(s32[8,128]{1,0:T(8,128)} %get-tuple-element.813), channel_id=1, source_target_pairs={{0,2},{1,3},{2,0},{3,1},{4,6},{5,7},{6,4},{7,5},{8,10},{9,11},{10,... | collective-permute-start | bytes 12296 | tf_op jit(solution)/shard_map/ppermute | solution.py:83
  27.9 66.9 %collective-permute-start = (bf16[1,1,1,64,1024]{4,3,2,1,0:T(8,128)(2,1)S(1)}, bf16[1,1,1,64,1024]{4,3,2,1,0:T(8,128)(2,1)}, u32[]{:S(2)}, u32[]{:S(2)}) collective-permute-start(bf16[1,1,1,64,1024]{4,3,2,1,0:T(8,128)(2,1)S(1)} %get-tuple-element.249), channel_id=1, source_target_pairs={{0,8},{1,9},{2,10},{3,11},{4,12},{5,13},{6,14},{7,15},{8,0},{9,1},... | collective-permute-start | bytes 393224 | tf_op jit(solution)/shard_map/ppermute | solution.py:83
  34.0 146.0 %all-gather.23.cloned.1.call-start = ((), (), s32[]{:S(2)}) async-start(), calls=%async_computation.3 | async-start | bytes 1310720 | tf_op jit(solution)/shard_map/all_gather | solution.py:147
  37.2 206.2 %all-gather.25.cloned.1.call-start = ((), (), s32[]{:S(2)}) async-start(), calls=%async_computation.4 | async-start | bytes 1310720 | tf_op jit(solution)/shard_map/all_gather | solution.py:147
  40.9 232.1 %all-gather.27.cloned.1.call-start = ((), (), s32[]{:S(2)}) async-start(), calls=%async_computation.5 | async-start | bytes 1310720 | tf_op jit(solution)/shard_map/all_gather | solution.py:147
  54.8 245.7 %all-gather.29.cloned.1.call-start = ((), (), s32[]{:S(2)}) async-start(), calls=%async_computation.6 | async-start | bytes 1310720 | tf_op jit(solution)/shard_map/all_gather | solution.py:147
  94.2 301.3 %all-gather.31.cloned.1.call-start = ((), (), s32[]{:S(2)}) async-start(), calls=%async_computation.7 | async-start | bytes 5242880 | tf_op jit(solution)/shard_map/all_gather | solution.py:1003
  120.9 35.9 %collective-permute-start.16 = (bf16[2,2,1,128,1024]{4,3,1,2,0:T(8,128)(2,1)S(1)}, bf16[2,2,1,128,1024]{4,3,1,2,0:T(8,128)(2,1)S(1)}, u32[]{:S(2)}, u32[]{:S(2)}) collective-permute-start(bf16[2,2,1,128,1024]{4,3,1,2,0:T(8,128)(2,1)S(1)} %constant_dynamic-update-slice_fusion.22), channel_id=1, source_target_pairs={{0,16},{1,17},{2,18},{3,19},{4,20},{5,21},{6,22},{7,23},{8,24},{9,... | collective-permute-start | bytes 3145736 | tf_op jit(solution)/shard_map/ppermute | solution.py:83
  122.6 35.2 %collective-permute-start.17 = (bf16[2,2,1,128,1024]{4,3,2,1,0:T(8,128)(2,1)S(1)}, bf16[2,2,1,128,1024]{4,3,2,1,0:T(8,128)(2,1)}, u32[]{:S(2)}, u32[]{:S(2)}) collective-permute-start(bf16[2,2,1,128,1024]{4,3,2,1,0:T(8,128)(2,1)S(1)} %constant_dynamic-update-slice_fusion.24.refs_2_), channel_id=1, source_target_pairs={{0,8},{1,9},{2,10},{3,11},{4,12},{5,13},{6,14},{7,15},{8,0},{9,1},... | collective-permute-start | bytes 3145736 | tf_op jit(solution)/shard_map/ppermute | solution.py:83
  162.9 35.6 %collective-permute-start.20 = (bf16[2,2,2,32,2048]{4,3,2,1,0:T(8,128)(2,1)}, bf16[2,2,2,32,2048]{4,3,2,1,0:T(8,128)(2,1)}, u32[]{:S(2)}, u32[]{:S(2)}) collective-permute-start(bf16[2,2,2,32,2048]{4,3,2,1,0:T(8,128)(2,1)} %constant_dynamic-update-slice_fusion.26.refs_0_), channel_id=1, source_target_pairs={{0,16},{1,17},{2,18},{3,19},{4,20},{5,21},{6,22},{7,23},{8,24},{9,... | collective-permute-start | bytes 3145736 | tf_op jit(solution)/shard_map/ppermute | solution.py:83
  203.6 39.9 %collective-permute-start.24 = (bf16[2,2,2,32,2048]{4,3,2,1,0:T(8,128)(2,1)}, bf16[2,2,2,32,2048]{4,3,2,1,0:T(8,128)(2,1)}, u32[]{:S(2)}, u32[]{:S(2)}) collective-permute-start(bf16[2,2,2,32,2048]{4,3,2,1,0:T(8,128)(2,1)} %constant_dynamic-update-slice_fusion.30.refs_0_), channel_id=1, source_target_pairs={{0,16},{1,17},{2,18},{3,19},{4,20},{5,21},{6,22},{7,23},{8,24},{9,... | collective-permute-start | bytes 3145736 | tf_op jit(solution)/shard_map/ppermute | solution.py:83
  205.1 38.3 %collective-permute-start.25 = (bf16[2,2,2,32,2048]{4,3,2,1,0:T(8,128)(2,1)S(1)}, bf16[2,2,2,32,2048]{4,3,2,1,0:T(8,128)(2,1)}, u32[]{:S(2)}, u32[]{:S(2)}) collective-permute-start(bf16[2,2,2,32,2048]{4,3,2,1,0:T(8,128)(2,1)S(1)} %constant_dynamic-update-slice_fusion.32.refs_2_), channel_id=1, source_target_pairs={{0,8},{1,9},{2,10},{3,11},{4,12},{5,13},{6,14},{7,15},{8,0},{9,1},... | collective-permute-start | bytes 3145736 | tf_op jit(solution)/shard_map/ppermute | solution.py:83
  206.8 36.6 %collective-permute-start.26 = (bf16[1,2,2,32,2048]{4,3,2,1,0:T(8,128)(2,1)}, bf16[1,2,2,32,2048]{4,3,2,1,0:T(8,128)(2,1)}, u32[]{:S(2)}, u32[]{:S(2)}) collective-permute-start(bf16[1,2,2,32,2048]{4,3,2,1,0:T(8,128)(2,1)} %get-tuple-element.283), channel_id=1, source_target_pairs={{0,8},{1,9},{2,10},{3,11},{4,12},{5,13},{6,14},{7,15},{8,0},{9,1},... | collective-permute-start | bytes 1572872 | tf_op jit(solution)/shard_map/ppermute | solution.py:83
  284.1 39.9 %collective-permute-start.33 = (bf16[2,2,8,2,2,16,256]{6,5,4,3,2,1,0:T(8,128)(2,1)S(1)}, bf16[2,2,8,2,2,16,256]{6,5,4,3,2,1,0:T(8,128)(2,1)}, u32[]{:S(2)}, u32[]{:S(2)}) collective-permute-start(bf16[2,2,8,2,2,16,256]{6,5,4,3,2,1,0:T(8,128)(2,1)S(1)} %constant_dynamic-update-slice_fusion.43.refs_0_), channel_id=1, source_target_pairs={{0,16},{1,17},{2,18},{3,19},{4,20},{5,21},{6,22},{7,23},{8,24},{9,... | collective-permute-start | bytes 3145736 | tf_op jit(solution)/shard_map/ppermute | solution.py:83
  287.1 36.9 %collective-permute-start.34 = (bf16[2,2,8,2,2,16,256]{6,5,4,3,2,1,0:T(8,128)(2,1)S(1)}, bf16[2,2,8,2,2,16,256]{6,5,4,3,2,1,0:T(8,128)(2,1)}, u32[]{:S(2)}, u32[]{:S(2)}) collective-permute-start(bf16[2,2,8,2,2,16,256]{6,5,4,3,2,1,0:T(8,128)(2,1)S(1)} %constant_dynamic-update-slice_fusion.45.refs_2_), channel_id=1, source_target_pairs={{0,8},{1,9},{2,10},{3,11},{4,12},{5,13},{6,14},{7,15},{8,0},{9,1},... | collective-permute-start | bytes 3145736 | tf_op jit(solution)/shard_map/ppermute | solution.py:83
  327.3 37.4 %collective-permute-start.38 = (bf16[2,2,2,32,2048]{4,3,2,1,0:T(8,128)(2,1)S(1)}, bf16[2,2,2,32,2048]{4,3,2,1,0:T(8,128)(2,1)S(1)}, u32[]{:S(2)}, u32[]{:S(2)}) collective-permute-start(bf16[2,2,2,32,2048]{4,3,2,1,0:T(8,128)(2,1)S(1)} %constant_dynamic-update-slice_fusion.47.refs_0_), channel_id=1, source_target_pairs={{0,16},{1,17},{2,18},{3,19},{4,20},{5,21},{6,22},{7,23},{8,24},{9,... | collective-permute-start | bytes 3145736 | tf_op jit(solution)/shard_map/ppermute | solution.py:83
  329.0 35.7 %collective-permute-start.39 = (bf16[2,2,2,32,2048]{4,3,2,1,0:T(8,128)(2,1)S(1)}, bf16[2,2,2,32,2048]{4,3,2,1,0:T(8,128)(2,1)S(1)}, u32[]{:S(2)}, u32[]{:S(2)}) collective-permute-start(bf16[2,2,2,32,2048]{4,3,2,1,0:T(8,128)(2,1)S(1)} %constant_dynamic-update-slice_fusion.49.refs_2_), channel_id=1, source_target_pairs={{0,8},{1,9},{2,10},{3,11},{4,12},{5,13},{6,14},{7,15},{8,0},{9,1},... | collective-permute-start | bytes 3145736 | tf_op jit(solution)/shard_map/ppermute | solution.py:83
  658.6 48.8 %collective-permute-start.77 = (bf16[4,4,32,256]{3,2,1,0:T(8,128)(2,1)}, bf16[4,4,32,256]{3,2,1,0:T(8,128)(2,1)}, u32[]{:S(2)}, u32[]{:S(2)}) collective-permute-start(bf16[4,4,32,256]{3,2,1,0:T(8,128)(2,1)} %fusion.148), channel_id=1, source_target_pairs={{0,4},{1,5},{2,6},{3,7},{4,0},{5,1},{6,2},{7,3},{8,12},{9,13},{10,... | collective-permute-start | bytes 786440 | tf_op jit(solution)/shard_map/ppermute | solution.py:83
  672.3 42.0 %collective-permute-start.74 = (bf16[256,1024]{1,0:T(8,128)(2,1)}, bf16[256,1024]{1,0:T(8,128)(2,1)}, u32[]{:S(2)}, u32[]{:S(2)}) collective-permute-start(bf16[256,1024]{1,0:T(8,128)(2,1)} %get-tuple-element.571), channel_id=1, source_target_pairs={{0,4},{1,5},{2,6},{3,7},{4,0},{5,1},{6,2},{7,3},{8,12},{9,13},{10,... | collective-permute-start | bytes 1572872 | tf_op jit(solution)/shard_map/ppermute | solution.py:83
  696.9 44.0 %collective-permute-start.76 = (bf16[512,1024]{1,0:T(8,128)(2,1)}, bf16[512,1024]{1,0:T(8,128)(2,1)}, u32[]{:S(2)}, u32[]{:S(2)}) collective-permute-start(bf16[512,1024]{1,0:T(8,128)(2,1)} %get-tuple-element.839), channel_id=1, source_target_pairs={{0,4},{1,5},{2,6},{3,7},{4,0},{5,1},{6,2},{7,3},{8,12},{9,13},{10,... | collective-permute-start | bytes 3145736 | tf_op jit(solution)/shard_map/ppermute | solution.py:83
  (315 other events, 2986.9 us)
Sparse Core Ops, SparseCore 0:
  19.8 35.7 all-gather.16
  57.8 36.7 all-gather.18
  96.7 26.1 all-gather.20
  124.9 27.4 all-gather.22
  154.4 27.4 all-gather.24
  183.8 27.4 all-gather.26
  213.4 27.4 all-gather.28
  242.5 80.2 all-gather.30
